TPU v7x, 32 devices: a whole 2x2x4 slice. The times are simulated.
32 devices in a mesh: seq: 4 (over y, x), fsdp: 8 (over z, core).
Axes of the slice: x: 2, y: 2, z: 4, core: 2. Of those that a mesh axis runs over, the one named last changes fastest.
Arguments:
- tokens: bfloat16 [8, 1536, 1536], P('fsdp', 'seq'), may hold values from -6 to 6
- cotangent: bfloat16 [8, 1536, 1536], P('fsdp', 'seq'), may hold values from -6 to 6
- prefix_len: int32 [8], P('fsdp'), may hold values from 153 to 768
- expert_ids: int32 [8, 1536, 8], P('fsdp', 'seq'), may hold values from 0 to 15, all different within a row
- slot_rank: int32 [8, 4, 3072], P('fsdp', 'seq'), may hold values from 0 to 3071, each once within a row
- norm1_gain: bfloat16 [2, 1536], P(None, ('seq', 'fsdp')), may hold values from 0.5 to 1.5
- qkv_weight: bfloat16 [2, 1536, 2560], P(None, ('seq', 'fsdp')), may hold values from -0.15625 to 0.15625
- out_weight: bfloat16 [2, 1536, 1536], P(None, ('seq', 'fsdp')), may hold values from -1.25 to 1.25
- norm2_gain: bfloat16 [2, 1536], P(None, ('seq', 'fsdp')), may hold values from 0.5 to 1.5
- router_weight: bfloat16 [2, 1536, 16], P(None, ('seq', 'fsdp')), may hold values from -0.078125 to 0.078125
- in_weight: bfloat16 [2, 1536, 16384], P(None, 'seq', 'fsdp'), may hold values from -0.15625 to 0.15625
- down_weight: bfloat16 [2, 1536, 8192], P(None, 'seq', 'fsdp'), may hold values from -1 to 1
Outputs:
- output: bfloat16 [8, 1536, 1536], P('fsdp', 'seq')
- input_grad: float32 [8, 1536, 1536], P('fsdp', 'seq')
- norm1_grad: float32 [2, 1536], P(None, ('seq', 'fsdp'))
- qkv_grad: float32 [2, 1536, 2560], P(None, ('seq', 'fsdp'))
- out_grad: float32 [2, 1536, 1536], P(None, ('seq', 'fsdp'))
- norm2_grad: float32 [2, 1536], P(None, ('seq', 'fsdp'))
- router_grad: float32 [2, 1536, 16], P(None, ('seq', 'fsdp'))
- in_grad: float32 [2, 1536, 16384], P(None, 'seq', 'fsdp')
- down_grad: float32 [2, 1536, 8192], P(None, 'seq', 'fsdp')
Inputs may be any that keep to these rules, and one draw needn't show every extreme that they name: `expert_ids`: each token names 8 different experts. `slot_rank`: for each sequence and piece, a permutation of 0 to 3071.
All inputs are finite; a program needn't handle non-finite values.
Results may differ from a plain program's by a relative error of at most 0.025.
Values may be sent and summed in bfloat16 or wider, within the bound.
No kernel may reach another device: no remote copies, remote signals or barrier semaphores. Data moves between devices by JAX's collectives and lax.ppermute only.
A program may use at most 832 MiB of HBM per device.

v0:
```python
import math

import jax
import jax.numpy as jnp
from jax import lax
from jax.sharding import PartitionSpec as P

HEADS = 24
KV_HEADS = 8
HEAD_DIM = 64
FF = 512
TOP = 8
EXPERTS = 16
LAYERS = 2


EPS = 1e-06
THETA = 10000.0
SCALE = 0.125


def normalize(values):
    factor = lax.rsqrt(jnp.mean(values * values, axis=-1, keepdims=True) + EPS)
    return (values * factor, factor)


def norm_back(grad_hat, hat_values, factor):
    inner = jnp.mean(grad_hat * hat_values, axis=-1, keepdims=True)
    return factor * (grad_hat - hat_values * inner)


def tables(positions):
    steps = jnp.arange(HEAD_DIM // 2, dtype=jnp.float32)
    freqs = THETA ** (-2.0 * steps / HEAD_DIM)
    angles = positions.astype(jnp.float32)[:, None] * freqs[None, :]
    angles = jnp.concatenate([angles, angles], axis=-1)
    return (jnp.cos(angles), jnp.sin(angles))


def turn(values):
    half = values.shape[-1] // 2
    return jnp.concatenate([-values[..., half:], values[..., :half]], axis=-1)


def turn_back(values):
    half = values.shape[-1] // 2
    return jnp.concatenate([values[..., half:], -values[..., :half]], axis=-1)


def rotate(values, cosine, sine):
    return values * cosine[:, None, :] + turn(values) * sine[:, None, :]


def unrotate(values, cosine, sine):
    return values * cosine[:, None, :] + turn_back(values * sine[:, None, :])


def rounded(values):
    return lax.optimization_barrier(values.astype(jnp.bfloat16)).astype(jnp.float32)


def routing(expert_ids, slot_rank, capacity):
    groups, piece_len, top_count = expert_ids.shape
    pairs = expert_ids.reshape(groups, piece_len * top_count)
    orders = slot_rank.reshape(groups, piece_len * top_count)
    experts = jnp.arange(EXPERTS, dtype=jnp.int32)
    pair_hot = (pairs[..., None] == experts).astype(jnp.bfloat16)
    earlier = (orders[:, None, :] < orders[:, :, None]).astype(jnp.bfloat16)
    before = jnp.einsum("gpq,gqe->gpe", earlier, pair_hot, preferred_element_type=jnp.float32)
    position = jnp.sum(before * pair_hot.astype(jnp.float32), axis=-1).astype(jnp.int32)
    slot_ids = jnp.where(position < capacity, pairs * capacity + position, -1)
    return slot_ids.reshape(groups, piece_len, top_count)


def slot_table(slot_ids, weights, slot_count):
    columns = jnp.arange(slot_count, dtype=jnp.int32)
    table = jnp.zeros(slot_ids.shape[:2] + (slot_count,), jnp.float32)
    for picked in range(slot_ids.shape[2]):
        matches = slot_ids[:, :, picked, None] == columns
        table = table + jnp.where(matches, weights[:, :, picked, None], 0.0)
    return table


def slot_pick(slot_ids, table):
    columns = jnp.arange(table.shape[-1], dtype=jnp.int32)
    picks = []
    for picked in range(slot_ids.shape[2]):
        matches = slot_ids[:, :, picked, None] == columns
        picks.append(jnp.sum(jnp.where(matches, table, 0.0), axis=-1))
    return jnp.stack(picks, axis=-1)


def expert_weights(in_part, down_part):
    in_cols, down_cols = (
        lax.all_gather(in_part, "fsdp", axis=1, tiled=True),
        lax.all_gather(down_part, "fsdp", axis=1, tiled=True),
    )
    in_full, down_full = (
        lax.all_gather(in_cols, "seq", axis=0, tiled=True),
        lax.all_gather(down_cols, "seq", axis=0, tiled=True),
    )
    return (in_full, down_full)


def expert_sums(in_term, down_term):
    in_cols, down_cols = (
        lax.psum_scatter(
            in_term.astype(jnp.bfloat16), "fsdp", scatter_dimension=1, tiled=True
        ).astype(jnp.float32),
        lax.psum_scatter(
            down_term.astype(jnp.bfloat16), "fsdp", scatter_dimension=1, tiled=True
        ).astype(jnp.float32),
    )
    in_share, down_share = (
        lax.psum_scatter(
            in_cols.astype(jnp.bfloat16), "seq", scatter_dimension=0, tiled=True
        ).astype(jnp.float32),
        lax.psum_scatter(
            down_cols.astype(jnp.bfloat16), "seq", scatter_dimension=0, tiled=True
        ).astype(jnp.float32),
    )
    return (in_share, down_share)


def score_block(query, keys, query_pos, prefix_one, block_start, block_len):
    key_rows = lax.dynamic_slice_in_dim(keys, block_start, block_len, 0)
    logits = (
        jnp.einsum("qhgd,khd->hgqk", query, key_rows, preferred_element_type=jnp.float32) * SCALE
    )
    key_pos = block_start + jnp.arange(block_len, dtype=jnp.int32)
    allowed = (key_pos[None, :] <= query_pos[:, None]) | (key_pos[None, :] < prefix_one)
    return (logits, allowed, key_rows)


def block_range(rows, row_start, prefix_one, block_len):
    query_pos = row_start + jnp.arange(rows, dtype=jnp.int32)
    reach = jnp.maximum(row_start + rows, prefix_one)
    return (query_pos, (reach + block_len - 1) // block_len)


def attention_forward(query, keys, values, row_start, prefix_one, block_len):
    rows = query.shape[0]
    query_pos, block_count = block_range(rows, row_start, prefix_one, block_len)
    state_shape = (query.shape[1], query.shape[2], rows)

    def max_pass(block_index, carried):
        running, summed = carried
        logits, allowed, unused = score_block(
            query, keys, query_pos, prefix_one, block_index * block_len, block_len
        )
        logits = jnp.where(allowed, logits, -jnp.inf)
        newest = jnp.maximum(running, jnp.max(logits, axis=-1))
        summed = summed * jnp.exp(running - newest) + jnp.sum(
            jnp.exp(logits - newest[..., None]), axis=-1
        )
        return (newest, summed)

    initial = (jnp.full(state_shape, -jnp.inf, jnp.float32), jnp.zeros(state_shape, jnp.float32))
    running, summed = lax.fori_loop(0, block_count, max_pass, initial)
    log_total = running + jnp.log(summed)

    def value_pass(block_index, attended):
        block_start = block_index * block_len
        logits, allowed, unused = score_block(
            query, keys, query_pos, prefix_one, block_start, block_len
        )
        weights = jnp.where(allowed, jnp.exp(logits - log_total[..., None]), 0.0).astype(
            jnp.bfloat16
        )
        value_rows = lax.dynamic_slice_in_dim(values, block_start, block_len, 0)
        return attended + jnp.einsum(
            "hgqk,khd->qhgd", weights, value_rows, preferred_element_type=jnp.float32
        )

    attended = lax.fori_loop(0, block_count, value_pass, jnp.zeros(query.shape, jnp.float32))
    return (attended, log_total)


def attention_backward(
    query, keys, values, row_start, prefix_one, block_len, log_total, grad_attended, delta
):
    rows = query.shape[0]
    query_pos, block_count = block_range(rows, row_start, prefix_one, block_len)

    def grad_pass(block_index, carried):
        grad_query, grad_keys, grad_values = carried
        block_start = block_index * block_len
        logits, allowed, key_rows = score_block(
            query, keys, query_pos, prefix_one, block_start, block_len
        )
        probs = jnp.where(allowed, jnp.exp(logits - log_total[..., None]), 0.0)
        value_rows = lax.dynamic_slice_in_dim(values, block_start, block_len, 0)
        grad_probs = jnp.einsum(
            "qhgd,khd->hgqk", grad_attended, value_rows, preferred_element_type=jnp.float32
        )
        grad_logits = (probs * (grad_probs - delta[..., None])).astype(jnp.bfloat16)
        grad_query = grad_query + SCALE * jnp.einsum(
            "hgqk,khd->qhgd", grad_logits, key_rows, preferred_element_type=jnp.float32
        )
        key_term = SCALE * jnp.einsum(
            "hgqk,qhgd->khd", grad_logits, query, preferred_element_type=jnp.float32
        )
        value_term = jnp.einsum(
            "hgqk,qhgd->khd",
            probs.astype(jnp.bfloat16),
            grad_attended,
            preferred_element_type=jnp.float32,
        )
        grad_keys = lax.dynamic_update_slice_in_dim(
            grad_keys,
            lax.dynamic_slice_in_dim(grad_keys, block_start, block_len, 0) + key_term,
            block_start,
            0,
        )
        grad_values = lax.dynamic_update_slice_in_dim(
            grad_values,
            lax.dynamic_slice_in_dim(grad_values, block_start, block_len, 0) + value_term,
            block_start,
            0,
        )
        return (grad_query, grad_keys, grad_values)

    initial = (
        jnp.zeros(query.shape, jnp.float32),
        jnp.zeros(keys.shape, jnp.float32),
        jnp.zeros(values.shape, jnp.float32),
    )
    return lax.fori_loop(0, block_count, grad_pass, initial)


def layer_forward(hidden_in, parts, routes, prefix_len, rotation, row_start, block_len):
    gain_one, qkv_part, out_part, gain_two, router_part, in_part, down_part = parts
    slot_ids, dispatch, ids_hot = routes
    cosine, sine = rotation
    groups = prefix_len.shape[0]
    tokens_here, model_width = hidden_in.shape
    piece_len = tokens_here // groups
    slot_count = dispatch.shape[2]
    capacity = slot_count // EXPERTS
    query_width = HEADS * HEAD_DIM
    key_width = KV_HEADS * HEAD_DIM
    hat_one, factor_one = normalize(hidden_in)
    fulls = (
        lax.all_gather(qkv_part, ("seq", "fsdp"), axis=0, tiled=True),
        lax.all_gather(out_part, ("seq", "fsdp"), axis=0, tiled=True),
        lax.all_gather(router_part, ("seq", "fsdp"), axis=0, tiled=True),
        lax.all_gather(gain_one, ("seq", "fsdp"), axis=0, tiled=True),
        lax.all_gather(gain_two, ("seq", "fsdp"), axis=0, tiled=True),
    )
    qkv_full, out_full, router_full, gain_one_full, gain_two_full = fulls
    normed_one = (hat_one * gain_one_full.astype(jnp.float32)[None, :]).astype(jnp.bfloat16)
    mixed = jnp.dot(normed_one, qkv_full, preferred_element_type=jnp.float32)
    query = rotate(
        mixed[:, :query_width].reshape(tokens_here, HEADS, HEAD_DIM), cosine, sine
    ).astype(jnp.bfloat16)
    keys_here = rotate(
        mixed[:, query_width : query_width + key_width].reshape(tokens_here, KV_HEADS, HEAD_DIM),
        cosine,
        sine,
    ).astype(jnp.bfloat16)
    values_here = mixed[:, query_width + key_width :].astype(jnp.bfloat16)
    keys_all, values_all = (
        lax.all_gather(keys_here.reshape(groups, piece_len, key_width), "seq", axis=1, tiled=True),
        lax.all_gather(
            values_here.reshape(groups, piece_len, key_width), "seq", axis=1, tiled=True
        ),
    )
    seq_len = keys_all.shape[1]
    grouped = query.reshape(groups, piece_len, KV_HEADS, HEADS // KV_HEADS, HEAD_DIM)
    attended_one, total_one = attention_forward(
        grouped[0],
        keys_all[0].reshape(seq_len, KV_HEADS, HEAD_DIM),
        values_all[0].reshape(seq_len, KV_HEADS, HEAD_DIM),
        row_start,
        prefix_len[0],
        block_len,
    )
    attended_list = [attended_one]
    totals_list = [total_one]
    attended = jnp.stack(attended_list).reshape(tokens_here, query_width)
    attended_low = attended.astype(jnp.bfloat16)
    hidden = hidden_in + jnp.einsum(
        "tj,dj->td", attended_low, out_full, preferred_element_type=jnp.float32
    )
    hat_two, factor_two = normalize(hidden)
    in_full, down_full = expert_weights(in_part, down_part)
    local_count = in_full.shape[1] // (2 * FF)
    normed_two = (hat_two * gain_two_full.astype(jnp.float32)[None, :]).astype(jnp.bfloat16)
    logits = jnp.dot(normed_two, router_full, preferred_element_type=jnp.float32)
    sent = jnp.einsum(
        "gts,gtn->gsn",
        dispatch,
        normed_two.reshape(groups, piece_len, model_width),
        preferred_element_type=jnp.float32,
    ).astype(jnp.bfloat16)
    work_sent = sent.reshape(groups, EXPERTS, capacity, model_width)
    both = jnp.einsum(
        "gecn,nef->gecf",
        work_sent,
        in_full.reshape(model_width, local_count, 2 * FF),
        preferred_element_type=jnp.float32,
    )
    chosen = jnp.sum(logits.reshape(groups, piece_len, 1, EXPERTS) * ids_hot, axis=-1)
    gates = jax.nn.softmax(chosen, axis=-1)
    combine = slot_table(slot_ids, gates, slot_count).astype(jnp.bfloat16)
    inner = (jax.nn.silu(both[..., :FF]) * both[..., FF:]).astype(jnp.bfloat16)
    work_returned = jnp.einsum(
        "gecf,nef->gecn",
        inner,
        down_full.reshape(model_width, local_count, FF),
        preferred_element_type=jnp.float32,
    ).astype(jnp.bfloat16)
    returned = work_returned.reshape(groups, slot_count, model_width)
    merged = jnp.einsum("gts,gsd->gtd", combine, returned, preferred_element_type=jnp.float32)
    result = hidden + merged.reshape(tokens_here, model_width)
    saved = (
        hat_one,
        factor_one,
        normed_one,
        grouped,
        keys_all,
        values_all,
        jnp.stack(totals_list),
        attended,
        attended_low,
        hat_two,
        factor_two,
        normed_two,
        work_sent,
        gates,
        combine,
        both,
        inner,
        returned,
    )
    return (result, saved, fulls)


def layer_backward(
    grad_result, saved, fulls, expert_parts, routes, prefix_len, rotation, row_start, block_len
):
    (
        hat_one,
        factor_one,
        normed_one,
        grouped,
        keys_all,
        values_all,
        log_totals,
        attended,
        attended_low,
        hat_two,
        factor_two,
        normed_two,
        work_sent,
        gates,
        combine,
        both,
        inner,
        returned,
    ) = saved
    qkv_full, out_full, router_full, gain_one_full, gain_two_full = fulls
    slot_ids, dispatch, ids_hot = routes
    cosine, sine = rotation
    groups = prefix_len.shape[0]
    tokens_here, model_width = grad_result.shape
    piece_len = tokens_here // groups
    slot_count = dispatch.shape[2]
    capacity = slot_count // EXPERTS
    seq_len = keys_all.shape[1]
    query_width = HEADS * HEAD_DIM
    key_width = KV_HEADS * HEAD_DIM
    in_full, down_full = expert_weights(expert_parts[0], expert_parts[1])
    local_count = in_full.shape[1] // (2 * FF)
    grad_merged = grad_result.astype(jnp.bfloat16).reshape(groups, piece_len, model_width)
    grad_returned = (
        jnp.einsum("gts,gtd->gsd", combine, grad_merged, preferred_element_type=jnp.float32)
        .astype(jnp.bfloat16)
        .reshape(groups, EXPERTS, capacity, model_width)
    )
    grad_combine = jnp.einsum(
        "gtd,gsd->gts", grad_merged, returned, preferred_element_type=jnp.float32
    )
    grad_gates = slot_pick(slot_ids, grad_combine)
    grad_chosen = gates * (grad_gates - jnp.sum(gates * grad_gates, axis=-1, keepdims=True))
    grad_logits = (
        jnp.sum(grad_chosen[..., None] * ids_hot, axis=2)
        .reshape(tokens_here, EXPERTS)
        .astype(jnp.bfloat16)
    )
    grad_inner = jnp.einsum(
        "gecn,nef->gecf",
        grad_returned,
        down_full.reshape(model_width, local_count, FF),
        preferred_element_type=jnp.float32,
    )
    down_term = jnp.einsum(
        "gecn,gecf->nef", grad_returned, inner, preferred_element_type=jnp.float32
    ).reshape(model_width, local_count * FF)
    gate_vals = both[..., :FF]
    up_vals = both[..., FF:]
    sigmoid = jax.nn.sigmoid(gate_vals)
    grad_gate = grad_inner * up_vals * sigmoid * (1.0 + gate_vals * (1.0 - sigmoid))
    grad_up = grad_inner * gate_vals * sigmoid
    grad_both = jnp.concatenate([grad_gate, grad_up], axis=-1).astype(jnp.bfloat16)
    in_term = jnp.einsum(
        "gecn,gecf->nef", work_sent, grad_both, preferred_element_type=jnp.float32
    ).reshape(model_width, local_count * 2 * FF)
    work_back = jnp.einsum(
        "gecf,nef->gecn",
        grad_both,
        in_full.reshape(model_width, local_count, 2 * FF),
        preferred_element_type=jnp.float32,
    ).astype(jnp.bfloat16)
    back_sent = work_back.reshape(groups, slot_count, model_width)
    in_share, down_share = expert_sums(in_term, down_term)
    router_term = jnp.einsum(
        "tn,te->ne", normed_two, grad_logits, preferred_element_type=jnp.float32
    )
    grad_normed_two = jnp.einsum(
        "gts,gsn->gtn", dispatch, back_sent, preferred_element_type=jnp.float32
    ).reshape(tokens_here, model_width)
    grad_normed_two = grad_normed_two + jnp.einsum(
        "te,ne->tn", grad_logits, router_full, preferred_element_type=jnp.float32
    )
    gain_two_term = jnp.sum(hat_two * grad_normed_two, axis=0)
    grad_hat_two = grad_normed_two * gain_two_full.astype(jnp.float32)[None, :]
    grad_hidden = grad_result + norm_back(grad_hat_two, hat_two, factor_two)
    grad_branch = grad_hidden.astype(jnp.bfloat16)
    grad_attended = jnp.einsum(
        "td,dj->tj", grad_branch, out_full, preferred_element_type=jnp.float32
    ).astype(jnp.bfloat16)
    out_term = jnp.einsum(
        "tn,tj->nj", grad_branch, attended_low, preferred_element_type=jnp.float32
    )
    grad_grouped = grad_attended.reshape(grouped.shape)
    delta = jnp.einsum(
        "bqhgd,bqhgd->bhgq", grad_grouped.astype(jnp.float32), attended.reshape(grouped.shape)
    )
    grad_query_one, grad_keys_one, grad_values_one = attention_backward(
        grouped[0],
        keys_all[0].reshape(seq_len, KV_HEADS, HEAD_DIM),
        values_all[0].reshape(seq_len, KV_HEADS, HEAD_DIM),
        row_start,
        prefix_len[0],
        block_len,
        log_totals[0],
        grad_grouped[0],
        delta[0],
    )
    query_list = [grad_query_one]
    key_list = [grad_keys_one.reshape(seq_len, key_width)]
    value_list = [grad_values_one.reshape(seq_len, key_width)]
    key_sums, value_sums = (
        lax.psum_scatter(
            jnp.stack(key_list).astype(jnp.bfloat16), "seq", scatter_dimension=1, tiled=True
        ).astype(jnp.float32),
        lax.psum_scatter(
            jnp.stack(value_list).astype(jnp.bfloat16), "seq", scatter_dimension=1, tiled=True
        ).astype(jnp.float32),
    )
    grad_query = rounded(jnp.stack(query_list).reshape(tokens_here, HEADS, HEAD_DIM))
    grad_query = unrotate(grad_query, cosine, sine).reshape(tokens_here, query_width)
    grad_keys = rounded(key_sums.reshape(tokens_here, KV_HEADS, HEAD_DIM))
    grad_keys = unrotate(grad_keys, cosine, sine).reshape(tokens_here, key_width)
    grad_mixed = jnp.concatenate(
        [grad_query, grad_keys, value_sums.reshape(tokens_here, key_width)], axis=-1
    ).astype(jnp.bfloat16)
    qkv_term = jnp.einsum("tn,tj->nj", normed_one, grad_mixed, preferred_element_type=jnp.float32)
    grad_normed_one = jnp.einsum(
        "tj,nj->tn", grad_mixed, qkv_full, preferred_element_type=jnp.float32
    )
    gain_one_term = jnp.sum(hat_one * grad_normed_one, axis=0)
    grad_hat_one = grad_normed_one * gain_one_full.astype(jnp.float32)[None, :]
    grad_input = grad_hidden + norm_back(grad_hat_one, hat_one, factor_one)
    qkv_share, out_share, router_share, gain_one_share, gain_two_share = (
        lax.psum_scatter(qkv_term, ("seq", "fsdp"), scatter_dimension=0, tiled=True),
        lax.psum_scatter(out_term, ("seq", "fsdp"), scatter_dimension=0, tiled=True),
        lax.psum_scatter(router_term, ("seq", "fsdp"), scatter_dimension=0, tiled=True),
        lax.psum_scatter(gain_one_term, ("seq", "fsdp"), scatter_dimension=0, tiled=True),
        lax.psum_scatter(gain_two_term, ("seq", "fsdp"), scatter_dimension=0, tiled=True),
    )
    return (
        grad_input,
        (gain_one_share, qkv_share, out_share, gain_two_share, router_share, in_share, down_share),
    )


def local(
    tokens,
    cotangent,
    prefix_len,
    expert_ids,
    slot_rank,
    norm1_gain,
    qkv_weight,
    out_weight,
    norm2_gain,
    router_weight,
    in_weight,
    down_weight,
):
    groups, piece_len, model_width = tokens.shape
    seq_len = piece_len * lax.axis_size("seq")
    row_start = lax.axis_index("seq") * piece_len
    capacity = (5 * piece_len * TOP + 4 * EXPERTS - 1) // (4 * EXPERTS)
    block_len = math.gcd(seq_len, 256)
    slot_ids = routing(expert_ids, slot_rank, capacity)
    dispatch = slot_table(
        slot_ids, jnp.ones(slot_ids.shape, jnp.float32), EXPERTS * capacity
    ).astype(jnp.bfloat16)
    ids_hot = (expert_ids[..., None] == jnp.arange(EXPERTS, dtype=jnp.int32)).astype(jnp.float32)
    routes = (slot_ids, dispatch, ids_hot)
    cosine, sine = tables(row_start + jnp.arange(piece_len, dtype=jnp.int32))
    rotation = (jnp.tile(cosine, (groups, 1)), jnp.tile(sine, (groups, 1)))
    all_weights = (
        norm1_gain,
        qkv_weight,
        out_weight,
        norm2_gain,
        router_weight,
        in_weight,
        down_weight,
    )
    hidden = tokens.astype(jnp.float32).reshape(groups * piece_len, model_width)
    kept_list = []
    full_list = []
    for layer_index in range(LAYERS):
        layer_parts = tuple((weight[layer_index] for weight in all_weights))
        hidden, saved, fulls = layer_forward(
            hidden, layer_parts, routes, prefix_len, rotation, row_start, block_len
        )
        kept_list.append(saved)
        full_list.append(fulls)
    output = hidden.reshape(groups, piece_len, model_width).astype(jnp.bfloat16)
    grad_stream = cotangent.astype(jnp.float32).reshape(groups * piece_len, model_width)
    layer_shares = [None] * LAYERS
    for layer_index in reversed(range(LAYERS)):
        fulls = (
            lax.all_gather(qkv_weight[layer_index], ("seq", "fsdp"), axis=0, tiled=True),
            lax.all_gather(out_weight[layer_index], ("seq", "fsdp"), axis=0, tiled=True),
            lax.all_gather(router_weight[layer_index], ("seq", "fsdp"), axis=0, tiled=True),
            lax.all_gather(norm1_gain[layer_index], ("seq", "fsdp"), axis=0, tiled=True),
            lax.all_gather(norm2_gain[layer_index], ("seq", "fsdp"), axis=0, tiled=True),
        )
        expert_parts = (in_weight[layer_index], down_weight[layer_index])
        grad_stream, layer_shares[layer_index] = layer_backward(
            grad_stream,
            kept_list[layer_index],
            fulls,
            expert_parts,
            routes,
            prefix_len,
            rotation,
            row_start,
            block_len,
        )
    stacked = tuple((jnp.stack([shares[member] for shares in layer_shares]) for member in range(7)))
    input_grad = grad_stream.reshape(groups, piece_len, model_width)
    return (
        output,
        input_grad,
        stacked[0],
        stacked[1],
        stacked[2],
        stacked[3],
        stacked[4],
        stacked[5],
        stacked[6],
    )


def solution(mesh):
    return jax.shard_map(
        local,
        mesh=mesh,
        in_specs=(
            P("fsdp", "seq", None),
            P("fsdp", "seq", None),
            P("fsdp"),
            P("fsdp", "seq", None),
            P("fsdp", "seq", None),
            P(None, ("seq", "fsdp")),
            P(None, ("seq", "fsdp"), None),
            P(None, ("seq", "fsdp"), None),
            P(None, ("seq", "fsdp")),
            P(None, ("seq", "fsdp"), None),
            P(None, "seq", "fsdp"),
            P(None, "seq", "fsdp"),
        ),
        out_specs=(
            P("fsdp", "seq", None),
            P("fsdp", "seq", None),
            P(None, ("seq", "fsdp")),
            P(None, ("seq", "fsdp"), None),
            P(None, ("seq", "fsdp"), None),
            P(None, ("seq", "fsdp")),
            P(None, ("seq", "fsdp"), None),
            P(None, "seq", "fsdp"),
            P(None, "seq", "fsdp"),
        ),
        check_vma=False,
    )
```

profile of v0, /device:TPU:0, one launch (start us, length us, event | category | flops | bytes accessed | tf_op | source)
XLA Modules:
  0.0 5298.5 jit_solution(6561907432105621640)
XLA Ops:
  17.4 42.5 all-reduce.9
  61.5 28.5 all-gather.39.cloned.1.call-done
  103.7 103.9 %all-gather.47.cloned.1.call-done = bf16[1,384,16384]{1,2,0:T(8,128)(2,1)} async-done(((bf16[1,384,2048]{1,2,0:T(8,128)(2,1)}), bf16[1,384,16384]{1,2,0:T(8,128)(2,1)}) %all-gather.47.cloned.1.call-update) | async-done | bytes 12582928 | tf_op jit(solution)/shard_map/all_gather | solution.py:95
  207.6 65.2 %all-gather.51.cloned.1.call-done = bf16[1,384,8192]{1,2,0:T(8,128)(2,1)} async-done(((bf16[1,384,1024]{1,2,0:T(8,128)(2,1)}), bf16[1,384,8192]{1,2,0:T(8,128)(2,1)}) %all-gather.51.cloned.1.call-update) | async-done | bytes 6291472 | tf_op jit(solution)/shard_map/all_gather | solution.py:96
  286.6 42.8 all-gather.6
  364.8 40.8 all-gather.45.cloned.1.call-done
  441.2 403.2 %all-gather.49.cloned.1.call-done = bf16[1,1536,16384]{1,2,0:T(8,128)(2,1)} async-done(((bf16[1,384,16384]{1,2,0:T(8,128)(2,1)}), bf16[1,1536,16384]{1,2,0:T(8,128)(2,1)}) %all-gather.49.cloned.1.call-update) | async-done | bytes 50331664 | tf_op jit(solution)/shard_map/all_gather | solution.py:99
  844.5 32.7 convolution_bitcast_fusion.3
  885.3 188.6 %all-gather.53.cloned.1.call-done = bf16[1,1536,8192]{1,2,0:T(8,128)(2,1)} async-done(((bf16[1,384,8192]{1,2,0:T(8,128)(2,1)}), bf16[1,1536,8192]{1,2,0:T(8,128)(2,1)}) %all-gather.53.cloned.1.call-update) | async-done | bytes 25165840 | tf_op jit(solution)/shard_map/all_gather | solution.py:100
  1100.9 51.6 all-gather.55.cloned.1.call-done
  1166.5 102.8 %all-gather.63.cloned.1.call-done = bf16[1,384,16384]{1,2,0:T(8,128)(2,1)} async-done(((bf16[1,384,2048]{1,2,0:T(8,128)(2,1)}), bf16[1,384,16384]{1,2,0:T(8,128)(2,1)}) %all-gather.63.cloned.1.call-update) | async-done | bytes 12582928 | tf_op jit(solution)/shard_map/all_gather | solution.py:95
  1269.4 65.1 %all-gather.67.cloned.1.call-done = bf16[1,384,8192]{1,2,0:T(8,128)(2,1)} async-done(((bf16[1,384,1024]{1,2,0:T(8,128)(2,1)}), bf16[1,384,8192]{1,2,0:T(8,128)(2,1)}) %all-gather.67.cloned.1.call-update) | async-done | bytes 6291472 | tf_op jit(solution)/shard_map/all_gather | solution.py:96
  1334.8 42.6 all-gather.17
  1425.6 42.1 all-gather.61.cloned.1.call-done
  1488.9 417.4 %all-gather.65.cloned.1.call-done = bf16[1,1536,16384]{1,2,0:T(8,128)(2,1)} async-done(((bf16[1,384,16384]{1,2,0:T(8,128)(2,1)}), bf16[1,1536,16384]{1,2,0:T(8,128)(2,1)}) %all-gather.65.cloned.1.call-update) | async-done | bytes 50331664 | tf_op jit(solution)/shard_map/all_gather | solution.py:99
  1906.4 32.9 convolution_bitcast_fusion.2
  1947.4 188.3 %all-gather.69.cloned.1.call-done = bf16[1,1536,8192]{1,2,0:T(8,128)(2,1)} async-done(((bf16[1,384,8192]{1,2,0:T(8,128)(2,1)}), bf16[1,1536,8192]{1,2,0:T(8,128)(2,1)}) %all-gather.69.cloned.1.call-update) | async-done | bytes 25165840 | tf_op jit(solution)/shard_map/all_gather | solution.py:100
  2188.6 21.5 fusion.164
  2210.2 25.6 convolution_convert_fusion.9
  2268.8 33.8 while.82
  2335.5 80.2 %reduce-scatter.57.cloned.1.call-done = bf16[384,512]{1,0:T(8,128)(2,1)} async-done(((bf16[1536,512]{1,0:T(8,128)(2,1)}), bf16[384,512]{1,0:T(8,128)(2,1)}) %reduce-scatter.57.cloned.1.call-update) | async-done | bytes 393232
  2418.7 30.7 reduce-scatter.55.cloned.1.call-done
  2489.4 21.6 fusion.165
  2511.0 25.9 convolution_convert_fusion.8
  2568.3 33.5 while.83
  2627.9 16.7 convolution_convert_fusion.2
  2644.5 30.3 copy.352
  2674.9 16.7 convolution_convert_fusion.3
  2691.6 32.8 copy.351
  2724.5 27.9 convolution_convert_fusion
  2752.4 58.5 %copy.350 = bf16[1536,16384]{1,0:T(8,128)(2,1)} copy(bf16[1536,16384]{0,1:T(8,128)(2,1)} %bitcast.695) | data formatting | bytes 100663296 | tf_op jit(solution)/shard_map/convert_element_type | solution.py:108
  2811.4 27.5 convolution_convert_fusion.1
  2838.9 61.0 %copy.349 = bf16[1536,16384]{1,0:T(8,128)(2,1)} copy(bf16[1536,16384]{0,1:T(8,128)(2,1)} %bitcast.696) | data formatting | bytes 100663296 | tf_op jit(solution)/shard_map/convert_element_type | solution.py:108
  2952.1 47.7 reduce-scatter.51.cloned.1.call-done
  2999.9 247.8 %reduce-scatter.47.cloned.1.call-done = bf16[1536,1024]{1,0:T(8,128)(2,1)} async-done(((bf16[1536,8192]{1,0:T(8,128)(2,1)}), bf16[1536,1024]{1,0:T(8,128)(2,1)}) %reduce-scatter.47.cloned.1.call-update) | async-done | bytes 3145744 | tf_op jit(solution)/shard_map/reduce_scatter | solution.py:110
  3247.8 483.8 %reduce-scatter.43.cloned.1.call-done = bf16[1536,2048]{1,0:T(8,128)(2,1)} async-done(((bf16[1536,16384]{1,0:T(8,128)(2,1)}), bf16[1536,2048]{1,0:T(8,128)(2,1)}) %reduce-scatter.43.cloned.1.call-update) | async-done | bytes 6291472 | tf_op jit(solution)/shard_map/reduce_scatter | solution.py:107
  3731.8 483.6 %reduce-scatter.39.cloned.1.call-done = bf16[1536,2048]{1,0:T(8,128)(2,1)} async-done(((bf16[1536,16384]{1,0:T(8,128)(2,1)}), bf16[1536,2048]{1,0:T(8,128)(2,1)}) %reduce-scatter.39.cloned.1.call-update) | async-done | bytes 6291472 | tf_op jit(solution)/shard_map/reduce_scatter | solution.py:107
  4230.4 84.0 %reduce-scatter.65.cloned.1.call-done = f32[48,16]{1,0:T(8,128)} async-done(((f32[1536,16]{1,0:T(8,128)}), f32[48,16]{1,0:T(8,128)}) %reduce-scatter.65.cloned.1.call-update) | async-done | bytes 3088
  4315.2 98.7 %reduce-scatter.63.cloned.1.call-done = f32[48,16]{1,0:T(8,128)} async-done(((f32[1536,16]{1,0:T(8,128)}), f32[48,16]{1,0:T(8,128)}) %reduce-scatter.63.cloned.1.call-update) | async-done | bytes 3088
  4424.9 41.1 all-reduce.8
  4472.5 81.8 %reduce-scatter.37.cloned.1.call-done = f32[48,1536]{1,0:T(8,128)} async-done(((f32[1536,1536]{1,0:T(8,128)}), f32[48,1536]{1,0:T(8,128)}) %reduce-scatter.37.cloned.1.call-update) | async-done | bytes 294928 | tf_op jit(solution)/shard_map/reduce_scatter | solution.py:478
  4554.3 141.5 %reduce-scatter.35.cloned.1.call-done = f32[48,1536]{1,0:T(8,128)} async-done(((f32[1536,1536]{1,0:T(8,128)}), f32[48,1536]{1,0:T(8,128)}) %reduce-scatter.35.cloned.1.call-update) | async-done | bytes 294928 | tf_op jit(solution)/shard_map/reduce_scatter | solution.py:478
  4697.6 173.7 %reduce-scatter.33.cloned.1.call-done = f32[48,2560]{1,0:T(8,128)} async-done(((f32[1536,2560]{1,0:T(8,128)}), f32[48,2560]{1,0:T(8,128)}) %reduce-scatter.33.cloned.1.call-update) | async-done | bytes 491536 | tf_op jit(solution)/shard_map/reduce_scatter | solution.py:477
  4871.3 175.7 %reduce-scatter.31.cloned.1.call-done = f32[48,2560]{1,0:T(8,128)} async-done(((f32[1536,2560]{1,0:T(8,128)}), f32[48,2560]{1,0:T(8,128)}) %reduce-scatter.31.cloned.1.call-update) | async-done | bytes 491536 | tf_op jit(solution)/shard_map/reduce_scatter | solution.py:477
  5049.2 43.9 reduce-scatter.53.cloned.1.call-done
  5093.1 47.0 reduce-scatter.49.cloned.1.call-done
  5143.4 69.8 %reduce-scatter.45.cloned.1.call-done = bf16[384,2048]{1,0:T(8,128)(2,1)} async-done(((bf16[1536,2048]{1,0:T(8,128)(2,1)}), bf16[384,2048]{1,0:T(8,128)(2,1)}) %reduce-scatter.45.cloned.1.call-update) | async-done | bytes 1572880 | tf_op jit(solution)/shard_map/reduce_scatter | solution.py:115
  5213.2 73.2 %reduce-scatter.41.cloned.1.call-done = bf16[384,2048]{1,0:T(8,128)(2,1)} async-done(((bf16[1536,2048]{1,0:T(8,128)(2,1)}), bf16[384,2048]{1,0:T(8,128)(2,1)}) %reduce-scatter.41.cloned.1.call-update) | async-done | bytes 1572880 | tf_op jit(solution)/shard_map/reduce_scatter | solution.py:115
  (749 shorter events, 656.7 us)
Async XLA Ops:
  7.2 82.8 %all-gather.39.cloned.1.call-start = ((), (), s32[]{:S(2)}) async-start(), calls=%async_computation.30 | async-start | bytes 8110080 | tf_op jit(solution)/shard_map/all_gather | solution.py:244
  9.1 198.5 %all-gather.47.cloned.1.call-start = ((), (), s32[]{:S(2)}) async-start(), calls=%async_computation.34 | async-start | bytes 14155776 | tf_op jit(solution)/shard_map/all_gather | solution.py:95
  14.1 258.7 %all-gather.51.cloned.1.call-start = ((), (), s32[]{:S(2)}) async-start(), calls=%async_computation.36 | async-start | bytes 7077888 | tf_op jit(solution)/shard_map/all_gather | solution.py:96
  16.4 321.7 %all-gather.43.cloned.1.call-start = ((), (), s32[]{:S(2)}) async-start(), calls=%async_computation.32 | async-start | bytes 1966080 | tf_op jit(solution)/shard_map/all_gather | solution.py:263
  100.6 249.2 %all-gather.41.cloned.1.call-start = ((), (), s32[]{:S(2)}) async-start(), calls=%async_computation.31 | async-start | bytes 1966080 | tf_op jit(solution)/shard_map/all_gather | solution.py:264
  102.8 302.8 %all-gather.45.cloned.1.call-start = ((), (), s32[]{:S(2)}) async-start(), calls=%async_computation.33 | async-start | bytes 4866048 | tf_op jit(solution)/shard_map/all_gather | solution.py:245
  103.6 740.8 %all-gather.49.cloned.1.call-start = ((), (), s32[]{:S(2)}) async-start(), calls=%async_computation.35 | async-start | bytes 62914560 | tf_op jit(solution)/shard_map/all_gather | solution.py:99
  207.6 66.1 %copy-start.42 = (bf16[1,384,2048]{2,1,0:T(8,128)(2,1)S(1)}, bf16[1,384,2048]{2,1,0:T(8,128)(2,1)}, u32[]{:S(2)}) copy-start(bf16[1,384,2048]{2,1,0:T(8,128)(2,1)} %get-tuple-element.753) | copy-start | bytes 4718596
  207.6 866.3 %all-gather.53.cloned.1.call-start = ((), (), s32[]{:S(2)}) async-start(), calls=%async_computation.37 | async-start | bytes 31457280 | tf_op jit(solution)/shard_map/all_gather | solution.py:100
  272.9 879.6 %all-gather.55.cloned.1.call-start = ((), (), s32[]{:S(2)}) async-start(), calls=%async_computation.38 | async-start | bytes 8110080 | tf_op jit(solution)/shard_map/all_gather | solution.py:244
  273.6 995.7 %all-gather.63.cloned.1.call-start = ((), (), s32[]{:S(2)}) async-start(), calls=%async_computation.42 | async-start | bytes 14155776 | tf_op jit(solution)/shard_map/all_gather | solution.py:95
  275.3 1059.3 %all-gather.67.cloned.1.call-start = ((), (), s32[]{:S(2)}) async-start(), calls=%async_computation.44 | async-start | bytes 7077888 | tf_op jit(solution)/shard_map/all_gather | solution.py:96
  276.5 1109.0 %all-gather.57.cloned.1.call-start = ((), (), s32[]{:S(2)}) async-start(), calls=%async_computation.39 | async-start | bytes 1966080 | tf_op jit(solution)/shard_map/all_gather | solution.py:264
  363.4 47.4 copy-start
  410.8 678.7 %copy-start.13 = (f32[384,1536]{1,0:T(8,128)}, f32[384,1536]{1,0:T(8,128)S(1)}, u32[]{:S(2)}) copy-start(f32[384,1536]{1,0:T(8,128)S(1)} %get-tuple-element.786) | copy-start | bytes 7077892
  1089.5 63.0 %copy-start.74 = (f32[1536]{0:T(1024)S(1)}, f32[1536]{0:T(1024)}, u32[]{:S(2)}) copy-start(f32[1536]{0:T(1024)} %convert_element_type.555) | copy-start | bytes 18436
  1100.9 51.6 copy-start.86
  1161.6 239.6 %all-gather.59.cloned.1.call-start = ((), (), s32[]{:S(2)}) async-start(), calls=%async_computation.40 | async-start | bytes 1966080 | tf_op jit(solution)/shard_map/all_gather | solution.py:263
  1165.8 301.8 %all-gather.61.cloned.1.call-start = ((), (), s32[]{:S(2)}) async-start(), calls=%async_computation.41 | async-start | bytes 4866048 | tf_op jit(solution)/shard_map/all_gather | solution.py:245
  1166.4 739.9 %all-gather.65.cloned.1.call-start = ((), (), s32[]{:S(2)}) async-start(), calls=%async_computation.43 | async-start | bytes 62914560 | tf_op jit(solution)/shard_map/all_gather | solution.py:99
  1269.3 65.3 %copy-start.147 = (bf16[1536]{0:T(1024)(128)(2,1)S(1)}, bf16[1536]{0:T(1024)(128)(2,1)}, u32[]{:S(2)}) copy-start(bf16[1536]{0:T(1024)(128)(2,1)} %get-tuple-element.742) | copy-start | bytes 9220
  1269.3 65.3 %copy-start.105 = (bf16[1,48,16]{1,2,0:T(8,128)(2,1)S(1)}, bf16[1,48,16]{1,2,0:T(8,128)(2,1)}, u32[]{:S(2)}) copy-start(bf16[1,48,16]{1,2,0:T(8,128)(2,1)} %get-tuple-element.779) | copy-start | bytes 4612
  1269.4 866.3 %all-gather.69.cloned.1.call-start = ((), (), s32[]{:S(2)}) async-start(), calls=%async_computation.45 | async-start | bytes 31457280 | tf_op jit(solution)/shard_map/all_gather | solution.py:100
  1334.6 1081.1 %reduce-scatter.57.cloned.1.call-start = ((), (), s32[]{:S(2)}) async-start(), calls=%async_computation.47 | async-start | bytes 1966080
  1334.6 138.7 %copy-start.81 = (f32[1536]{0:T(1024)}, f32[1536]{0:T(1024)S(1)}, u32[]{:S(2)}) copy-start(f32[1536]{0:T(1024)S(1)} %convert_element_type.556) | copy-start | bytes 18436
  1424.2 49.1 copy-start.2
  1424.2 49.0 copy-start.20
  1475.0 695.7 %copy-start.28 = (bf16[384,1536]{1,0:T(8,128)(2,1)}, bf16[384,1536]{1,0:T(8,128)(2,1)S(1)}, u32[]{:S(2)}) copy-start(bf16[384,1536]{1,0:T(8,128)(2,1)S(1)} %multiply_convert_fusion.2) | copy-start | bytes 3538948
  2317.7 131.7 %reduce-scatter.55.cloned.1.call-start = ((), (), s32[]{:S(2)}) async-start(), calls=%async_computation.46 | async-start | bytes 1966080
  2332.9 601.0 %reduce-scatter.61.cloned.1.call-start = ((), (), s32[]{:S(2)}) async-start(), calls=%async_computation.49 | async-start | bytes 1966080
  2618.0 319.3 %reduce-scatter.59.cloned.1.call-start = ((), (), s32[]{:S(2)}) async-start(), calls=%async_computation.48 | async-start | bytes 1966080
  2627.8 372.0 %reduce-scatter.51.cloned.1.call-start = ((), (), s32[]{:S(2)}) async-start(), calls=%async_computation.28 | async-start | bytes 28311552 | tf_op jit(solution)/shard_map/reduce_scatter | solution.py:110
  2674.9 572.8 %reduce-scatter.47.cloned.1.call-start = ((), (), s32[]{:S(2)}) async-start(), calls=%async_computation.26 | async-start | bytes 28311552 | tf_op jit(solution)/shard_map/reduce_scatter | solution.py:110
  2724.5 1007.1 %reduce-scatter.43.cloned.1.call-start = ((), (), s32[]{:S(2)}) async-start(), calls=%async_computation.24 | async-start | bytes 56623104 | tf_op jit(solution)/shard_map/reduce_scatter | solution.py:107
  2811.0 1404.5 %reduce-scatter.39.cloned.1.call-start = ((), (), s32[]{:S(2)}) async-start(), calls=%async_computation.22 | async-start | bytes 56623104 | tf_op jit(solution)/shard_map/reduce_scatter | solution.py:107
  2899.9 1414.4 %reduce-scatter.65.cloned.1.call-start = ((), (), s32[]{:S(2)}) async-start(), calls=%async_computation.51 | async-start | bytes 811008
  2903.8 1510.1 %reduce-scatter.63.cloned.1.call-start = ((), (), s32[]{:S(2)}) async-start(), calls=%async_computation.50 | async-start | bytes 811008
  2906.1 1648.2 %reduce-scatter.37.cloned.1.call-start = ((), (), s32[]{:S(2)}) async-start(), calls=%async_computation.21 | async-start | bytes 9732096 | tf_op jit(solution)/shard_map/reduce_scatter | solution.py:478
  2912.6 1783.1 %reduce-scatter.35.cloned.1.call-start = ((), (), s32[]{:S(2)}) async-start(), calls=%async_computation.20 | async-start | bytes 9732096 | tf_op jit(solution)/shard_map/reduce_scatter | solution.py:478
  2919.7 1951.7 %reduce-scatter.33.cloned.1.call-start = ((), (), s32[]{:S(2)}) async-start(), calls=%async_computation.19 | async-start | bytes 16220160 | tf_op jit(solution)/shard_map/reduce_scatter | solution.py:477
  2930.8 2116.3 %reduce-scatter.31.cloned.1.call-start = ((), (), s32[]{:S(2)}) async-start(), calls=%async_computation.18 | async-start | bytes 16220160 | tf_op jit(solution)/shard_map/reduce_scatter | solution.py:477
  2952.1 2141.1 %reduce-scatter.53.cloned.1.call-start = ((), (), s32[]{:S(2)}) async-start(), calls=%async_computation.29 | async-start | bytes 3932160 | tf_op jit(solution)/shard_map/reduce_scatter | solution.py:118
  2999.8 2140.3 %reduce-scatter.49.cloned.1.call-start = ((), (), s32[]{:S(2)}) async-start(), calls=%async_computation.27 | async-start | bytes 3932160 | tf_op jit(solution)/shard_map/reduce_scatter | solution.py:118
  3247.7 1965.5 %reduce-scatter.45.cloned.1.call-start = ((), (), s32[]{:S(2)}) async-start(), calls=%async_computation.25 | async-start | bytes 7864320 | tf_op jit(solution)/shard_map/reduce_scatter | solution.py:115
  3731.6 483.9 %copy-start.17 = (f32[384,1536]{1,0:T(8,128)S(1)}, f32[384,1536]{1,0:T(8,128)}, u32[]{:S(2)}) copy-start(f32[384,1536]{1,0:T(8,128)} %copy-done.15) | copy-start | bytes 7077892
  3731.6 483.9 %copy-start.109 = (s32[384]{0:T(512)S(1)}, s32[384]{0:T(512)}, u32[]{:S(2)}) copy-start(s32[384]{0:T(512)} %get-tuple-element.591) | copy-start | bytes 4612
  3731.6 1554.8 %reduce-scatter.41.cloned.1.call-start = ((), (), s32[]{:S(2)}) async-start(), calls=%async_computation.23 | async-start | bytes 7864320 | tf_op jit(solution)/shard_map/reduce_scatter | solution.py:115
  4415.3 53.5 %copy-start.11 = (f32[384,1536]{1,0:T(8,128)S(1)}, f32[384,1536]{1,0:T(8,128)}, u32[]{:S(2)}) copy-start(f32[384,1536]{1,0:T(8,128)} %copy-done.9) | copy-start | bytes 7077892
  (158 other events, 1386.7 us)
Sparse Core Ops, SparseCore 0:
  11.6 78.3 all-gather.38
  92.2 115.2 all-gather.46
  209.8 62.9 all-gather.50
  274.5 30.9 all-gather.42
  307.7 31.2 all-gather.40
  341.9 63.6 all-gather.44
  407.4 437.0 all-gather.48
  846.3 227.5 all-gather.52
  1076.9 75.4 all-gather.54
  1154.0 115.2 all-gather.62
  1271.5 62.9 all-gather.66
  1336.8 31.4 all-gather.56
  1370.1 30.9 all-gather.58
  1404.0 63.5 all-gather.60
  1469.4 436.9 all-gather.64
  1908.1 227.5 all-gather.68
  2317.8 97.7 reduce-scatter.56
  2418.5 30.9 reduce-scatter.54
  2618.1 97.7 reduce-scatter.60
  2719.2 30.9 reduce-scatter.58
  2752.6 247.1 reduce-scatter.50
  3002.1 245.5 reduce-scatter.46
  3250.1 481.4 reduce-scatter.42
  3733.9 481.4 reduce-scatter.38
  4220.5 93.7 reduce-scatter.64
  4319.3 94.5 reduce-scatter.62
  4419.6 134.6 reduce-scatter.36
  4561.2 134.5 reduce-scatter.34
  4701.8 169.5 reduce-scatter.32
  4877.2 169.7 reduce-scatter.30
  5050.0 43.0 reduce-scatter.52
  5096.1 43.9 reduce-scatter.48
  5142.9 70.2 reduce-scatter.44
  5216.2 70.2 reduce-scatter.40
where the time goes:
time: 5310 us; the launch traced here: 5300 us
  waiting for transfers between devices  4080 us (77%)
  matrix products  600 us (11%)
  local copies, waits for them, and re-layouts  329 us (6%)
  blocking collectives  169 us (3%)
  other arithmetic  102 us (2%)
    reduce_scatter x2, waiting for transfers between devices, expert_sums(): lax.psum_scatter(in_term.astype(jnp.bfloat16), 'fsdp', scatter_dimension=...  967 us
    all_gather x2, waiting for transfers between devices, expert_weights(): lax.all_gather(in_cols, 'seq', axis=0, tiled=True)  821 us
    all_gather x2, waiting for transfers between devices, expert_weights(): lax.all_gather(down_cols, 'seq', axis=0, tiled=True)  377 us
    reduce_scatter x2, waiting for transfers between devices, layer_backward(): lax.psum_scatter(qkv_term, ('seq', 'fsdp'), scatter_dimension=0, tiled=True)  349 us
    reduce_scatter x2, waiting for transfers between devices, expert_sums(): lax.psum_scatter(down_term.astype(jnp.bfloat16), 'fsdp', scatter_dimensio...  296 us
    unnamed x40, waiting for transfers between devices  295 us
    reduce_scatter x2, waiting for transfers between devices, layer_backward(): lax.psum_scatter(out_term, ('seq', 'fsdp'), scatter_dimension=0, tiled=True)  223 us
    all_gather x2, waiting for transfers between devices, expert_weights(): lax.all_gather(in_part, 'fsdp', axis=1, tiled=True)  207 us
  transfers between devices with their start and end apart: 34, of which 29 were waited for; matrix products, arithmetic and copies ran while one was open for 12% of the time, Pallas kernels for 0%

commit v1 on v0

v1 whole, which is shorter than its diff:
```python
import functools

import jax
import jax.numpy as jnp
from jax import lax
from jax.experimental import pallas as pl
from jax.experimental.pallas import tpu as pltpu
from jax.sharding import Mesh
from jax.sharding import PartitionSpec as P

HEADS = 24
KV_HEADS = 8
HEAD_DIM = 64
FF = 512
TOP = 8
EXPERTS = 16
LAYERS = 2
EPS = 1e-06
THETA = 10000.0
SCALE = 0.125
Q_WIDTH = HEADS * HEAD_DIM
K_WIDTH = KV_HEADS * HEAD_DIM
PAD = 128
SEQ_AXES = ("s1", "s0")
FSDP_AXES = ("fh", "fl", "c")
ALL_AXES = SEQ_AXES + FSDP_AXES
BF = jnp.bfloat16
F32 = jnp.float32


def normalize(values):
    factor = lax.rsqrt(jnp.mean(values * values, axis=-1, keepdims=True) + EPS)
    return (values * factor, factor)


def norm_back(grad_hat, hat_values, factor):
    inner = jnp.mean(grad_hat * hat_values, axis=-1, keepdims=True)
    return factor * (grad_hat - hat_values * inner)


def tables(positions):
    steps = jnp.arange(HEAD_DIM // 2, dtype=F32)
    freqs = THETA ** (-2.0 * steps / HEAD_DIM)
    angles = positions.astype(F32)[:, None] * freqs[None, :]
    cosine, sine = jnp.cos(angles), jnp.sin(angles)
    none = jnp.zeros_like(sine)
    return (
        jnp.concatenate([cosine, cosine], axis=-1),
        jnp.concatenate([-sine, none], axis=-1),
        jnp.concatenate([none, sine], axis=-1),
    )


def rotate(values, rotation, sign):
    cosine, ahead, behind = (
        jnp.tile(table, (1, values.shape[1] // HEAD_DIM)) for table in rotation
    )
    half = HEAD_DIM // 2
    later = jnp.roll(values, -half, axis=1)
    sooner = jnp.roll(values, half, axis=1)
    return values * cosine + sign * (later * ahead + sooner * behind)


def rounded(values):
    return lax.optimization_barrier(values.astype(BF)).astype(F32)


def swap(values, axis):
    return lax.ppermute(values, axis, [(0, 1), (1, 0)])


def tie(*values):
    return lax.optimization_barrier(values)


class Side:
    def __init__(self, steps):
        self.steps = steps
        self.pending = next(steps)
        self.result = None

    def advance(self, value):
        if self.result is not None:
            return
        try:
            self.pending = self.steps.send(value)
        except StopIteration as stop:
            self.pending, self.result = (), stop.value


def meet(sides, *values):
    pending, values = tie([side.pending for side in sides], values)
    for side, value in zip(sides, pending):
        side.advance(value)
    return values[0] if len(values) == 1 else values


def ring_start(values, axis):
    size = lax.axis_size(axis)
    blocks = []
    for step in range(1, size):
        values = lax.ppermute(values, axis, [(i, (i + 1) % size) for i in range(size)])
        blocks.append(values)
    return blocks


def in_order(blocks, axis):
    size = len(blocks)
    index = lax.axis_index(axis)
    if size == 2:
        first = index == 0
        return jnp.stack(
            [jnp.where(first, blocks[0], blocks[1]), jnp.where(first, blocks[1], blocks[0])]
        )
    result = jnp.zeros((size,) + blocks[0].shape, blocks[0].dtype)
    for step, block in enumerate(blocks):
        result = lax.dynamic_update_index_in_dim(result, block, (index - step) % size, 0)
    return result


def ring_gather(values, axis):
    return in_order([values] + ring_start(values, axis), axis)


def pick(blocks, index):
    return lax.dynamic_index_in_dim(blocks, index, 0, False)


def scatter_start(blocks, axis):
    size = lax.axis_size(axis)
    index = lax.axis_index(axis)
    carried = pick(blocks, (index + size - 1) % size)
    for step in range(1, size):
        carried = lax.ppermute(carried, axis, [(i, (i + 1) % size) for i in range(size)])
        if step < size - 1:
            mine = pick(blocks, (index + size - 1 - step) % size)
            carried = (carried.astype(F32) + mine.astype(F32)).astype(BF)
    return carried


def scatter_end(blocks, carried, axis):
    return carried.astype(F32) + pick(blocks, lax.axis_index(axis)).astype(F32)


def ring_scatter(blocks, axis):
    return scatter_end(blocks, scatter_start(blocks, axis), axis)


def high_end(part, received):
    rows, cols = part.shape
    high = lax.axis_size("fh")
    low_index = lax.axis_index("s0")
    if high == 2:
        same = lax.axis_index("fh") == low_index
        return (jnp.where(same, part, received[0]), jnp.where(same, received[0], part))
    blocks = in_order([part] + received, "fh").reshape(2, high // 2, rows, cols)
    join = lambda these: these.transpose(1, 0, 2).reshape(rows, high // 2 * cols)
    return (join(pick(blocks, low_index)), join(pick(blocks, 1 - low_index)))


def low_end(keep, received):
    rows, cols = keep.shape
    return in_order([keep, received], "s0").reshape(2 * rows, cols)


def rows_end(block, received):
    return in_order([block] + received, "s1").reshape(-1, block.shape[1])


def by_rows(full):
    return full.reshape(lax.axis_size("s1"), -1, full.shape[1])


def low_split(summed):
    high = lax.axis_size("fh")
    rows = summed.shape[0] // 2
    cols = summed.shape[1] // (high // 2)
    low_index = lax.axis_index("s0")
    halves = summed.reshape(2, rows, high // 2, cols).transpose(0, 2, 1, 3)
    return (pick(halves, low_index), pick(halves, 1 - low_index))


def all_high(keep, received):
    both = in_order([keep, received], "s0")
    return both.reshape((lax.axis_size("fh"),) + keep.shape[1:])


def on_chip_pairs(message, on_chip, sides):
    half = message.shape[0] // 2
    near = swap(message, "s0")
    low = swap(message, "fl")
    own = on_chip(message, swap(message, "c"))
    near, low, own = meet(sides, near, low, own)
    far_top = swap(low[:half], "s0")
    far_bottom = swap(near[half:], "fl")
    near_mate, low_mate = tie(swap(near, "c"), swap(low, "c"))
    near, low = tie(on_chip(near, near_mate), low)
    near_sum = swap(near[1], "c")
    own_sum = swap(own[1], "c")
    low = on_chip(low, low_mate)
    far_top, far_bottom, low, near_sum, own_sum = meet(
        sides, far_top, far_bottom, low, near_sum, own_sum
    )
    far = jnp.concatenate([far_top, far_bottom], axis=0)
    return (own, near, low, far, own_sum, near_sum)


def sums_home(own, near, low, far, own_sum, near_sum, on_chip, sides, late=None, last=None):
    half = far.shape[0] // 2
    far_mate = swap(far, "c")
    low_sum = swap(low[1], "c")
    near_sum = near[0].astype(F32) + near_sum.astype(F32)
    near_top = swap(near_sum[:half].astype(BF), "s0")
    far_mate, low_sum = tie(far_mate, low_sum)
    low_sum = low[0].astype(F32) + low_sum.astype(F32)
    low_bottom = swap(low_sum[half:].astype(BF), "fl")
    far = on_chip(far, far_mate)
    near_top, low_bottom, far = tie(near_top, low_bottom, far)
    far_sum = (far[0].astype(F32) + swap(far[1], "c").astype(F32)).astype(BF)
    kept = [own[2:], near[2:], low[2:], far[2:]]
    far_top = swap(far_sum[:half], "s0")
    far_bottom = swap(far_sum[half:], "fl")
    if late is not None:
        late = late(kept)
    far_top, far_bottom, late = tie(far_top, far_bottom, late)
    near_bottom = swap((near_sum[half:] + far_bottom.astype(F32)).astype(BF), "s0")
    low_top = swap((low_sum[:half] + far_top.astype(F32)).astype(BF), "fl")
    if last is not None:
        last = last(kept)
    near_bottom, low_top, last = meet(sides, near_bottom, low_top, last)
    own_sum = own[0].astype(F32) + own_sum.astype(F32)
    top = own_sum[:half] + near_top.astype(F32) + low_top.astype(F32)
    bottom = own_sum[half:] + near_bottom.astype(F32) + low_bottom.astype(F32)
    return (jnp.concatenate([top, bottom], axis=0), kept, late, last)


def through_experts(message, on_chip, sides, late=None, last=None):
    return sums_home(
        *on_chip_pairs(message, on_chip, sides), on_chip, sides, late=late, last=last
    )


def chip_sums_home(own, near, low, far):
    half = own[0].shape[0] // 2
    own, near, low, far = (
        pair[0].astype(F32) + swap(pair[1], "c").astype(F32) for pair in (own, near, low, far)
    )
    far = far.astype(BF)
    far_top = swap(far[:half], "s0").astype(F32)
    far_bottom = swap(far[half:], "fl").astype(F32)
    near = jnp.concatenate([near[:half], near[half:] + far_bottom], axis=0).astype(BF)
    low = jnp.concatenate([low[:half] + far_top, low[half:]], axis=0).astype(BF)
    return own + swap(near, "s0").astype(F32) + swap(low, "fl").astype(F32)


def sequence_gather(keys, values, sides):
    keys_near, values_near = ring_start(keys, "s0"), ring_start(values, "s1")
    keys_near, values_near = meet(sides, keys_near, values_near)
    keys_half = in_order([keys] + keys_near, "s0")
    values_half = in_order([values] + values_near, "s1")
    keys_far, values_far = ring_start(keys_half, "s1"), ring_start(values_half, "s0")
    keys_far, values_far = meet(sides, keys_far, values_far)
    keys_all = in_order([keys_half] + keys_far, "s1")
    values_all = in_order([values_half] + values_far, "s0").transpose(1, 0, 2, 3)
    return (keys_all.reshape(-1, keys.shape[1]), values_all.reshape(-1, values.shape[1]))


def sequence_scatter(keys, values):
    outer = lax.axis_size("s1")
    width = keys.shape[1]
    keys = keys.reshape(outer, 2, -1, width)
    values = values.reshape(outer, 2, -1, width).transpose(1, 0, 2, 3)
    keys = ring_scatter(ring_scatter(keys, "s1").astype(BF), "s0")
    values = ring_scatter(ring_scatter(values, "s0").astype(BF), "s1")
    return (keys, values)


def routing(expert_ids, slot_rank, capacity):
    rows, top_count = expert_ids.shape
    pairs = expert_ids.reshape(rows * top_count)
    orders = slot_rank.reshape(rows * top_count)
    experts = jnp.arange(EXPERTS, dtype=jnp.int32)
    pair_hot = (pairs[:, None] == experts).astype(BF)
    earlier = (orders[None, :] < orders[:, None]).astype(BF)
    before = jnp.dot(earlier, pair_hot, preferred_element_type=F32)
    hot = pair_hot.astype(F32).reshape(rows, top_count, EXPERTS)
    chosen = jnp.sum(hot, axis=1)
    position = jnp.sum(before.reshape(rows, top_count, EXPERTS) * hot, axis=1)
    held = (chosen > 0.5) & (position < capacity)
    return (jnp.where(held, position, -1.0), chosen > 0.5)


VMEM_BYTES = 44 * 1024 * 1024


def params():
    return pltpu.CompilerParams(vmem_limit_bytes=VMEM_BYTES)


def hint(micros):
    flops = int(micros * 1.15e9 * 0.3)
    return pl.CostEstimate(flops=flops, bytes_accessed=1000, transcendentals=0)


def dot(left, right):
    return jnp.dot(left, right, preferred_element_type=F32)


def dot_lanes(left, right):
    return lax.dot_general(left, right, (((1,), (1,)), ((), ())), preferred_element_type=F32)


def dot_rows(left, right):
    return lax.dot_general(left, right, (((0,), (0,)), ((), ())), preferred_element_type=F32)


REPEATS = HEADS // KV_HEADS


def head_rows(block, which):
    start = which * REPEATS * HEAD_DIM
    return jnp.concatenate(
        [
            block[:, start + k * HEAD_DIM : start + (k + 1) * HEAD_DIM]
            for k in range(REPEATS)
        ],
        axis=0,
    )


def visible(block_start, rows, row_start, prefix_one, shape):
    key_pos = block_start + lax.broadcasted_iota(jnp.int32, shape, 0)
    query_pos = row_start + lax.broadcasted_iota(jnp.int32, shape, 1) % rows
    return (key_pos <= query_pos) | (key_pos < prefix_one)


def attend_kernel(place_ref, q_ref, k_ref, v_ref, o_ref, total_ref):
    rows = q_ref.shape[0]
    prefix_one, row_start = place_ref[0], place_ref[1]
    own_block = row_start // rows
    reach = jnp.maximum(row_start + rows, prefix_one)
    blocks = (reach + rows - 1) // rows
    cols = REPEATS * rows
    outs = []
    totals = []
    q_block = q_ref[...]
    for which in range(2):
        lanes = slice(which * HEAD_DIM, (which + 1) * HEAD_DIM)
        query = head_rows(q_block, which)

        def step(block, carried, masked, lanes=lanes, query=query):
            top, total, acc = carried
            start = pl.multiple_of(block * rows, rows)
            keys = k_ref[pl.ds(start, rows), lanes]
            vals = v_ref[pl.ds(start, rows), lanes]
            score = dot_lanes(keys, query)
            if masked:
                score = jnp.where(
                    visible(start, rows, row_start, prefix_one, score.shape), score, -1e30
                )
            new_top = jnp.maximum(top, jnp.max(score, axis=0, keepdims=True))
            weight = jnp.exp(score - new_top)
            shrink = jnp.exp(top - new_top)
            total = total * shrink + jnp.sum(weight, axis=0, keepdims=True)
            acc = acc * shrink + dot_rows(vals, weight.astype(BF))
            return (new_top, total, acc)

        carried = (
            jnp.full((1, cols), -1e30, F32),
            jnp.zeros((1, cols), F32),
            jnp.zeros((HEAD_DIM, cols), F32),
        )
        carried = lax.fori_loop(0, own_block, functools.partial(step, masked=False), carried)
        carried = lax.fori_loop(own_block, blocks, functools.partial(step, masked=True), carried)
        top, total, acc = carried
        result = (acc / total).T
        log_total = top + jnp.log(total)
        for k in range(REPEATS):
            outs.append(result[k * rows : (k + 1) * rows])
            totals.append(log_total[:, k * rows : (k + 1) * rows])
    o_ref[...] = jnp.concatenate(outs, axis=1).astype(BF)
    total_ref[0] = jnp.concatenate(totals + totals[:2], axis=0)


def attend(query, keys, values, place):
    rows = query.shape[0]
    seq_len = keys.shape[0]
    wide = 2 * REPEATS * HEAD_DIM
    pairs = KV_HEADS // 2
    return pl.pallas_call(
        attend_kernel,
        grid_spec=pltpu.PrefetchScalarGridSpec(
            num_scalar_prefetch=1,
            grid=(pairs,),
            in_specs=[
                pl.BlockSpec((rows, wide), lambda i, p: (0, i)),
                pl.BlockSpec((seq_len, 2 * HEAD_DIM), lambda i, p: (0, i)),
                pl.BlockSpec((seq_len, 2 * HEAD_DIM), lambda i, p: (0, i)),
            ],
            out_specs=[
                pl.BlockSpec((rows, wide), lambda i, p: (0, i)),
                pl.BlockSpec((1, 8, rows), lambda i, p: (i, 0, 0)),
            ],
        ),
        out_shape=[
            jax.ShapeDtypeStruct((rows, Q_WIDTH), BF),
            jax.ShapeDtypeStruct((pairs, 8, rows), F32),
        ],
        compiler_params=params(),
        cost_estimate=hint(36),
        name="attend",
    )(place, query, keys, values)


def attend_back_kernel(
    place_ref, q_ref, k_ref, v_ref, do_ref, o_ref, total_ref, dq_ref, dk_ref, dv_ref
):
    rows = q_ref.shape[0]
    prefix_one, row_start = place_ref[0], place_ref[1]
    own_block = row_start // rows
    reach = jnp.maximum(row_start + rows, prefix_one)
    blocks = (reach + rows - 1) // rows
    cols = REPEATS * rows
    dk_ref[...] = jnp.zeros_like(dk_ref)
    dv_ref[...] = jnp.zeros_like(dv_ref)
    q_block, do_block, o_block = q_ref[...], do_ref[...], o_ref[...]
    grads = []
    for which in range(2):
        lanes = slice(which * HEAD_DIM, (which + 1) * HEAD_DIM)
        query = head_rows(q_block, which)
        grad = head_rows(do_block, which)
        attended = head_rows(o_block, which)
        product = grad.astype(F32) * attended.astype(F32)
        delta = lax.dot_general(
            jnp.ones((8, HEAD_DIM), F32),
            product,
            (((1,), (1,)), ((), ())),
            precision=lax.Precision.HIGHEST,
            preferred_element_type=F32,
        )[:1]
        log_total = jnp.concatenate(
            [total_ref[0, which * REPEATS + k][None, :] for k in range(REPEATS)], axis=1
        )

        def step(
            block,
            acc,
            masked,
            lanes=lanes,
            query=query,
            grad=grad,
            delta=delta,
            log_total=log_total,
        ):
            start = pl.multiple_of(block * rows, rows)
            keys = k_ref[pl.ds(start, rows), lanes]
            vals = v_ref[pl.ds(start, rows), lanes]
            score = dot_lanes(keys, query)
            prob = jnp.exp(score - log_total)
            if masked:
                prob = jnp.where(
                    visible(start, rows, row_start, prefix_one, score.shape), prob, 0.0
                )
            grad_prob = dot_lanes(vals, grad)
            grad_score = (prob * (grad_prob - delta)).astype(BF)
            dv_ref[pl.ds(start, rows), lanes] = dot(prob.astype(BF), grad).astype(BF)
            dk_ref[pl.ds(start, rows), lanes] = dot(grad_score, query).astype(BF)
            return acc + dot_rows(keys, grad_score)

        acc = jnp.zeros((HEAD_DIM, cols), F32)
        acc = lax.fori_loop(0, own_block, functools.partial(step, masked=False), acc)
        acc = lax.fori_loop(own_block, blocks, functools.partial(step, masked=True), acc)
        result = (acc * SCALE).T
        for k in range(REPEATS):
            grads.append(result[k * rows : (k + 1) * rows])
    dq_ref[...] = jnp.concatenate(grads, axis=1).astype(BF)


def attend_back(query, keys, values, grad, attended, log_total, place):
    rows = query.shape[0]
    seq_len = keys.shape[0]
    wide = 2 * REPEATS * HEAD_DIM
    pairs = KV_HEADS // 2
    queries = pl.BlockSpec((rows, wide), lambda i, p: (0, i))
    stripe = pl.BlockSpec((seq_len, 2 * HEAD_DIM), lambda i, p: (0, i))
    return pl.pallas_call(
        attend_back_kernel,
        grid_spec=pltpu.PrefetchScalarGridSpec(
            num_scalar_prefetch=1,
            grid=(pairs,),
            in_specs=[
                queries,
                stripe,
                stripe,
                queries,
                queries,
                pl.BlockSpec((1, 8, rows), lambda i, p: (i, 0, 0)),
            ],
            out_specs=[queries, stripe, stripe],
        ),
        out_shape=[
            jax.ShapeDtypeStruct((rows, Q_WIDTH), BF),
            jax.ShapeDtypeStruct((seq_len, K_WIDTH), BF),
            jax.ShapeDtypeStruct((seq_len, K_WIDTH), BF),
        ],
        compiler_params=params(),
        cost_estimate=hint(54),
        name="attend_back",
    )(place, query, keys, values, grad, attended, log_total)


def slot_rows(positions_row, slots, rows):
    index = lax.broadcasted_iota(jnp.int32, (slots, rows), 0).astype(F32)
    return index == positions_row


def experts_kernel(
    sel_ref,
    own_ref,
    mate_ref,
    gate_ref,
    up_ref,
    down_ref,
    own_part_ref,
    mate_part_ref,
    sent_ref,
    act_ref,
    row_ref,
    inner_ref,
    ret_ref,
):
    rows = own_ref.shape[0]
    width = gate_ref.shape[0]
    local, slots = sent_ref.shape[1:3]
    ff = down_ref.shape[1] // local
    many = 2 * slots
    combines = []
    for p, x_ref in enumerate((own_ref, mate_ref)):
        info = dot_lanes(sel_ref[...], x_ref[:, width:])
        row_ref[p] = info
        parts = []
        for e in range(local):
            hits = slot_rows(info[e : e + 1], slots, rows)
            hot = hits.astype(F32).astype(BF)
            parts.append(jnp.where(hits, info[local + e : local + e + 1], 0.0))
            for n in range(0, width, 512):
                sent_ref[p, e, :, n : n + 512] = dot(hot, x_ref[:, n : n + 512]).astype(BF)
        combines.append(jnp.concatenate(parts, axis=0).T.astype(BF))
    for e in range(local):
        sent = sent_ref[:, e].reshape(many, width)
        for f in range(0, ff, 256):
            lanes = slice(e * ff + f, e * ff + f + 256)
            gate = dot(sent, gate_ref[:, lanes])
            up = dot(sent, up_ref[:, lanes])
            act_ref[:, e, :, f : f + 256] = gate.astype(BF).reshape(2, slots, 256)
            act_ref[:, e, :, ff + f : ff + f + 256] = up.astype(BF).reshape(2, slots, 256)
            inner_ref[:, f : f + 256] = (gate / (1.0 + jnp.exp(-gate)) * up).astype(BF)
        inner = inner_ref[...]
        for n in range(0, width, 512):
            back = dot_lanes(inner, down_ref[n : n + 512, e * ff : (e + 1) * ff])
            ret_ref[:, e * slots : (e + 1) * slots, n : n + 512] = back.astype(BF).reshape(
                2, slots, 512
            )
    for p, part_ref in enumerate((own_part_ref, mate_part_ref)):
        for n in range(0, width, 512):
            part_ref[:, n : n + 512] = dot(combines[p], ret_ref[p, :, n : n + 512]).astype(BF)


def experts(sel, own, mate, weights, slots):
    rows = own.shape[0]
    width, all_ff = weights[2].shape
    local = EXPERTS // 8
    ff = all_ff // local
    return pl.pallas_call(
        experts_kernel,
        out_shape=[
            jax.ShapeDtypeStruct((rows, width), BF),
            jax.ShapeDtypeStruct((rows, width), BF),
            jax.ShapeDtypeStruct((2, local, slots, width), BF),
            jax.ShapeDtypeStruct((2, local, slots, 2 * ff), BF),
            jax.ShapeDtypeStruct((2, 8, rows), F32),
        ],
        scratch_shapes=[
            pltpu.VMEM((2 * slots, ff), BF),
            pltpu.VMEM((2, local * slots, width), BF),
        ],
        compiler_params=params(),
        cost_estimate=hint(12),
        name="experts",
    )(sel, own, mate, *weights)


def experts_back_kernel(
    ids_ref,
    own_ref,
    mate_ref,
    row_ref,
    act_ref,
    gate_ref,
    up_ref,
    down_ref,
    own_back_ref,
    mate_back_ref,
    rows_ref,
    both_ref,
    weighted_ref,
    sent_ref,
):
    rows, width = own_ref.shape
    local, slots = act_ref.shape[1:3]
    ff = down_ref.shape[1] // local
    many = 2 * slots
    hots = []
    for p, grad_ref in enumerate((own_ref, mate_ref)):
        parts = []
        for e in range(local):
            hot = slot_rows(row_ref[p, e : e + 1], slots, rows).astype(F32)
            parts.append(hot)
            for n in range(0, width, 512):
                rows_ref[p, e, :, n : n + 512] = dot(
                    hot.astype(BF), grad_ref[:, n : n + 512]
                ).astype(BF)
        hots.append(parts)
    for e in range(local):
        gates = jnp.concatenate(
            [
                jnp.sum(
                    hots[p][e] * row_ref[p, local + e : local + e + 1], axis=1, keepdims=True
                )
                for p in range(2)
            ],
            axis=0,
        )
        grad = rows_ref[:, e].reshape(many, width)
        slot_grad = jnp.zeros((many, 1), F32)
        for f in range(0, ff, 256):
            through = dot(grad, down_ref[:, e * ff + f : e * ff + f + 256])
            gate = act_ref[:, e, :, f : f + 256].reshape(many, 256).astype(F32)
            up = act_ref[:, e, :, ff + f : ff + f + 256].reshape(many, 256).astype(F32)
            sigmoid = 1.0 / (1.0 + jnp.exp(-gate))
            silu = gate * sigmoid
            inner = silu * up
            slot_grad = slot_grad + jnp.sum(inner * through, axis=1, keepdims=True)
            grad_inner = gates * through
            grad_gate = grad_inner * up * sigmoid * (1.0 + gate * (1.0 - sigmoid))
            both_ref[:, e, :, f : f + 256] = grad_gate.astype(BF).reshape(2, slots, 256)
            both_ref[:, e, :, ff + f : ff + f + 256] = (
                (grad_inner * silu).astype(BF).reshape(2, slots, 256)
            )
            weighted_ref[:, e, :, f : f + 256] = (
                (gates * inner).astype(BF).reshape(2, slots, 256)
            )
        both = both_ref[:, e].reshape(many, 2 * ff)
        lanes = slice(e * ff, (e + 1) * ff)
        for n in range(0, width, 512):
            back = dot_lanes(both[:, :ff], gate_ref[n : n + 512, lanes])
            back = back + dot_lanes(both[:, ff:], up_ref[n : n + 512, lanes])
            sent_ref[:, e * slots : (e + 1) * slots, n : n + 512] = back.astype(BF).reshape(
                2, slots, 512
            )
        high = slot_grad.astype(BF).astype(F32)
        low = slot_grad - high
        lane = lax.broadcasted_iota(jnp.int32, (many, PAD), 1)
        expert = ids_ref[e]
        extra = jnp.where(lane == expert, high, 0.0) + jnp.where(
            lane == expert + EXPERTS, low, 0.0
        )
        sent_ref[:, e * slots : (e + 1) * slots, width:] = extra.astype(BF).reshape(
            2, slots, PAD
        )
    for p, back_ref in enumerate((own_back_ref, mate_back_ref)):
        hot = jnp.concatenate(hots[p], axis=0).T.astype(BF)
        for n in range(0, width, 512):
            back_ref[:, n : n + 512] = dot(hot, sent_ref[p, :, n : n + 512]).astype(BF)
        back_ref[:, width:] = dot(hot, sent_ref[p, :, width:]).astype(BF)


def experts_back(ids, own, mate, kept, weights):
    unused, act, row_info = kept
    rows, width = own.shape
    local, slots = act.shape[1:3]
    ff = weights[2].shape[1] // local
    vmem = pl.BlockSpec(memory_space=pltpu.VMEM)
    return pl.pallas_call(
        experts_back_kernel,
        in_specs=[pl.BlockSpec(memory_space=pltpu.SMEM)] + [vmem] * 7,
        out_shape=[
            jax.ShapeDtypeStruct((rows, width + PAD), BF),
            jax.ShapeDtypeStruct((rows, width + PAD), BF),
            jax.ShapeDtypeStruct((2, local, slots, width), BF),
            jax.ShapeDtypeStruct((2, local, slots, 2 * ff), BF),
            jax.ShapeDtypeStruct((2, local, slots, ff), BF),
        ],
        scratch_shapes=[pltpu.VMEM((2, local * slots, width + PAD), BF)],
        compiler_params=params(),
        cost_estimate=hint(12.5),
        name="experts_back",
    )(ids, own, mate, row_info, act, *weights)


def grads_kernel(*refs):
    count = (len(refs) - 2) // 2
    lefts, rights, out_ref, turned_ref = refs[:count], refs[count:-2], refs[-2], refs[-1]
    members, unused, slots, width = lefts[0].shape
    depth = members * slots

    @pl.when(pl.program_id(1) == 0)
    def turn_once():
        for k, left_ref in enumerate(lefts):
            for n in range(0, width, 256):
                turned_ref[n : n + 256, k * depth : (k + 1) * depth] = (
                    left_ref[:, 0, :, n : n + 256].reshape(depth, 256).T
                )

    right = jnp.concatenate(
        [right_ref[:, 0].reshape(depth, right_ref.shape[3]) for right_ref in rights], axis=0
    )

    def rows_of(index, unused):
        start = pl.multiple_of(index * 256, 256)
        out_ref[0, pl.ds(start, 256), :] = dot(turned_ref[pl.ds(start, 256), :], right).astype(BF)
        return unused

    lax.fori_loop(0, width // 256, rows_of, 0)


def expert_grads(lefts, rights):
    members, local, slots, width = lefts[0].shape
    cols = rights[0].shape[3]
    step = FF
    count = len(lefts)
    return pl.pallas_call(
        grads_kernel,
        grid=(local, cols // step),
        in_specs=[pl.BlockSpec((members, 1, slots, width), lambda e, n: (0, e, 0, 0))] * count
        + [pl.BlockSpec((members, 1, slots, step), lambda e, n: (0, e, 0, n))] * count,
        out_specs=pl.BlockSpec((1, width, step), lambda e, n: (n, 0, e)),
        out_shape=jax.ShapeDtypeStruct((cols // step, width, local * step), BF),
        scratch_shapes=[pltpu.VMEM((width, count * members * slots), BF)],
        compiler_params=params(),
        cost_estimate=hint(9 * local * cols // FF),
        name="expert_grads",
    )(*lefts, *rights)


def attention_in(hidden_in, lead, rotation, sides):
    query_full, key_value_full, unused, gain_one, unused = lead
    hat_one, factor_one = normalize(hidden_in)
    normed_one = (hat_one * gain_one[None, :]).astype(BF)
    mixed = dot(normed_one, key_value_full)
    keys_here = rotate(mixed[:, :K_WIDTH], rotation, 1.0).astype(BF)
    keys_all, values_all = sequence_gather(keys_here, mixed[:, K_WIDTH:].astype(BF), sides)
    query = dot(normed_one, query_full)
    query = rotate(query, rotation, 1.0).astype(BF) * jnp.asarray(SCALE, BF)
    return ((query, keys_all, values_all), (hat_one, factor_one, normed_one))


def attention_out(hidden_in, attended, out_full, lead, routes):
    router_full, gain_two = lead[2], lead[4]
    positions, chosen_mask, sel, ids, slots = routes
    rows = hidden_in.shape[0]
    hidden = hidden_in + dot_lanes(attended, out_full)
    hat_two, factor_two = normalize(hidden)
    normed_two = (hat_two * gain_two[None, :]).astype(BF)
    logits = dot(normed_two, router_full)
    gates = jax.nn.softmax(jnp.where(chosen_mask, logits, -jnp.inf), axis=-1)
    extra = jnp.concatenate(
        [gates.astype(BF), positions.astype(BF), jnp.zeros((rows, PAD - 2 * EXPERTS), BF)], axis=1
    )
    message = jnp.concatenate([normed_two, extra], axis=1)
    return (hidden, message, (hat_two, factor_two, normed_two, gates))


def norm_two_grad(grad_result, back, kept, lead):
    hat_two, factor_two, normed_two, gates = kept
    router_full, gain_two = lead[2], lead[4]
    width = grad_result.shape[1]
    gate_grad = back[:, width : width + EXPERTS] + back[:, width + EXPERTS : width + 2 * EXPERTS]
    grad_logits = (gates * (gate_grad - jnp.sum(gates * gate_grad, axis=-1, keepdims=True))).astype(
        BF
    )
    router_term = dot_rows(grad_logits, normed_two)
    grad_normed_two = back[:, :width] + dot_lanes(grad_logits, router_full)
    gain_two_term = jnp.sum(hat_two * grad_normed_two, axis=0)
    grad_hat_two = grad_normed_two * gain_two[None, :]
    grad_hidden = grad_result + norm_back(grad_hat_two, hat_two, factor_two)
    return (grad_hidden, router_term, gain_two_term)


def to_rows(term):
    return lax.psum_scatter(term.astype(BF), ALL_AXES, scatter_dimension=0, tiled=True)


def norm_one_grad(grad_hidden, grad_mixed, kept, lead):
    hat_one, factor_one, normed_one = kept
    query_full, key_value_full, unused, gain_one, unused = lead
    grad_normed_one = dot_lanes(grad_mixed[:, :Q_WIDTH], query_full)
    grad_normed_one = grad_normed_one + dot_lanes(grad_mixed[:, Q_WIDTH:], key_value_full)
    gain_one_term = jnp.sum(hat_one * grad_normed_one, axis=0)
    grad_hat_one = grad_normed_one * gain_one[None, :]
    return (grad_hidden + norm_back(grad_hat_one, hat_one, factor_one), gain_one_term)


FETCH0 = ("h0", "x0", "y0 h1", "x1 h2", "y1 x2")
FETCH1 = ("", "h0", "h1 x0", "", "h2 y0", "x1", "y1 x2")
DOWN1 = ("", "y0", "x0", "h0")
IN1 = ("y0", "y1 x0", "x1 h0", "", "h1")
DOWN0 = ("", "y0", "x0")
IN0 = ("", "y0", "y1 x0")


def local(
    tokens,
    cotangent,
    prefix_len,
    expert_ids,
    slot_rank,
    norm1_gain,
    qkv_weight,
    out_weight,
    norm2_gain,
    router_weight,
    in_weight,
    down_weight,
):
    groups, rows, width = tokens.shape
    row_start = lax.axis_index(SEQ_AXES) * rows
    capacity = (5 * rows * TOP + 4 * EXPERTS - 1) // (4 * EXPERTS)
    slots = (capacity + 15) // 16 * 16
    positions, chosen_mask = routing(expert_ids[0], slot_rank[0, 0], capacity)
    fsdp = lax.axis_size(FSDP_AXES)
    stored = EXPERTS // fsdp
    high = lax.axis_size("fh")
    mine = []
    for high_index in range(high // 2):
        for within in range(stored):
            owner = (lax.axis_index("s0") * (high // 2) + high_index) * 4
            owner = owner + lax.axis_index("fl") * 2 + lax.axis_index("c")
            mine.append(owner * stored + within)
    ids = jnp.stack(mine).astype(jnp.int32)
    lanes = jnp.arange(PAD)[None, :]
    sel = jnp.concatenate(
        [
            (lanes == ids[:, None] + EXPERTS).astype(BF),
            (lanes == ids[:, None]).astype(BF),
            jnp.zeros((8 - 2 * len(mine), PAD), BF),
        ],
        axis=0,
    )
    routes = (positions, chosen_mask, sel, ids, slots)
    rotation = tables(row_start + jnp.arange(rows, dtype=jnp.int32))
    place = jnp.stack([prefix_len[0], row_start]).astype(jnp.int32)
    part_rows = qkv_weight.shape[1]
    weight_rows = in_weight.shape[1]

    def lead_part(index):
        return jnp.concatenate(
            [
                qkv_weight[index],
                router_weight[index],
                norm1_gain[index][:, None],
                norm2_gain[index][:, None],
                jnp.zeros((part_rows, PAD - EXPERTS - 2), BF),
            ],
            axis=1,
        )

    def gather_all(part):
        return lax.all_gather(part, ALL_AXES, axis=0, tiled=True)

    def split_lead(lead):
        wide = Q_WIDTH + 2 * K_WIDTH
        return (
            lead[:, :Q_WIDTH],
            lead[:, Q_WIDTH:wide],
            lead[:, wide : wide + EXPERTS],
            lead[:, wide + EXPERTS].astype(F32),
            lead[:, wide + EXPERTS + 1].astype(F32),
        )

    def expert_parts(index):
        part = in_weight[index]
        gates = [part[:, e * 2 * FF : e * 2 * FF + FF] for e in range(stored)]
        ups = [part[:, e * 2 * FF + FF : (e + 1) * 2 * FF] for e in range(stored)]
        return [
            jnp.concatenate(gates, axis=1),
            jnp.concatenate(ups, axis=1),
            down_weight[index],
        ]

    def forward_experts(weights):
        return lambda own, mate: experts(sel, own, mate, weights, slots)

    def backward_experts(weights, kept):
        chips = iter(kept)
        return lambda own, mate: experts_back(ids, own, mate, next(chips), weights)

    def down_grads(kept):
        return expert_grads([chip[0] for chip in kept], [chip[2] for chip in kept])[0]

    def in_grads(sents, kept):
        both = expert_grads([chip[0] for chip in sents], [chip[1] for chip in kept])
        return [both[0], both[1]]

    def follow(hops, count, plan):
        names = [name for name in hops if name != "from"]
        state = {k: hops["from"][k] for k in range(count)}
        begun = {}

        def begin(name, k):
            if (name, k) not in begun:
                begun[name, k] = hops[name][0](state[k])

        def finish(name, k, raw):
            state[k] = hops[name][1](state[k], raw)

        done = set()
        for stretch in plan:
            ends = []
            for word in stretch.split():
                name, k = word[-2], int(word[-1])
                begin(name, k)
                if word[0] != "+":
                    ends.append((name, k))
            raws = yield [begun[end] for end in ends]
            for (name, k), raw in zip(ends, raws):
                finish(name, k, raw)
                done.add((name, k))
        for name in names:
            for k in range(count):
                if (name, k) not in done:
                    begin(name, k)
                    finish(name, k, begun[name, k])
        return [state[k] for k in range(count)]

    def fetch(parts, plan):
        hops = {
            "from": parts,
            "h": (lambda part: ring_start(part, "fh"), high_end),
            "x": (lambda pair: swap(pair[1], "s0"), lambda pair, raw: low_end(pair[0], raw)),
            "y": (lambda block: ring_start(block, "s1"), rows_end),
        }
        return follow(hops, len(parts), plan)

    def deliver(terms, plan):
        hops = {
            "from": [by_rows(term) for term in terms],
            "y": (
                lambda blocks: scatter_start(blocks, "s1"),
                lambda blocks, raw: low_split(scatter_end(blocks, raw, "s1").astype(BF)),
            ),
            "x": (lambda pair: swap(pair[1], "s0"), lambda pair, raw: all_high(pair[0], raw)),
            "h": (
                lambda blocks: scatter_start(blocks, "fh"),
                lambda blocks, raw: scatter_end(blocks, raw, "fh"),
            ),
        }
        return follow(hops, len(terms), plan)

    stream = tokens.astype(F32).reshape(rows, width)
    lead0 = gather_all(lead_part(0))
    lead0, parts, out_part = tie(lead0, expert_parts(0), out_weight[0])
    fetch0 = Side(fetch(parts, FETCH0))
    out0 = lax.all_gather(out_part, FSDP_AXES, axis=0, tiled=True)
    out0 = lax.all_gather(out0, SEQ_AXES, axis=0, tiled=True)
    lead0 = split_lead(lead0)
    ready0, kept_one0 = attention_in(stream, lead0, rotation, [fetch0])
    ready0 = meet([fetch0], ready0)
    attended0, total0 = attend(*ready0, place)
    attended0 = meet([fetch0], attended0)
    hidden0, message0, kept_two0 = attention_out(stream, attended0, out0, lead0, routes)
    message0, lead_next, out_next, parts = meet(
        [fetch0], message0, lead_part(1), out_weight[1], expert_parts(1)
    )
    fetch1 = Side(fetch(parts, FETCH1))
    lead1, out1 = gather_all(lead_next), gather_all(out_next)
    weights0 = fetch0.result
    merged, kept_experts0, unused, unused = through_experts(
        message0, forward_experts(weights0), [fetch1]
    )
    stream1 = hidden0 + merged
    lead1 = split_lead(lead1)
    ready1, kept_one1 = attention_in(stream1, lead1, rotation, [fetch1])
    ready1, grad = meet([fetch1], ready1, cotangent)
    attended1, total1 = attend(*ready1, place)
    attended1 = meet([fetch1], attended1)
    hidden1, message1, kept_two1 = attention_out(stream1, attended1, out1, lead1, routes)
    message1 = meet([fetch1], message1)
    while fetch1.result is None:
        meet([fetch1])
    weights1 = fetch1.result
    forward1 = forward_experts(weights1)
    own, near, low, far, unused, unused = on_chip_pairs(message1, forward1, [])
    far = forward1(far, swap(far, "c"))
    chips1 = [own, near, low, far]
    kept_experts1 = [chip[2:] for chip in chips1]

    def attention_grad(grad_hidden, ready, attended, total, out_full, sides):
        grad_branch = grad_hidden.astype(BF)
        grad_attended = dot(grad_branch, out_full).astype(BF)
        out_term = dot_rows(grad_branch, attended).astype(BF)
        grad_attended, out_term = meet(sides, grad_attended, out_term)
        grads = attend_back(*ready, grad_attended, attended, total, place)
        share = to_rows(out_term)
        return (share, meet(sides, grads))

    def mixed_grad(grads, sides, extra):
        grad_query, grad_keys, grad_values = grads
        sums = sequence_scatter(grad_keys, grad_values)
        (key_sums, value_sums), extra = meet(sides, sums, extra)
        grad_query = rotate(grad_query.astype(F32), rotation, -1.0)
        grad_keys = rotate(rounded(key_sums), rotation, -1.0)
        return (
            jnp.concatenate([grad_query, grad_keys, value_sums], axis=-1).astype(BF),
            extra,
        )

    back1, kept, down_term, unused = through_experts(
        grad.reshape(rows, width),
        backward_experts(weights1, kept_experts1),
        [],
        late=down_grads,
    )
    back1, pairs1 = tie(back1, [chip[:2] for chip in chips1])
    output = hidden1 + chip_sums_home(*pairs1)
    grad = grad.astype(F32).reshape(rows, width)
    down_side1 = Side(deliver([down_term], DOWN1))
    grad_hidden1, router1, gain_two1 = norm_two_grad(grad, back1, kept_two1, lead1)
    out_share1, grads = attention_grad(
        grad_hidden1, ready1, attended1, total1, out1, [down_side1]
    )
    grads, kept, output = tie(grads, kept, output)
    output = output.reshape(groups, rows, width).astype(BF)
    grad_mixed1, (in_terms, out_share1) = mixed_grad(
        grads, [down_side1], (in_grads(kept_experts1, kept), out_share1)
    )
    in_side1 = Side(deliver(in_terms, IN1))
    qkv_term = dot_rows(kept_one1[2], grad_mixed1).astype(BF)
    grad, gain_one1 = norm_one_grad(grad_hidden1, grad_mixed1, kept_one1, lead1)
    grad, qkv_term = tie(grad, qkv_term)
    qkv_share1 = to_rows(qkv_term)

    side1 = [down_side1, in_side1]
    back0, unused, (down_term, qkv_share1), in_terms = through_experts(
        grad.astype(BF),
        backward_experts(weights0, kept_experts0),
        side1,
        late=lambda kept: (down_grads(kept), qkv_share1),
        last=lambda kept: in_grads(kept_experts0, kept),
    )
    down_side0 = Side(deliver([down_term], DOWN0))
    in_side0 = Side(deliver(in_terms, IN0))
    sides = side1 + [down_side0, in_side0]
    grad_hidden0, router0, gain_two0 = norm_two_grad(grad, back0, kept_two0, lead0)
    out_share0, grads = attention_grad(
        grad_hidden0, ready0, attended0, total0, out0, sides
    )
    grad_mixed0, out_share0 = mixed_grad(grads, sides, out_share0)
    grad, gain_one0 = norm_one_grad(grad_hidden0, grad_mixed0, kept_one0, lead0)
    while any(side.result is None for side in sides):
        meet(sides)
    gate_share1, up_share1 = in_side1.result
    gate_share0, up_share0 = in_side0.result
    down_share1, down_share0 = down_side1.result[0], down_side0.result[0]
    gains = jnp.stack([gain_one0, gain_one1, gain_two0, gain_two1])
    smalls = jnp.concatenate(
        [router0, router1, jnp.pad(gains, ((0, PAD - 2 * EXPERTS - 4), (0, 0)))], axis=0
    ).astype(BF)
    left = jnp.concatenate([kept_one0[2], smalls], axis=0)
    right = jnp.concatenate(
        [
            jnp.pad(grad_mixed0, ((0, 0), (0, PAD))),
            jnp.pad(jnp.eye(PAD, dtype=BF), ((0, 0), (Q_WIDTH + 2 * K_WIDTH, 0))),
        ],
        axis=0,
    )
    rest = to_rows(dot_rows(left, right))
    smalls = rest[:, Q_WIDTH + 2 * K_WIDTH :].astype(F32)
    routers = jnp.stack([smalls[:, :EXPERTS], smalls[:, EXPERTS : 2 * EXPERTS]])
    gains = smalls[:, 2 * EXPERTS : 2 * EXPERTS + 4].T
    qkv_share0 = rest[:, : Q_WIDTH + 2 * K_WIDTH]

    def in_share(gate, up):
        columns = []
        for e in range(stored):
            columns += [gate[:, e * FF : (e + 1) * FF], up[:, e * FF : (e + 1) * FF]]
        return jnp.concatenate(columns, axis=1)

    return (
        output,
        grad.reshape(groups, rows, width),
        gains[:2],
        jnp.stack([qkv_share0, qkv_share1]).astype(F32),
        jnp.stack([out_share0, out_share1]).astype(F32),
        gains[2:],
        routers,
        jnp.stack([in_share(gate_share0, up_share0), in_share(gate_share1, up_share1)]),
        jnp.stack([down_share0, down_share1]),
    )


def solution(mesh):
    seq, fsdp = mesh.devices.shape
    inner_mesh = Mesh(mesh.devices.reshape(seq // 2, 2, fsdp // 4, 2, 2), ALL_AXES)
    rows = P(None, ALL_AXES)
    flat = P(None, ALL_AXES, None)
    expert = P(None, SEQ_AXES, FSDP_AXES)
    token = P(FSDP_AXES, SEQ_AXES, None)
    return jax.shard_map(
        local,
        mesh=inner_mesh,
        in_specs=(
            token,
            token,
            P(FSDP_AXES),
            token,
            token,
            rows,
            flat,
            flat,
            rows,
            flat,
            expert,
            expert,
        ),
        out_specs=(token, token, rows, flat, flat, rows, flat, expert, expert),
        check_vma=False,
    )
```

time: 5310 us -> 1640 us (0.31)
  waiting for transfers between devices: 4080 us -> 638 us
  matrix products: 600 us -> 95.3 us
  Pallas kernels: 0 us -> 406 us
  blocking collectives: 169 us -> 0 us
  local copies, waits for them, and re-layouts: 329 us -> 161 us
  starting transfers between devices: 2.17 us -> 168 us
    reduce_scatter x12 -> x4, waiting for transfers between devices: 2070 us -> 18.5 us  [to_rows(): lax.psum_scatter(term.astype(BF), ALL_AXES, scatter_dimension=0, tiled=True)]
    all_gather x16 -> x5, waiting for transfers between devices: 1710 us -> 60.7 us  [the longest x3 60.7 us: gather_all(): return lax.all_gather(part, ALL_AXES, axis=0, tiled=True)]
    ppermute x0 -> x122, waiting for transfers between devices: none -> 559 us  [the longest x20 226 us: ring_start(): lax.ppermute(values, axis, [(i, (i + 1) % size) for i in range(size)])]
    dot_general x67 -> x23, matrix products: 595 us -> 95.3 us  [the longest x8 33 us: dot_lanes(): lax.dot_general(left, right, (((1,), (1,)), ((), ())), preferred_element_...]
    pallas_call x0 -> x24, Pallas kernels: none -> 406 us  [the longest x8 104 us: experts_back(): pl.pallas_call(experts_back_kernel, in_specs=[pl.BlockSpec(memory_space=p...]
    unnamed x40 -> x9, waiting for transfers between devices: 295 us -> 0.15 us
    convert_element_type x7 -> x0, local copies, waits for them, and re-layouts: 186 us -> none  [the longest x2 119 us: expert_sums(): in_term.astype(jnp.bfloat16)]
    ppermute x0 -> x122, starting transfers between devices: none -> 167 us  [the longest x20 65.1 us: scatter_start(): lax.ppermute(carried, axis, [(i, (i + 1) % size) for i in range(size)])]
  transfers between devices with their start and end apart: 34 -> 131, of which waited for: 29 -> 55; matrix products, arithmetic and copies ran while one was open for 12% -> 17% of each run, Pallas kernels for 0% -> 25%
where the time goes in v1:
time: 1640 us; the launch traced here: 1630 us
  waiting for transfers between devices  638 us (39%)
  Pallas kernels  406 us (25%)
  starting transfers between devices  168 us (10%)
  local copies, waits for them, and re-layouts  161 us (10%)
  other arithmetic  145 us (9%)
  matrix products  95.3 us (6%)
  between operations  18.7 us (1%)
    ppermute x20, waiting for transfers between devices, ring_start(): lax.ppermute(values, axis, [(i, (i + 1) % size) for i in range(size)])  226 us
    ppermute x20, waiting for transfers between devices, scatter_start(): lax.ppermute(carried, axis, [(i, (i + 1) % size) for i in range(size)])  193 us
    ppermute x82, waiting for transfers between devices, swap(): return lax.ppermute(values, axis, [(0, 1), (1, 0)])  139 us
    pallas_call x8, Pallas kernels, experts_back(): pl.pallas_call(experts_back_kernel, in_specs=[pl.BlockSpec(memory_space=p...  104 us
    pallas_call x8, Pallas kernels, experts(): pl.pallas_call(experts_kernel, out_shape=[jax.ShapeDtypeStruct((rows, wid...  99 us
    pallas_call x4, Pallas kernels, expert_grads(): pl.pallas_call(grads_kernel, grid=(local, cols // step), in_specs=[pl.Blo...  92.7 us
    unnamed x529, local copies, waits for them, and re-layouts  82.2 us
    pallas_call x2, Pallas kernels, attend_back(): pl.pallas_call(attend_back_kernel, grid_spec=pltpu.PrefetchScalarGridSpec...  68.5 us
  transfers between devices with their start and end apart: 131, of which 55 were waited for; matrix products, arithmetic and copies ran while one was open for 17% of the time, Pallas kernels for 25%

profile of v1, /device:TPU:0, one launch (start us, length us, event | category | flops | bytes accessed | tf_op | source)
XLA Modules:
  0.0 1632.6 jit_solution(4019106710420291627)
XLA Ops:
  30.7 60.6 %all-gather.6.cloned.1.call-done = bf16[1536,2688]{1,0:T(8,128)(2,1)} async-done(((bf16[48,2688]{1,0:T(8,128)(2,1)}), bf16[1536,2688]{1,0:T(8,128)(2,1)}) %all-gather.6.cloned.1.call-update) | async-done | bytes 8257552 | tf_op jit(solution)/shard_map/all_gather | solution.py:869
  159.0 26.1 %collective-permute-done.5 = bf16[2,384,512]{2,1,0:T(8,128)(2,1)S(1)} collective-permute-done((bf16[2,384,512]{2,1,0:T(8,128)(2,1)S(1)}, bf16[2,384,512]{2,1,0:T(8,128)(2,1)S(1)}, u32[]{:S(2)}, u32[]{:S(2)}) %collective-permute-start.5) | collective-permute-done | bytes 786464 | tf_op jit(solution)/shard_map/ppermute | solution.py:102
  186.5 25.6 %collective-permute-done.3 = bf16[384,1024]{1,0:T(8,128)(2,1)S(1)} collective-permute-done((bf16[384,1024]{1,0:T(8,128)(2,1)S(1)}, bf16[384,1024]{1,0:T(8,128)(2,1)S(1)}, u32[]{:S(2)}, u32[]{:S(2)}) %collective-permute-start.3) | collective-permute-done | bytes 786464 | tf_op jit(solution)/shard_map/ppermute | solution.py:69
  218.8 28.8 %collective-permute-done.6 = bf16[768,1024]{1,0:T(8,128)(2,1)} collective-permute-done((bf16[768,1024]{1,0:T(8,128)(2,1)S(1)}, bf16[768,1024]{1,0:T(8,128)(2,1)}, u32[]{:S(2)}, u32[]{:S(2)}) %collective-permute-start.6) | collective-permute-done | bytes 1572896 | tf_op jit(solution)/shard_map/ppermute | solution.py:102
  250.4 21.0 %attend.2 = (bf16[384,1536]{1,0:T(8,128)(2,1)S(1)}, f32[4,8,384]{2,1,0:T(8,128)S(1)}) custom-call(s32[2]{0:T(128)S(1)} %pad_add_fusion.1.place_ref, bf16[384,1536]{1,0:T(8,128)(2,1)S(1)} %fusion.104.q_ref, bf16[1536,512]{1,0:T(8,128)(2,1)S(1)} %bitcast.451, bf16[1536,512]{1,0:T(8,128)(2,1)S(1)} %bitcast.449), custom_call_target="tpu_custom_call" | custom-call | flops 12419999744 | bytes 1000 | tf_op jit(solution)/shard_map/attend/pallas_call | solution.py:390
  275.5 13.9 collective-permute-start.10
  298.4 23.0 %collective-permute-done.10 = bf16[768,1024]{1,0:T(8,128)(2,1)} collective-permute-done((bf16[768,1024]{1,0:T(8,128)(2,1)}, bf16[768,1024]{1,0:T(8,128)(2,1)}, u32[]{:S(2)}, u32[]{:S(2)}) %collective-permute-start.10) | collective-permute-done | bytes 1572896 | tf_op jit(solution)/shard_map/ppermute | solution.py:102
  334.9 27.2 %collective-permute-done.17 = bf16[768,1024]{1,0:T(8,128)(2,1)S(1)} collective-permute-done((bf16[768,1024]{1,0:T(8,128)(2,1)S(1)}, bf16[768,1024]{1,0:T(8,128)(2,1)S(1)}, u32[]{:S(2)}, u32[]{:S(2)}) %collective-permute-start.17) | collective-permute-done | bytes 1572896 | tf_op jit(solution)/shard_map/ppermute | solution.py:102
  364.6 11.8 experts.8
  386.6 12.0 experts.9
  408.9 11.8 experts.10
  420.8 24.0 %collective-permute-done.13 = bf16[384,1024]{1,0:T(8,128)(2,1)S(1)} collective-permute-done((bf16[384,1024]{1,0:T(8,128)(2,1)S(1)}, bf16[384,1024]{1,0:T(8,128)(2,1)S(1)}, u32[]{:S(2)}, u32[]{:S(2)}) %collective-permute-start.13) | collective-permute-done | bytes 786464 | tf_op jit(solution)/shard_map/ppermute | solution.py:102
  452.8 12.0 experts.11
  490.7 13.7 collective-permute-done.31
  509.3 24.1 %collective-permute-done.12 = bf16[384,1024]{1,0:T(8,128)(2,1)} collective-permute-done((bf16[384,1024]{1,0:T(8,128)(2,1)S(1)}, bf16[384,1024]{1,0:T(8,128)(2,1)}, u32[]{:S(2)}, u32[]{:S(2)}) %collective-permute-start.12) | collective-permute-done | bytes 786464 | tf_op jit(solution)/shard_map/ppermute | solution.py:102
  562.3 16.4 %collective-permute-done.35 = bf16[384,512]{1,0:T(8,128)(2,1)S(1)} collective-permute-done((bf16[384,512]{1,0:T(8,128)(2,1)S(1)}, bf16[384,512]{1,0:T(8,128)(2,1)S(1)}, u32[]{:S(2)}, u32[]{:S(2)}) %collective-permute-start.35) | collective-permute-done | bytes 393248 | tf_op jit(solution)/shard_map/ppermute | solution.py:102
  578.7 14.6 collective-permute-done.36
  597.7 12.6 collective-permute-done.40
  618.0 21.4 %attend.3 = (bf16[384,1536]{1,0:T(8,128)(2,1)S(1)}, f32[4,8,384]{2,1,0:T(8,128)S(1)}) custom-call(s32[2]{0:T(128)S(1)} %pad_add_fusion.1.place_ref, bf16[384,1536]{1,0:T(8,128)(2,1)S(1)} %fusion.103.q_ref, bf16[1536,512]{1,0:T(8,128)(2,1)S(1)} %bitcast.455, bf16[1536,512]{1,0:T(8,128)(2,1)S(1)} %bitcast.453), custom_call_target="tpu_custom_call" | custom-call | flops 12419999744 | bytes 1000 | tf_op jit(solution)/shard_map/attend/pallas_call | solution.py:390
  689.0 12.8 experts.12
  707.8 12.9 experts_back.8
  737.5 12.8 experts.13
  757.1 14.2 experts_back.9
  776.5 12.8 experts.14
  791.9 12.5 experts_back.10
  815.2 13.0 experts.15
  829.2 13.4 experts_back.11
  858.4 18.4 %expert_grads.4 = bf16[1,1536,1024]{2,1,0:T(8,128)(2,1)} custom-call(bf16[2,2,240,1536]{3,2,1,0:T(8,128)(2,1)S(1)} %copy-done.24, bf16[2,2,240,1536]{3,2,1,0:T(8,128)(2,1)S(1)} %copy-done.25, bf16[2,2,240,1536]{3,2,1,0:T(8,128)(2,1)} %get-tuple-element.492.refs_2_, bf16[2,2,240,1536]{3,2,1,0:T(8,128)(2,1)} %get-tuple-element.493.refs_3_, ...), custom_call_target="tpu_custom_call" | custom-call | flops 6209999872 | bytes 1000 | tf_op jit(solution)/shard_map/expert_grads/pallas_call | solution.py:732
  936.9 34.4 %attend_back.2 = (bf16[384,1536]{1,0:T(8,128)(2,1)S(1)}, bf16[1536,512]{1,0:T(8,128)(2,1)S(1)}, bf16[1536,512]{1,0:T(8,128)(2,1)S(1)}) custom-call(s32[2]{0:T(128)S(1)} %pad_add_fusion.1.place_ref, bf16[384,1536]{1,0:T(8,128)(2,1)S(1)} %copy-done.17, bf16[1536,512]{1,0:T(8,128)(2,1)S(1)} %bitcast.456, bf16[1536,512]{1,0:T(8,128)(2,1)} %bitcast.454, ...), custom_call_target="tpu_custom_call" | custom-call | flops 18630000640 | bytes 1000 | tf_op jit(solution)/shard_map/attend_back/pallas_call | solution.py:486
  982.7 18.0 %collective-permute-start.80 = (bf16[2,384,512]{2,1,0:T(8,128)(2,1)}, bf16[2,384,512]{2,1,0:T(8,128)(2,1)S(1)}, u32[]{:S(2)}, u32[]{:S(2)}) collective-permute-start(bf16[2,384,512]{2,1,0:T(8,128)(2,1)} %dynamic-slice_bitcast_fusion.14), channel_id=1, source_target_pairs={{0,16},{16,0},{1,17},{17,1},{2,18},{18,2},{3,19},{19,3},{4,20},{20... | collective-permute-start | bytes 2359304 | tf_op jit(solution)/shard_map/ppermute | solution.py:134
  1003.7 28.1 %expert_grads.5 = bf16[2,1536,1024]{2,1,0:T(8,128)(2,1)} custom-call(bf16[2,2,240,1536]{3,2,1,0:T(8,128)(2,1)} %copy-done.61, bf16[2,2,240,1536]{3,2,1,0:T(8,128)(2,1)} %copy-done.62, bf16[2,2,240,1536]{3,2,1,0:T(8,128)(2,1)} %copy-done.63, bf16[2,2,240,1536]{3,2,1,0:T(8,128)(2,1)} %copy-done.64, bf16[2,2,240,1024]{3,2,1,0:T(8,128)(2,1)S(1)} %copy-done.42, ...), custom_call_target="tpu_custom_call" | custom-call | flops 12419999744 | bytes 1000 | tf_op jit(solution)/shard_map/expert_grads/pallas_call | solution.py:732
  1080.8 13.0 experts_back.12
  1095.1 20.2 %collective-permute-done.84 = bf16[384,1024]{1,0:T(8,128)(2,1)} collective-permute-done((bf16[384,1024]{1,0:T(8,128)(2,1)}, bf16[384,1024]{1,0:T(8,128)(2,1)}, u32[]{:S(2)}, u32[]{:S(2)}) %collective-permute-start.84) | collective-permute-done | bytes 786464 | tf_op jit(solution)/shard_map/ppermute | solution.py:134
  1121.4 12.5 experts_back.13
  1138.7 30.2 %collective-permute-done.89 = bf16[768,1024]{1,0:T(8,128)(2,1)} collective-permute-done((bf16[768,1024]{1,0:T(8,128)(2,1)}, bf16[768,1024]{1,0:T(8,128)(2,1)}, u32[]{:S(2)}, u32[]{:S(2)}) %collective-permute-start.89) | collective-permute-done | bytes 1572896 | tf_op jit(solution)/shard_map/ppermute | solution.py:134
  1169.0 12.5 experts_back.14
  1196.0 12.8 experts_back.15
  1229.7 28.2 %expert_grads.7 = bf16[2,1536,1024]{2,1,0:T(8,128)(2,1)} custom-call(bf16[2,2,240,1536]{3,2,1,0:T(8,128)(2,1)} %copy-done.57, bf16[2,2,240,1536]{3,2,1,0:T(8,128)(2,1)} %copy-done.58, bf16[2,2,240,1536]{3,2,1,0:T(8,128)(2,1)} %copy-done.59, bf16[2,2,240,1536]{3,2,1,0:T(8,128)(2,1)} %copy-done.60, bf16[2,2,240,1024]{3,2,1,0:T(8,128)(2,1)S(1)} %copy-done.50, ...), custom_call_target="tpu_custom_call" | custom-call | flops 12419999744 | bytes 1000 | tf_op jit(solution)/shard_map/expert_grads/pallas_call | solution.py:732
  1257.9 18.0 %expert_grads.6 = bf16[1,1536,1024]{2,1,0:T(8,128)(2,1)} custom-call(bf16[2,2,240,1536]{3,2,1,0:T(8,128)(2,1)S(1)} %copy-done.26, bf16[2,2,240,1536]{3,2,1,0:T(8,128)(2,1)S(1)} %copy-done.27, bf16[2,2,240,1536]{3,2,1,0:T(8,128)(2,1)} %get-tuple-element.609.refs_2_, bf16[2,2,240,1536]{3,2,1,0:T(8,128)(2,1)} %get-tuple-element.610.refs_3_, ...), custom_call_target="tpu_custom_call" | custom-call | flops 6209999872 | bytes 1000 | tf_op jit(solution)/shard_map/expert_grads/pallas_call | solution.py:732
  1320.8 34.2 %attend_back.3 = (bf16[384,1536]{1,0:T(8,128)(2,1)S(1)}, bf16[1536,512]{1,0:T(8,128)(2,1)S(1)}, bf16[1536,512]{1,0:T(8,128)(2,1)S(1)}) custom-call(s32[2]{0:T(128)S(1)} %pad_add_fusion.1.place_ref, bf16[384,1536]{1,0:T(8,128)(2,1)S(1)} %copy-done.15, bf16[1536,512]{1,0:T(8,128)(2,1)S(1)} %bitcast.452, bf16[1536,512]{1,0:T(8,128)(2,1)} %bitcast.450, ...), custom_call_target="tpu_custom_call" | custom-call | flops 18630000640 | bytes 1000 | tf_op jit(solution)/shard_map/attend_back/pallas_call | solution.py:486
  1360.7 17.9 %collective-permute-start.114 = (bf16[2,384,512]{2,1,0:T(8,128)(2,1)S(1)}, bf16[2,384,512]{2,1,0:T(8,128)(2,1)S(1)}, u32[]{:S(2)}, u32[]{:S(2)}) collective-permute-start(bf16[2,384,512]{2,1,0:T(8,128)(2,1)S(1)} %dynamic-slice_bitcast_fusion.8), channel_id=1, source_target_pairs={{0,16},{16,0},{1,17},{17,1},{2,18},{18,2},{3,19},{19,3},{4,20},{20... | collective-permute-start | bytes 2359304 | tf_op jit(solution)/shard_map/ppermute | solution.py:134
  1386.6 10.7 collective-permute-start.117
  1397.3 25.6 %collective-permute-done.114 = bf16[2,384,512]{2,1,0:T(8,128)(2,1)S(1)} collective-permute-done((bf16[2,384,512]{2,1,0:T(8,128)(2,1)S(1)}, bf16[2,384,512]{2,1,0:T(8,128)(2,1)S(1)}, u32[]{:S(2)}, u32[]{:S(2)}) %collective-permute-start.114) | collective-permute-done | bytes 786464 | tf_op jit(solution)/shard_map/ppermute | solution.py:134
  1476.9 13.3 collective-permute-done.119
  1492.1 66.0 %collective-permute-done.121 = bf16[384,1024]{1,0:T(8,128)(2,1)S(1)} collective-permute-done((bf16[384,1024]{1,0:T(8,128)(2,1)S(1)}, bf16[384,1024]{1,0:T(8,128)(2,1)S(1)}, u32[]{:S(2)}, u32[]{:S(2)}) %collective-permute-start.121) | collective-permute-done | bytes 786464 | tf_op jit(solution)/shard_map/ppermute | solution.py:134
  1560.4 17.9 %collective-permute-done.118 = bf16[384,1024]{1,0:T(8,128)(2,1)S(1)} collective-permute-done((bf16[384,1024]{1,0:T(8,128)(2,1)S(1)}, bf16[384,1024]{1,0:T(8,128)(2,1)S(1)}, u32[]{:S(2)}, u32[]{:S(2)}) %collective-permute-start.118) | collective-permute-done | bytes 786464 | tf_op jit(solution)/shard_map/ppermute | solution.py:134
  1579.0 23.2 %collective-permute-done.120 = bf16[384,1024]{1,0:T(8,128)(2,1)S(1)} collective-permute-done((bf16[384,1024]{1,0:T(8,128)(2,1)S(1)}, bf16[384,1024]{1,0:T(8,128)(2,1)S(1)}, u32[]{:S(2)}, u32[]{:S(2)}) %collective-permute-start.120) | collective-permute-done | bytes 786464 | tf_op jit(solution)/shard_map/ppermute | solution.py:134
  1606.2 14.4 reduce-scatter.11.cloned.1.call-done
  (1090 shorter events, 639.3 us)
Async XLA Ops:
  7.2 84.1 %all-gather.6.cloned.1.call-start = ((), (), s32[]{:S(2)}) async-start(), calls=%async_computation.4 | async-start | bytes 8515584 | tf_op jit(solution)/shard_map/all_gather | solution.py:869
  11.7 111.8 %all-gather.8.cloned.1.call-start = ((), (), s32[]{:S(2)}) async-start(), calls=%async_computation.5 | async-start | bytes 1327104 | tf_op jit(solution)/shard_map/all_gather | solution.py:964
  91.4 198.0 %all-gather.10.cloned.1.call-start = ((), (), s32[]{:S(2)}) async-start(), calls=%async_computation.6 | async-start | bytes 5898240 | tf_op jit(solution)/shard_map/all_gather | solution.py:965
  123.5 422.6 %all-gather.12.cloned.1.call-start = ((), (), s32[]{:S(2)}) async-start(), calls=%async_computation.7 | async-start | bytes 8515584 | tf_op jit(solution)/shard_map/all_gather | solution.py:869
  154.6 57.4 %collective-permute-start.3 = (bf16[384,1024]{1,0:T(8,128)(2,1)S(1)}, bf16[384,1024]{1,0:T(8,128)(2,1)S(1)}, u32[]{:S(2)}, u32[]{:S(2)}) collective-permute-start(bf16[384,1024]{1,0:T(8,128)(2,1)S(1)} %broadcast_select_fusion.10), channel_id=1, source_target_pairs={{0,8},{8,0},{1,9},{9,1},{2,10},{10,2},{3,11},{11,3},{4,12},{12,4},... | collective-permute-start | bytes 2359304 | tf_op jit(solution)/shard_map/ppermute | solution.py:69
  155.1 63.7 %collective-permute-start.7 = (bf16[384,1024]{1,0:T(8,128)(2,1)S(1)}, bf16[384,1024]{1,0:T(8,128)(2,1)}, u32[]{:S(2)}, u32[]{:S(2)}) collective-permute-start(bf16[384,1024]{1,0:T(8,128)(2,1)S(1)} %copy-done.155), channel_id=1, source_target_pairs={{0,4},{4,0},{1,5},{5,1},{2,6},{6,2},{3,7},{7,3},{8,12},{12,8},{9,1... | collective-permute-start | bytes 2359304 | tf_op jit(solution)/shard_map/ppermute | solution.py:102
  155.8 115.6 %collective-permute-start.9 = (bf16[384,1024]{1,0:T(8,128)(2,1)S(1)}, bf16[384,1024]{1,0:T(8,128)(2,1)}, u32[]{:S(2)}, u32[]{:S(2)}) collective-permute-start(bf16[384,1024]{1,0:T(8,128)(2,1)S(1)} %copy-done.165), channel_id=1, source_target_pairs={{0,4},{4,0},{1,5},{5,1},{2,6},{6,2},{3,7},{7,3},{8,12},{12,8},{9,1... | collective-permute-start | bytes 2359304 | tf_op jit(solution)/shard_map/ppermute | solution.py:102
  275.5 45.9 %collective-permute-start.10 = (bf16[768,1024]{1,0:T(8,128)(2,1)}, bf16[768,1024]{1,0:T(8,128)(2,1)}, u32[]{:S(2)}, u32[]{:S(2)}) collective-permute-start(bf16[768,1024]{1,0:T(8,128)(2,1)} %bitcast.34), channel_id=1, source_target_pairs={{0,16},{16,0},{1,17},{17,1},{2,18},{18,2},{3,19},{19,3},{4,20},{20... | collective-permute-start | bytes 4718600 | tf_op jit(solution)/shard_map/ppermute | solution.py:102
  321.4 330.1 %all-gather.14.cloned.1.call-start = ((), (), s32[]{:S(2)}) async-start(), calls=%async_computation.8 | async-start | bytes 4866048 | tf_op jit(solution)/shard_map/all_gather | solution.py:869
  329.4 50.5 %collective-permute-start.14 = (bf16[384,1664]{1,0:T(8,128)(2,1)S(1)}, bf16[384,1664]{1,0:T(8,128)(2,1)S(1)}, u32[]{:S(2)}, u32[]{:S(2)}) collective-permute-start(bf16[384,1664]{1,0:T(8,128)(2,1)S(1)} %concatenate.160.own_ref), channel_id=1, source_target_pairs={{0,8},{8,0},{1,9},{9,1},{2,10},{10,2},{3,11},{11,3},{4,12},{12,4},... | collective-permute-start | bytes 3833864 | tf_op jit(solution)/shard_map/ppermute | solution.py:69
  330.8 49.1 %collective-permute-start.15 = (bf16[384,1664]{1,0:T(8,128)(2,1)S(1)}, bf16[384,1664]{1,0:T(8,128)(2,1)S(1)}, u32[]{:S(2)}, u32[]{:S(2)}) collective-permute-start(bf16[384,1664]{1,0:T(8,128)(2,1)S(1)} %concatenate.160.own_ref), channel_id=1, source_target_pairs={{0,2},{2,0},{1,3},{3,1},{4,6},{6,4},{5,7},{7,5},{8,10},{10,8},{9,1... | collective-permute-start | bytes 3833864 | tf_op jit(solution)/shard_map/ppermute | solution.py:69
  380.5 64.3 %collective-permute-start.23 = (bf16[384,1536]{1,0:T(8,128)(2,1)S(1)}, bf16[384,1536]{1,0:T(8,128)(2,1)}, u32[]{:S(2)}, u32[]{:S(2)}) collective-permute-start(bf16[384,1536]{1,0:T(8,128)(2,1)S(1)} %get-tuple-element.378), channel_id=1, source_target_pairs={{0,1},{1,0},{2,3},{3,2},{4,5},{5,4},{6,7},{7,6},{8,9},{9,8},{10,11... | collective-permute-start | bytes 3538952 | tf_op jit(solution)/shard_map/ppermute | solution.py:69
  400.2 44.6 %collective-permute-start.22 = (bf16[384,1536]{1,0:T(8,128)(2,1)S(1)}, bf16[384,1536]{1,0:T(8,128)(2,1)}, u32[]{:S(2)}, u32[]{:S(2)}) collective-permute-start(bf16[384,1536]{1,0:T(8,128)(2,1)S(1)} %get-tuple-element.377), channel_id=1, source_target_pairs={{0,1},{1,0},{2,3},{3,2},{4,5},{5,4},{6,7},{7,6},{8,9},{9,8},{10,11... | collective-permute-start | bytes 3538952 | tf_op jit(solution)/shard_map/ppermute | solution.py:69
  475.1 58.3 %collective-permute-start.12 = (bf16[384,1024]{1,0:T(8,128)(2,1)S(1)}, bf16[384,1024]{1,0:T(8,128)(2,1)}, u32[]{:S(2)}, u32[]{:S(2)}) collective-permute-start(bf16[384,1024]{1,0:T(8,128)(2,1)S(1)} %copy-done.151), channel_id=1, source_target_pairs={{0,4},{4,0},{1,5},{5,1},{2,6},{6,2},{3,7},{7,3},{8,12},{12,8},{9,1... | collective-permute-start | bytes 2359304 | tf_op jit(solution)/shard_map/ppermute | solution.py:102
  476.6 121.1 %collective-permute-start.37 = (bf16[384,1024]{1,0:T(8,128)(2,1)}, bf16[384,1024]{1,0:T(8,128)(2,1)}, u32[]{:S(2)}, u32[]{:S(2)}) collective-permute-start(bf16[384,1024]{1,0:T(8,128)(2,1)} %get-tuple-element.406), channel_id=1, source_target_pairs={{0,4},{4,0},{1,5},{5,1},{2,6},{6,2},{3,7},{7,3},{8,12},{12,8},{9,1... | collective-permute-start | bytes 2359304 | tf_op jit(solution)/shard_map/ppermute | solution.py:102
  478.1 569.9 %reduce-scatter.5.cloned.1.call-start = ((), (), s32[]{:S(2)}) async-start(), calls=%async_computation.9 | async-start | bytes 4866048 | tf_op jit(solution)/shard_map/reduce_scatter | solution.py:791
  479.5 53.9 %collective-permute-start.24 = (bf16[384,1024]{1,0:T(8,128)(2,1)S(1)}, bf16[384,1024]{1,0:T(8,128)(2,1)S(1)}, u32[]{:S(2)}, u32[]{:S(2)}) collective-permute-start(bf16[384,1024]{1,0:T(8,128)(2,1)S(1)} %broadcast_select_fusion.5), channel_id=1, source_target_pairs={{0,8},{8,0},{1,9},{9,1},{2,10},{10,2},{3,11},{11,3},{4,12},{12,4},... | collective-permute-start | bytes 2359304 | tf_op jit(solution)/shard_map/ppermute | solution.py:69
  541.8 55.9 %collective-permute-start.38 = (bf16[768,1024]{1,0:T(8,128)(2,1)}, bf16[768,1024]{1,0:T(8,128)(2,1)}, u32[]{:S(2)}, u32[]{:S(2)}) collective-permute-start(bf16[768,1024]{1,0:T(8,128)(2,1)} %bitcast.61), channel_id=1, source_target_pairs={{0,16},{16,0},{1,17},{17,1},{2,18},{18,2},{3,19},{19,3},{4,20},{20... | collective-permute-start | bytes 4718600 | tf_op jit(solution)/shard_map/ppermute | solution.py:102
  544.0 67.2 %collective-permute-start.34 = (bf16[384,1024]{1,0:T(8,128)(2,1)}, bf16[384,1024]{1,0:T(8,128)(2,1)}, u32[]{:S(2)}, u32[]{:S(2)}) collective-permute-start(bf16[384,1024]{1,0:T(8,128)(2,1)} %broadcast_select_fusion.4), channel_id=1, source_target_pairs={{0,8},{8,0},{1,9},{9,1},{2,10},{10,2},{3,11},{11,3},{4,12},{12,4},... | collective-permute-start | bytes 2359304 | tf_op jit(solution)/shard_map/ppermute | solution.py:69
  678.7 48.4 %collective-permute-start.41 = (bf16[384,1536]{1,0:T(8,128)(2,1)S(1)}, bf16[384,1536]{1,0:T(8,128)(2,1)S(1)}, u32[]{:S(2)}, u32[]{:S(2)}) collective-permute-start(bf16[384,1536]{1,0:T(8,128)(2,1)S(1)} %bitcast.466), channel_id=1, source_target_pairs={{0,8},{8,0},{1,9},{9,1},{2,10},{10,2},{3,11},{11,3},{4,12},{12,4},... | collective-permute-start | bytes 3538952 | tf_op jit(solution)/shard_map/ppermute | solution.py:69
  682.1 47.4 %collective-permute-start.42 = (bf16[384,1536]{1,0:T(8,128)(2,1)S(1)}, bf16[384,1536]{1,0:T(8,128)(2,1)S(1)}, u32[]{:S(2)}, u32[]{:S(2)}) collective-permute-start(bf16[384,1536]{1,0:T(8,128)(2,1)S(1)} %bitcast.467), channel_id=1, source_target_pairs={{0,2},{2,0},{1,3},{3,1},{4,6},{6,4},{5,7},{7,5},{8,10},{10,8},{9,1... | collective-permute-start | bytes 3538952 | tf_op jit(solution)/shard_map/ppermute | solution.py:69
  730.9 45.3 %collective-permute-start.56 = (bf16[192,1664]{1,0:T(8,128)(2,1)}, bf16[192,1664]{1,0:T(8,128)(2,1)S(1)}, u32[]{:S(2)}, u32[]{:S(2)}) collective-permute-start(bf16[192,1664]{1,0:T(8,128)(2,1)} %slice.493), channel_id=1, source_target_pairs={{0,8},{8,0},{1,9},{9,1},{2,10},{10,2},{3,11},{11,3},{4,12},{12,4},... | collective-permute-start | bytes 1916936 | tf_op jit(solution)/shard_map/ppermute | solution.py:69
  733.4 73.3 %collective-permute-start.59 = (bf16[384,1664]{1,0:T(8,128)(2,1)S(1)}, bf16[384,1664]{1,0:T(8,128)(2,1)}, u32[]{:S(2)}, u32[]{:S(2)}) collective-permute-start(bf16[384,1664]{1,0:T(8,128)(2,1)S(1)} %get-tuple-element.471), channel_id=1, source_target_pairs={{0,1},{1,0},{2,3},{3,2},{4,5},{5,4},{6,7},{7,6},{8,9},{9,8},{10,11... | collective-permute-start | bytes 3833864 | tf_op jit(solution)/shard_map/ppermute | solution.py:69
  884.1 87.2 %collective-permute-start.68 = (bf16[768,1024]{1,0:T(8,128)(2,1)}, bf16[768,1024]{1,0:T(8,128)(2,1)}, u32[]{:S(2)}, u32[]{:S(2)}) collective-permute-start(bf16[768,1024]{1,0:T(8,128)(2,1)} %dynamic-slice_bitcast_fusion.5), channel_id=1, source_target_pairs={{0,16},{16,0},{1,17},{17,1},{2,18},{18,2},{3,19},{19,3},{4,20},{20... | collective-permute-start | bytes 4718600 | tf_op jit(solution)/shard_map/ppermute | solution.py:134
  897.2 78.5 %collective-permute-start.71 = (bf16[384,1536]{1,0:T(8,128)(2,1)}, bf16[384,1536]{1,0:T(8,128)(2,1)}, u32[]{:S(2)}, u32[]{:S(2)}) collective-permute-start(bf16[384,1536]{1,0:T(8,128)(2,1)} %get-tuple-element.529), channel_id=1, source_target_pairs={{0,1},{1,0},{2,3},{3,2},{4,5},{5,4},{6,7},{7,6},{8,9},{9,8},{10,11... | collective-permute-start | bytes 3538952 | tf_op jit(solution)/shard_map/ppermute | solution.py:69
  912.8 363.1 %reduce-scatter.7.cloned.1.call-start = ((), (), s32[]{:S(2)}) async-start(), calls=%async_computation.10 | async-start | bytes 8110080 | tf_op jit(solution)/shard_map/reduce_scatter | solution.py:791
  975.7 72.2 %collective-permute-start.79 = (bf16[1,384,1024]{2,1,0:T(8,128)(2,1)}, bf16[1,384,1024]{2,1,0:T(8,128)(2,1)}, u32[]{:S(2)}, u32[]{:S(2)}) collective-permute-start(bf16[1,384,1024]{2,1,0:T(8,128)(2,1)} %dynamic-slice_bitcast_fusion.15), channel_id=1, source_target_pairs={{0,8},{8,0},{1,9},{9,1},{2,10},{10,2},{3,11},{11,3},{4,12},{12,4},... | collective-permute-start | bytes 2359304 | tf_op jit(solution)/shard_map/ppermute | solution.py:69
  979.8 56.4 %collective-permute-start.82 = (bf16[2,384,512]{2,1,0:T(8,128)(2,1)}, bf16[2,384,512]{2,1,0:T(8,128)(2,1)S(1)}, u32[]{:S(2)}, u32[]{:S(2)}) collective-permute-start(bf16[2,384,512]{2,1,0:T(8,128)(2,1)} %dynamic-slice_bitcast_fusion.13), channel_id=1, source_target_pairs={{0,8},{8,0},{1,9},{9,1},{2,10},{10,2},{3,11},{11,3},{4,12},{12,4},... | collective-permute-start | bytes 2359304 | tf_op jit(solution)/shard_map/ppermute | solution.py:134
  982.7 55.7 %collective-permute-start.80 = (bf16[2,384,512]{2,1,0:T(8,128)(2,1)}, bf16[2,384,512]{2,1,0:T(8,128)(2,1)S(1)}, u32[]{:S(2)}, u32[]{:S(2)}) collective-permute-start(bf16[2,384,512]{2,1,0:T(8,128)(2,1)} %dynamic-slice_bitcast_fusion.14), channel_id=1, source_target_pairs={{0,16},{16,0},{1,17},{17,1},{2,18},{18,2},{3,19},{19,3},{4,20},{20... | collective-permute-start | bytes 2359304 | tf_op jit(solution)/shard_map/ppermute | solution.py:134
  1071.1 45.4 %collective-permute-start.85 = (bf16[768,1024]{1,0:T(8,128)(2,1)}, bf16[768,1024]{1,0:T(8,128)(2,1)}, u32[]{:S(2)}, u32[]{:S(2)}) collective-permute-start(bf16[768,1024]{1,0:T(8,128)(2,1)} %dynamic-slice_bitcast_fusion.4), channel_id=1, source_target_pairs={{0,16},{16,0},{1,17},{17,1},{2,18},{18,2},{3,19},{19,3},{4,20},{20... | collective-permute-start | bytes 4718600 | tf_op jit(solution)/shard_map/ppermute | solution.py:134
  1077.9 357.3 %reduce-scatter.9.cloned.1.call-start = ((), (), s32[]{:S(2)}) async-start(), calls=%async_computation.11 | async-start | bytes 4866048 | tf_op jit(solution)/shard_map/reduce_scatter | solution.py:791
  1118.3 50.7 %collective-permute-start.89 = (bf16[768,1024]{1,0:T(8,128)(2,1)}, bf16[768,1024]{1,0:T(8,128)(2,1)}, u32[]{:S(2)}, u32[]{:S(2)}) collective-permute-start(bf16[768,1024]{1,0:T(8,128)(2,1)} %dynamic-slice_bitcast_fusion.3), channel_id=1, source_target_pairs={{0,16},{16,0},{1,17},{17,1},{2,18},{18,2},{3,19},{19,3},{4,20},{20... | collective-permute-start | bytes 4718600 | tf_op jit(solution)/shard_map/ppermute | solution.py:134
  1120.0 67.5 %collective-permute-start.96 = (bf16[384,1664]{1,0:T(8,128)(2,1)S(1)}, bf16[384,1664]{1,0:T(8,128)(2,1)}, u32[]{:S(2)}, u32[]{:S(2)}) collective-permute-start(bf16[384,1664]{1,0:T(8,128)(2,1)S(1)} %get-tuple-element.585), channel_id=1, source_target_pairs={{0,1},{1,0},{2,3},{3,2},{4,5},{5,4},{6,7},{7,6},{8,9},{9,8},{10,11... | collective-permute-start | bytes 3833864 | tf_op jit(solution)/shard_map/ppermute | solution.py:69
  1133.9 53.6 %collective-permute-start.95 = (bf16[384,1664]{1,0:T(8,128)(2,1)S(1)}, bf16[384,1664]{1,0:T(8,128)(2,1)}, u32[]{:S(2)}, u32[]{:S(2)}) collective-permute-start(bf16[384,1664]{1,0:T(8,128)(2,1)S(1)} %get-tuple-element.584), channel_id=1, source_target_pairs={{0,1},{1,0},{2,3},{3,2},{4,5},{5,4},{6,7},{7,6},{8,9},{9,8},{10,11... | collective-permute-start | bytes 3833864 | tf_op jit(solution)/shard_map/ppermute | solution.py:69
  1136.5 51.1 %collective-permute-start.90 = (bf16[1,384,1024]{2,1,0:T(8,128)(2,1)S(1)}, bf16[1,384,1024]{2,1,0:T(8,128)(2,1)S(1)}, u32[]{:S(2)}, u32[]{:S(2)}) collective-permute-start(bf16[1,384,1024]{2,1,0:T(8,128)(2,1)S(1)} %dynamic-slice_bitcast_fusion.12), channel_id=1, source_target_pairs={{0,8},{8,0},{1,9},{9,1},{2,10},{10,2},{3,11},{11,3},{4,12},{12,4},... | collective-permute-start | bytes 2359304 | tf_op jit(solution)/shard_map/ppermute | solution.py:69
  1219.2 69.3 %collective-permute-start.102 = (bf16[384,1024]{1,0:T(8,128)(2,1)}, bf16[384,1024]{1,0:T(8,128)(2,1)}, u32[]{:S(2)}, u32[]{:S(2)}) collective-permute-start(bf16[384,1024]{1,0:T(8,128)(2,1)} %fusion.124), channel_id=1, source_target_pairs={{0,4},{4,0},{1,5},{5,1},{2,6},{6,2},{3,7},{7,3},{8,12},{12,8},{9,1... | collective-permute-start | bytes 2359304 | tf_op jit(solution)/shard_map/ppermute | solution.py:134
  1222.6 65.9 %collective-permute-start.101 = (bf16[1,384,1024]{2,1,0:T(8,128)(2,1)}, bf16[1,384,1024]{2,1,0:T(8,128)(2,1)}, u32[]{:S(2)}, u32[]{:S(2)}) collective-permute-start(bf16[1,384,1024]{2,1,0:T(8,128)(2,1)} %dynamic-slice_bitcast_fusion.11), channel_id=1, source_target_pairs={{0,8},{8,0},{1,9},{9,1},{2,10},{10,2},{3,11},{11,3},{4,12},{12,4},... | collective-permute-start | bytes 2359304 | tf_op jit(solution)/shard_map/ppermute | solution.py:69
  1227.1 48.8 %collective-permute-start.104 = (bf16[192,1664]{1,0:T(8,128)(2,1)}, bf16[192,1664]{1,0:T(8,128)(2,1)}, u32[]{:S(2)}, u32[]{:S(2)}) collective-permute-start(bf16[192,1664]{1,0:T(8,128)(2,1)} %get-tuple-element.802), channel_id=1, source_target_pairs={{0,8},{8,0},{1,9},{9,1},{2,10},{10,2},{3,11},{11,3},{4,12},{12,4},... | collective-permute-start | bytes 1916936 | tf_op jit(solution)/shard_map/ppermute | solution.py:69
  1227.8 48.1 %collective-permute-start.105 = (bf16[192,1664]{1,0:T(8,128)(2,1)}, bf16[192,1664]{1,0:T(8,128)(2,1)}, u32[]{:S(2)}, u32[]{:S(2)}) collective-permute-start(bf16[192,1664]{1,0:T(8,128)(2,1)} %get-tuple-element.801), channel_id=1, source_target_pairs={{0,2},{2,0},{1,3},{3,1},{4,6},{6,4},{5,7},{7,5},{8,10},{10,8},{9,1... | collective-permute-start | bytes 1916936 | tf_op jit(solution)/shard_map/ppermute | solution.py:69
  1288.4 68.3 %collective-permute-start.109 = (bf16[768,1024]{1,0:T(8,128)(2,1)}, bf16[768,1024]{1,0:T(8,128)(2,1)}, u32[]{:S(2)}, u32[]{:S(2)}) collective-permute-start(bf16[768,1024]{1,0:T(8,128)(2,1)} %dynamic-slice_bitcast_fusion.2), channel_id=1, source_target_pairs={{0,16},{16,0},{1,17},{17,1},{2,18},{18,2},{3,19},{19,3},{4,20},{20... | collective-permute-start | bytes 4718600 | tf_op jit(solution)/shard_map/ppermute | solution.py:134
  1316.5 304.1 %reduce-scatter.11.cloned.1.call-start = ((), (), s32[]{:S(2)}) async-start(), calls=%async_computation.12 | async-start | bytes 8515584 | tf_op jit(solution)/shard_map/reduce_scatter | solution.py:791
  1319.0 112.1 %collective-permute-start.112 = (bf16[768,1024]{1,0:T(8,128)(2,1)S(1)}, bf16[768,1024]{1,0:T(8,128)(2,1)}, u32[]{:S(2)}, u32[]{:S(2)}) collective-permute-start(bf16[768,1024]{1,0:T(8,128)(2,1)S(1)} %dynamic-slice_bitcast_fusion), channel_id=1, source_target_pairs={{0,16},{16,0},{1,17},{17,1},{2,18},{18,2},{3,19},{19,3},{4,20},{20... | collective-permute-start | bytes 4718600 | tf_op jit(solution)/shard_map/ppermute | solution.py:134
  1360.7 62.2 %collective-permute-start.114 = (bf16[2,384,512]{2,1,0:T(8,128)(2,1)S(1)}, bf16[2,384,512]{2,1,0:T(8,128)(2,1)S(1)}, u32[]{:S(2)}, u32[]{:S(2)}) collective-permute-start(bf16[2,384,512]{2,1,0:T(8,128)(2,1)S(1)} %dynamic-slice_bitcast_fusion.8), channel_id=1, source_target_pairs={{0,16},{16,0},{1,17},{17,1},{2,18},{18,2},{3,19},{19,3},{4,20},{20... | collective-permute-start | bytes 2359304 | tf_op jit(solution)/shard_map/ppermute | solution.py:134
  1380.3 50.9 %collective-permute-start.113 = (bf16[1,384,1024]{2,1,0:T(8,128)(2,1)}, bf16[1,384,1024]{2,1,0:T(8,128)(2,1)}, u32[]{:S(2)}, u32[]{:S(2)}) collective-permute-start(bf16[1,384,1024]{2,1,0:T(8,128)(2,1)} %dynamic-slice_bitcast_fusion.9), channel_id=1, source_target_pairs={{0,8},{8,0},{1,9},{9,1},{2,10},{10,2},{3,11},{11,3},{4,12},{12,4},... | collective-permute-start | bytes 2359304 | tf_op jit(solution)/shard_map/ppermute | solution.py:69
  1384.3 46.9 %collective-permute-start.111 = (bf16[1,384,1024]{2,1,0:T(8,128)(2,1)}, bf16[1,384,1024]{2,1,0:T(8,128)(2,1)}, u32[]{:S(2)}, u32[]{:S(2)}) collective-permute-start(bf16[1,384,1024]{2,1,0:T(8,128)(2,1)} %dynamic-slice_bitcast_fusion.10), channel_id=1, source_target_pairs={{0,8},{8,0},{1,9},{9,1},{2,10},{10,2},{3,11},{11,3},{4,12},{12,4},... | collective-permute-start | bytes 2359304 | tf_op jit(solution)/shard_map/ppermute | solution.py:69
  1465.4 92.7 %collective-permute-start.121 = (bf16[384,1024]{1,0:T(8,128)(2,1)S(1)}, bf16[384,1024]{1,0:T(8,128)(2,1)S(1)}, u32[]{:S(2)}, u32[]{:S(2)}) collective-permute-start(bf16[384,1024]{1,0:T(8,128)(2,1)S(1)} %fusion.108), channel_id=1, source_target_pairs={{0,4},{4,0},{1,5},{5,1},{2,6},{6,2},{3,7},{7,3},{8,12},{12,8},{9,1... | collective-permute-start | bytes 2359304 | tf_op jit(solution)/shard_map/ppermute | solution.py:134
  1468.5 109.8 %collective-permute-start.118 = (bf16[384,1024]{1,0:T(8,128)(2,1)S(1)}, bf16[384,1024]{1,0:T(8,128)(2,1)S(1)}, u32[]{:S(2)}, u32[]{:S(2)}) collective-permute-start(bf16[384,1024]{1,0:T(8,128)(2,1)S(1)} %fusion.116), channel_id=1, source_target_pairs={{0,4},{4,0},{1,5},{5,1},{2,6},{6,2},{3,7},{7,3},{8,12},{12,8},{9,1... | collective-permute-start | bytes 2359304 | tf_op jit(solution)/shard_map/ppermute | solution.py:134
  1490.6 111.5 %collective-permute-start.120 = (bf16[384,1024]{1,0:T(8,128)(2,1)S(1)}, bf16[384,1024]{1,0:T(8,128)(2,1)S(1)}, u32[]{:S(2)}, u32[]{:S(2)}) collective-permute-start(bf16[384,1024]{1,0:T(8,128)(2,1)S(1)} %fusion.112), channel_id=1, source_target_pairs={{0,4},{4,0},{1,5},{5,1},{2,6},{6,2},{3,7},{7,3},{8,12},{12,8},{9,1... | collective-permute-start | bytes 2359304 | tf_op jit(solution)/shard_map/ppermute | solution.py:134
  (344 other events, 4956.3 us)
Sparse Core Ops, SparseCore 0:
  11.8 79.5 all-gather.5
  93.0 21.2 all-gather.7
  123.6 85.2 all-gather.9
  321.5 112.2 all-gather.11
  478.2 108.3 all-gather.13
  912.9 104.4 reduce-scatter.4
  1078.1 163.7 reduce-scatter.6
  1316.6 118.5 reduce-scatter.8
  1455.0 165.5 reduce-scatter.10

commit v2 on v1

--- a/solution.py
+++ b/solution.py
@@ -76,8 +76,8 @@
 class Side:
     def __init__(self, steps):
         self.steps = steps
-        self.pending = next(steps)
         self.result = None
+        self.advance(None)
 
     def advance(self, value):
         if self.result is not None:
@@ -514,13 +514,29 @@
     return index == positions_row
 
 
+def start_copies(sources, targets, sems):
+    copies = [
+        pltpu.make_async_copy(source, target, sems.at[k])
+        for k, (source, target) in enumerate(zip(sources, targets))
+    ]
+    for copy in copies:
+        copy.start()
+    return copies
+
+
+def weight_scratch(weights):
+    return [pltpu.VMEM(weight.shape, BF) for weight in weights] + [
+        pltpu.SemaphoreType.DMA((len(weights),))
+    ]
+
+
 def experts_kernel(
     sel_ref,
     own_ref,
     mate_ref,
-    gate_ref,
-    up_ref,
-    down_ref,
+    gate_any,
+    up_any,
+    down_any,
     own_part_ref,
     mate_part_ref,
     sent_ref,
@@ -528,7 +544,12 @@
     row_ref,
     inner_ref,
     ret_ref,
+    gate_ref,
+    up_ref,
+    down_ref,
+    sems,
 ):
+    copies = start_copies((gate_any, up_any, down_any), (gate_ref, up_ref, down_ref), sems)
     rows = own_ref.shape[0]
     width = gate_ref.shape[0]
     local, slots = sent_ref.shape[1:3]
@@ -546,6 +567,8 @@
             for n in range(0, width, 512):
                 sent_ref[p, e, :, n : n + 512] = dot(hot, x_ref[:, n : n + 512]).astype(BF)
         combines.append(jnp.concatenate(parts, axis=0).T.astype(BF))
+    copies[0].wait()
+    copies[1].wait()
     for e in range(local):
         sent = sent_ref[:, e].reshape(many, width)
         for f in range(0, ff, 256):
@@ -556,6 +579,8 @@
             act_ref[:, e, :, ff + f : ff + f + 256] = up.astype(BF).reshape(2, slots, 256)
             inner_ref[:, f : f + 256] = (gate / (1.0 + jnp.exp(-gate)) * up).astype(BF)
         inner = inner_ref[...]
+        if e == 0:
+            copies[2].wait()
         for n in range(0, width, 512):
             back = dot_lanes(inner, down_ref[n : n + 512, e * ff : (e + 1) * ff])
             ret_ref[:, e * slots : (e + 1) * slots, n : n + 512] = back.astype(BF).reshape(
@@ -571,8 +596,10 @@
     width, all_ff = weights[2].shape
     local = EXPERTS // 8
     ff = all_ff // local
+    vmem = pl.BlockSpec(memory_space=pltpu.VMEM)
     return pl.pallas_call(
         experts_kernel,
+        in_specs=[vmem] * 3 + [pl.BlockSpec(memory_space=pl.ANY)] * 3,
         out_shape=[
             jax.ShapeDtypeStruct((rows, width), BF),
             jax.ShapeDtypeStruct((rows, width), BF),
@@ -583,7 +610,8 @@
         scratch_shapes=[
             pltpu.VMEM((2 * slots, ff), BF),
             pltpu.VMEM((2, local * slots, width), BF),
-        ],
+        ]
+        + weight_scratch(weights),
         compiler_params=params(),
         cost_estimate=hint(12),
         name="experts",
@@ -596,16 +624,21 @@
     mate_ref,
     row_ref,
     act_ref,
-    gate_ref,
-    up_ref,
-    down_ref,
+    gate_any,
+    up_any,
+    down_any,
     own_back_ref,
     mate_back_ref,
     rows_ref,
     both_ref,
     weighted_ref,
     sent_ref,
+    down_ref,
+    gate_ref,
+    up_ref,
+    sems,
 ):
+    copies = start_copies((down_any, gate_any, up_any), (down_ref, gate_ref, up_ref), sems)
     rows, width = own_ref.shape
     local, slots = act_ref.shape[1:3]
     ff = down_ref.shape[1] // local
@@ -621,6 +654,7 @@
                     hot.astype(BF), grad_ref[:, n : n + 512]
                 ).astype(BF)
         hots.append(parts)
+    copies[0].wait()
     for e in range(local):
         gates = jnp.concatenate(
             [
@@ -651,6 +685,9 @@
                 (gates * inner).astype(BF).reshape(2, slots, 256)
             )
         both = both_ref[:, e].reshape(many, 2 * ff)
+        if e == 0:
+            copies[1].wait()
+            copies[2].wait()
         lanes = slice(e * ff, (e + 1) * ff)
         for n in range(0, width, 512):
             back = dot_lanes(both[:, :ff], gate_ref[n : n + 512, lanes])
@@ -683,7 +720,9 @@
     vmem = pl.BlockSpec(memory_space=pltpu.VMEM)
     return pl.pallas_call(
         experts_back_kernel,
-        in_specs=[pl.BlockSpec(memory_space=pltpu.SMEM)] + [vmem] * 7,
+        in_specs=[pl.BlockSpec(memory_space=pltpu.SMEM)]
+        + [vmem] * 4
+        + [pl.BlockSpec(memory_space=pl.ANY)] * 3,
         out_shape=[
             jax.ShapeDtypeStruct((rows, width + PAD), BF),
             jax.ShapeDtypeStruct((rows, width + PAD), BF),
@@ -691,7 +730,7 @@
             jax.ShapeDtypeStruct((2, local, slots, 2 * ff), BF),
             jax.ShapeDtypeStruct((2, local, slots, ff), BF),
         ],
-        scratch_shapes=[pltpu.VMEM((2, local * slots, width + PAD), BF)],
+        scratch_shapes=[pltpu.VMEM((2, local * slots, width + PAD), BF)] + weight_scratch(weights),
         compiler_params=params(),
         cost_estimate=hint(12.5),
         name="experts_back",
@@ -801,11 +840,11 @@
     return (grad_hidden + norm_back(grad_hat_one, hat_one, factor_one), gain_one_term)
 
 
-FETCH0 = ("h0", "x0", "y0 h1", "x1 h2", "y1 x2")
+FETCH0 = ("", "h0", "", "h1 x0", "h2 x1 y0")
 FETCH1 = ("", "h0", "h1 x0", "", "h2 y0", "x1", "y1 x2")
 DOWN1 = ("", "y0", "x0", "h0")
 IN1 = ("y0", "y1 x0", "x1 h0", "", "h1")
-DOWN0 = ("", "y0", "x0")
+DOWN0 = ()
 IN0 = ("", "y0", "y1 x0")
 
 
@@ -1041,21 +1080,25 @@
     qkv_share1 = to_rows(qkv_term)
 
     side1 = [down_side1, in_side1]
-    back0, unused, (down_term, qkv_share1), in_terms = through_experts(
+    back0, kept, qkv_share1, in_terms = through_experts(
         grad.astype(BF),
         backward_experts(weights0, kept_experts0),
         side1,
-        late=lambda kept: (down_grads(kept), qkv_share1),
+        late=lambda kept: qkv_share1,
         last=lambda kept: in_grads(kept_experts0, kept),
     )
-    down_side0 = Side(deliver([down_term], DOWN0))
     in_side0 = Side(deliver(in_terms, IN0))
-    sides = side1 + [down_side0, in_side0]
+    sides = side1 + [in_side0]
     grad_hidden0, router0, gain_two0 = norm_two_grad(grad, back0, kept_two0, lead0)
     out_share0, grads = attention_grad(
         grad_hidden0, ready0, attended0, total0, out0, sides
     )
-    grad_mixed0, out_share0 = mixed_grad(grads, sides, out_share0)
+    grads, kept = tie(grads, kept)
+    grad_mixed0, (out_share0, down_term) = mixed_grad(
+        grads, sides, (out_share0, down_grads(kept))
+    )
+    down_side0 = Side(deliver([down_term], DOWN0))
+    sides = sides + [down_side0]
     grad, gain_one0 = norm_one_grad(grad_hidden0, grad_mixed0, kept_one0, lead0)
     while any(side.result is None for side in sides):
         meet(sides)

time: 1640 us -> 1620 us (0.988)
    unnamed x529 -> x509, local copies, waits for them, and re-layouts: 82.2 us -> 80.8 us
  transfers between devices with their start and end apart: 131 -> 131, of which waited for: 55 -> 54; matrix products, arithmetic and copies ran while one was open for 17% -> 16% of each run, Pallas kernels for 25% -> 24%
where the time goes in v2:
time: 1620 us; the launch traced here: 1610 us
  waiting for transfers between devices  623 us (38%)
  Pallas kernels  395 us (24%)
  starting transfers between devices  175 us (11%)
  local copies, waits for them, and re-layouts  164 us (10%)
  other arithmetic  144 us (9%)
  matrix products  94.1 us (6%)
  between operations  18.5 us (1%)
    ppermute x20, waiting for transfers between devices, ring_start(): lax.ppermute(values, axis, [(i, (i + 1) % size) for i in range(size)])  224 us
    ppermute x20, waiting for transfers between devices, scatter_start(): lax.ppermute(carried, axis, [(i, (i + 1) % size) for i in range(size)])  184 us
    ppermute x82, waiting for transfers between devices, swap(): return lax.ppermute(values, axis, [(0, 1), (1, 0)])  144 us
    pallas_call x8, Pallas kernels, experts_back(): pl.pallas_call(experts_back_kernel, in_specs=[pl.BlockSpec(memory_space=p...  97.8 us
    pallas_call x8, Pallas kernels, experts(): pl.pallas_call(experts_kernel, in_specs=[vmem] * 3 + [pl.BlockSpec(memory...  93 us
    pallas_call x4, Pallas kernels, expert_grads(): pl.pallas_call(grads_kernel, grid=(local, cols // step), in_specs=[pl.Blo...  92.8 us
    unnamed x509, local copies, waits for them, and re-layouts  80.8 us
    ppermute x82, starting transfers between devices, swap(): return lax.ppermute(values, axis, [(0, 1), (1, 0)])  74.6 us
  transfers between devices with their start and end apart: 131, of which 54 were waited for; matrix products, arithmetic and copies ran while one was open for 16% of the time, Pallas kernels for 24%

profile of v2, /device:TPU:0, one launch (start us, length us, event | category | flops | bytes accessed | tf_op | source)
XLA Modules:
  0.0 1612.9 jit_solution(13277905074127310690)
XLA Ops:
  24.6 66.7 %all-gather.6.cloned.1.call-done = bf16[1536,2688]{1,0:T(8,128)(2,1)} async-done(((bf16[48,2688]{1,0:T(8,128)(2,1)}), bf16[1536,2688]{1,0:T(8,128)(2,1)}) %all-gather.6.cloned.1.call-update) | async-done | bytes 8257552 | tf_op jit(solution)/shard_map/all_gather | solution.py:908
  156.2 46.6 %collective-permute-done.2 = bf16[384,1024]{1,0:T(8,128)(2,1)S(1)} collective-permute-done((bf16[384,1024]{1,0:T(8,128)(2,1)S(1)}, bf16[384,1024]{1,0:T(8,128)(2,1)S(1)}, u32[]{:S(2)}, u32[]{:S(2)}) %collective-permute-start.2) | collective-permute-done | bytes 786464 | tf_op jit(solution)/shard_map/ppermute | solution.py:102
  208.0 21.2 %attend.2 = (bf16[384,1536]{1,0:T(8,128)(2,1)S(1)}, f32[4,8,384]{2,1,0:T(8,128)S(1)}) custom-call(s32[2]{0:T(128)S(1)} %pad_add_fusion.1.place_ref, bf16[384,1536]{1,0:T(8,128)(2,1)S(1)} %fusion.104.q_ref, bf16[1536,512]{1,0:T(8,128)(2,1)S(1)} %bitcast.451, bf16[1536,512]{1,0:T(8,128)(2,1)S(1)} %bitcast.449), custom_call_target="tpu_custom_call" | custom-call | flops 12419999744 | bytes 1000 | tf_op jit(solution)/shard_map/attend/pallas_call | solution.py:390
  284.9 13.4 collective-permute-done.16
  307.5 18.4 %collective-permute-done.15 = bf16[768,1024]{1,0:T(8,128)(2,1)S(1)} collective-permute-done((bf16[768,1024]{1,0:T(8,128)(2,1)S(1)}, bf16[768,1024]{1,0:T(8,128)(2,1)S(1)}, u32[]{:S(2)}, u32[]{:S(2)}) %collective-permute-start.15) | collective-permute-done | bytes 1572896 | tf_op jit(solution)/shard_map/ppermute | solution.py:102
  328.4 41.7 %collective-permute-done.17 = bf16[768,1024]{1,0:T(8,128)(2,1)S(1)} collective-permute-done((bf16[768,1024]{1,0:T(8,128)(2,1)S(1)}, bf16[768,1024]{1,0:T(8,128)(2,1)S(1)}, u32[]{:S(2)}, u32[]{:S(2)}) %collective-permute-start.17) | collective-permute-done | bytes 1572896 | tf_op jit(solution)/shard_map/ppermute | solution.py:102
  372.6 11.1 experts.8
  393.7 11.2 experts.9
  411.3 11.0 experts.10
  422.4 21.5 %collective-permute-done.11 = bf16[384,1024]{1,0:T(8,128)(2,1)S(1)} collective-permute-done((bf16[384,1024]{1,0:T(8,128)(2,1)S(1)}, bf16[384,1024]{1,0:T(8,128)(2,1)S(1)}, u32[]{:S(2)}, u32[]{:S(2)}) %collective-permute-start.11) | collective-permute-done | bytes 786464 | tf_op jit(solution)/shard_map/ppermute | solution.py:102
  452.1 11.0 experts.11
  479.7 10.3 collective-permute-done.30
  490.1 13.2 collective-permute-done.31
  508.8 22.9 %collective-permute-done.10 = bf16[384,1024]{1,0:T(8,128)(2,1)} collective-permute-done((bf16[384,1024]{1,0:T(8,128)(2,1)S(1)}, bf16[384,1024]{1,0:T(8,128)(2,1)}, u32[]{:S(2)}, u32[]{:S(2)}) %collective-permute-start.10) | collective-permute-done | bytes 786464 | tf_op jit(solution)/shard_map/ppermute | solution.py:102
  559.8 17.8 %collective-permute-done.35 = bf16[384,512]{1,0:T(8,128)(2,1)S(1)} collective-permute-done((bf16[384,512]{1,0:T(8,128)(2,1)S(1)}, bf16[384,512]{1,0:T(8,128)(2,1)S(1)}, u32[]{:S(2)}, u32[]{:S(2)}) %collective-permute-start.35) | collective-permute-done | bytes 393248 | tf_op jit(solution)/shard_map/ppermute | solution.py:102
  577.6 13.8 collective-permute-done.36
  596.4 12.6 collective-permute-done.40
  617.1 21.2 %attend.3 = (bf16[384,1536]{1,0:T(8,128)(2,1)S(1)}, f32[4,8,384]{2,1,0:T(8,128)S(1)}) custom-call(s32[2]{0:T(128)S(1)} %pad_add_fusion.1.place_ref, bf16[384,1536]{1,0:T(8,128)(2,1)S(1)} %fusion.103.q_ref, bf16[1536,512]{1,0:T(8,128)(2,1)S(1)} %bitcast.455, bf16[1536,512]{1,0:T(8,128)(2,1)S(1)} %bitcast.453), custom_call_target="tpu_custom_call" | custom-call | flops 12419999744 | bytes 1000 | tf_op jit(solution)/shard_map/attend/pallas_call | solution.py:390
  688.2 12.0 experts.12
  706.2 11.9 experts_back.8
  736.4 12.0 experts.13
  755.1 13.1 experts_back.9
  773.6 12.2 experts.14
  788.5 11.7 experts_back.10
  811.0 12.4 experts.15
  824.5 11.7 experts_back.11
  852.2 18.0 %expert_grads.4 = bf16[1,1536,1024]{2,1,0:T(8,128)(2,1)} custom-call(bf16[2,2,240,1536]{3,2,1,0:T(8,128)(2,1)S(1)} %copy-done.26, bf16[2,2,240,1536]{3,2,1,0:T(8,128)(2,1)S(1)} %copy-done.27, bf16[2,2,240,1536]{3,2,1,0:T(8,128)(2,1)} %get-tuple-element.497.refs_2_, bf16[2,2,240,1536]{3,2,1,0:T(8,128)(2,1)} %get-tuple-element.498.refs_3_, ...), custom_call_target="tpu_custom_call" | custom-call | flops 6209999872 | bytes 1000 | tf_op jit(solution)/shard_map/expert_grads/pallas_call | solution.py:771
  877.3 10.2 collective-permute-done.70
  930.3 34.3 %attend_back.2 = (bf16[384,1536]{1,0:T(8,128)(2,1)S(1)}, bf16[1536,512]{1,0:T(8,128)(2,1)S(1)}, bf16[1536,512]{1,0:T(8,128)(2,1)S(1)}) custom-call(s32[2]{0:T(128)S(1)} %pad_add_fusion.1.place_ref, bf16[384,1536]{1,0:T(8,128)(2,1)S(1)} %copy-done.17, bf16[1536,512]{1,0:T(8,128)(2,1)S(1)} %bitcast.456, bf16[1536,512]{1,0:T(8,128)(2,1)} %bitcast.454, ...), custom_call_target="tpu_custom_call" | custom-call | flops 18630000640 | bytes 1000 | tf_op jit(solution)/shard_map/attend_back/pallas_call | solution.py:486
  975.1 18.9 %collective-permute-start.80 = (bf16[2,384,512]{2,1,0:T(8,128)(2,1)}, bf16[2,384,512]{2,1,0:T(8,128)(2,1)S(1)}, u32[]{:S(2)}, u32[]{:S(2)}) collective-permute-start(bf16[2,384,512]{2,1,0:T(8,128)(2,1)} %dynamic-slice_bitcast_fusion.14), channel_id=1, source_target_pairs={{0,16},{16,0},{1,17},{17,1},{2,18},{18,2},{3,19},{19,3},{4,20},{20... | collective-permute-start | bytes 2359304 | tf_op jit(solution)/shard_map/ppermute | solution.py:134
  996.9 28.5 %expert_grads.5 = bf16[2,1536,1024]{2,1,0:T(8,128)(2,1)} custom-call(bf16[2,2,240,1536]{3,2,1,0:T(8,128)(2,1)} %copy-done.61, bf16[2,2,240,1536]{3,2,1,0:T(8,128)(2,1)} %copy-done.62, bf16[2,2,240,1536]{3,2,1,0:T(8,128)(2,1)} %copy-done.63, bf16[2,2,240,1536]{3,2,1,0:T(8,128)(2,1)} %copy-done.64, bf16[2,2,240,1024]{3,2,1,0:T(8,128)(2,1)S(1)} %copy-done.42, ...), custom_call_target="tpu_custom_call" | custom-call | flops 12419999744 | bytes 1000 | tf_op jit(solution)/shard_map/expert_grads/pallas_call | solution.py:771
  1070.0 12.1 experts_back.12
  1083.4 23.7 %collective-permute-done.84 = bf16[384,1024]{1,0:T(8,128)(2,1)S(1)} collective-permute-done((bf16[384,1024]{1,0:T(8,128)(2,1)S(1)}, bf16[384,1024]{1,0:T(8,128)(2,1)S(1)}, u32[]{:S(2)}, u32[]{:S(2)}) %collective-permute-start.84) | collective-permute-done | bytes 786464 | tf_op jit(solution)/shard_map/ppermute | solution.py:134
  1112.5 13.0 experts_back.13
  1131.9 28.6 %collective-permute-done.89 = bf16[768,1024]{1,0:T(8,128)(2,1)} collective-permute-done((bf16[768,1024]{1,0:T(8,128)(2,1)}, bf16[768,1024]{1,0:T(8,128)(2,1)}, u32[]{:S(2)}, u32[]{:S(2)}) %collective-permute-start.89) | collective-permute-done | bytes 1572896 | tf_op jit(solution)/shard_map/ppermute | solution.py:134
  1160.5 12.6 experts_back.14
  1173.1 12.5 collective-permute-done.92
  1194.1 11.8 experts_back.15
  1224.8 28.0 %expert_grads.6 = bf16[2,1536,1024]{2,1,0:T(8,128)(2,1)} custom-call(bf16[2,2,240,1536]{3,2,1,0:T(8,128)(2,1)} %copy-done.57, bf16[2,2,240,1536]{3,2,1,0:T(8,128)(2,1)} %copy-done.58, bf16[2,2,240,1536]{3,2,1,0:T(8,128)(2,1)} %copy-done.59, bf16[2,2,240,1536]{3,2,1,0:T(8,128)(2,1)} %copy-done.60, bf16[2,2,240,1024]{3,2,1,0:T(8,128)(2,1)S(1)} %copy-done.50, ...), custom_call_target="tpu_custom_call" | custom-call | flops 12419999744 | bytes 1000 | tf_op jit(solution)/shard_map/expert_grads/pallas_call | solution.py:771
  1301.4 34.2 %attend_back.3 = (bf16[384,1536]{1,0:T(8,128)(2,1)S(1)}, bf16[1536,512]{1,0:T(8,128)(2,1)S(1)}, bf16[1536,512]{1,0:T(8,128)(2,1)S(1)}) custom-call(s32[2]{0:T(128)S(1)} %pad_add_fusion.1.place_ref, bf16[384,1536]{1,0:T(8,128)(2,1)S(1)} %copy-done.15, bf16[1536,512]{1,0:T(8,128)(2,1)S(1)} %bitcast.452, bf16[1536,512]{1,0:T(8,128)(2,1)} %bitcast.450, ...), custom_call_target="tpu_custom_call" | custom-call | flops 18630000640 | bytes 1000 | tf_op jit(solution)/shard_map/attend_back/pallas_call | solution.py:486
  1339.3 21.8 %collective-permute-start.112 = (bf16[2,384,512]{2,1,0:T(8,128)(2,1)}, bf16[2,384,512]{2,1,0:T(8,128)(2,1)S(1)}, u32[]{:S(2)}, u32[]{:S(2)}) collective-permute-start(bf16[2,384,512]{2,1,0:T(8,128)(2,1)} %dynamic-slice_bitcast_fusion.9), channel_id=1, source_target_pairs={{0,16},{16,0},{1,17},{17,1},{2,18},{18,2},{3,19},{19,3},{4,20},{20... | collective-permute-start | bytes 2359304 | tf_op jit(solution)/shard_map/ppermute | solution.py:134
  1370.3 10.2 collective-permute-start.115
  1380.5 16.6 %collective-permute-done.112 = bf16[2,384,512]{2,1,0:T(8,128)(2,1)S(1)} collective-permute-done((bf16[2,384,512]{2,1,0:T(8,128)(2,1)}, bf16[2,384,512]{2,1,0:T(8,128)(2,1)S(1)}, u32[]{:S(2)}, u32[]{:S(2)}) %collective-permute-start.112) | collective-permute-done | bytes 786464 | tf_op jit(solution)/shard_map/ppermute | solution.py:134
  1398.2 18.4 %expert_grads.7 = bf16[1,1536,1024]{2,1,0:T(8,128)(2,1)} custom-call(bf16[2,2,240,1536]{3,2,1,0:T(8,128)(2,1)S(1)} %copy-done.24, bf16[2,2,240,1536]{3,2,1,0:T(8,128)(2,1)S(1)} %copy-done.25, bf16[2,2,240,1536]{3,2,1,0:T(8,128)(2,1)} %get-tuple-element.652.refs_2_, bf16[2,2,240,1536]{3,2,1,0:T(8,128)(2,1)} %get-tuple-element.653.refs_3_, ...), custom_call_target="tpu_custom_call" | custom-call | flops 6209999872 | bytes 1000 | tf_op jit(solution)/shard_map/expert_grads/pallas_call | solution.py:771
  1461.6 11.2 collective-permute-done.117
  1485.4 40.4 %collective-permute-done.116 = bf16[384,1024]{1,0:T(8,128)(2,1)S(1)} collective-permute-done((bf16[384,1024]{1,0:T(8,128)(2,1)S(1)}, bf16[384,1024]{1,0:T(8,128)(2,1)S(1)}, u32[]{:S(2)}, u32[]{:S(2)}) %collective-permute-start.116) | collective-permute-done | bytes 786464 | tf_op jit(solution)/shard_map/ppermute | solution.py:134
  1526.5 16.5 %collective-permute-done.118 = bf16[384,1024]{1,0:T(8,128)(2,1)S(1)} collective-permute-done((bf16[384,1024]{1,0:T(8,128)(2,1)S(1)}, bf16[384,1024]{1,0:T(8,128)(2,1)S(1)}, u32[]{:S(2)}, u32[]{:S(2)}) %collective-permute-start.118) | collective-permute-done | bytes 786464 | tf_op jit(solution)/shard_map/ppermute | solution.py:134
  1547.7 47.7 %collective-permute-done.121 = bf16[384,1024]{1,0:T(8,128)(2,1)S(1)} collective-permute-done((bf16[384,1024]{1,0:T(8,128)(2,1)S(1)}, bf16[384,1024]{1,0:T(8,128)(2,1)S(1)}, u32[]{:S(2)}, u32[]{:S(2)}) %collective-permute-start.121) | collective-permute-done | bytes 786464 | tf_op jit(solution)/shard_map/ppermute | solution.py:134
  (1069 shorter events, 642.3 us)
Async XLA Ops:
  7.2 84.1 %all-gather.6.cloned.1.call-start = ((), (), s32[]{:S(2)}) async-start(), calls=%async_computation.4 | async-start | bytes 8515584 | tf_op jit(solution)/shard_map/all_gather | solution.py:908
  11.6 111.2 %all-gather.8.cloned.1.call-start = ((), (), s32[]{:S(2)}) async-start(), calls=%async_computation.5 | async-start | bytes 1327104 | tf_op jit(solution)/shard_map/all_gather | solution.py:1003
  91.3 155.9 %all-gather.10.cloned.1.call-start = ((), (), s32[]{:S(2)}) async-start(), calls=%async_computation.6 | async-start | bytes 5898240 | tf_op jit(solution)/shard_map/all_gather | solution.py:1004
  122.9 422.3 %all-gather.12.cloned.1.call-start = ((), (), s32[]{:S(2)}) async-start(), calls=%async_computation.7 | async-start | bytes 8515584 | tf_op jit(solution)/shard_map/all_gather | solution.py:908
  131.1 71.7 %collective-permute-start.2 = (bf16[384,1024]{1,0:T(8,128)(2,1)S(1)}, bf16[384,1024]{1,0:T(8,128)(2,1)S(1)}, u32[]{:S(2)}, u32[]{:S(2)}) collective-permute-start(bf16[384,1024]{1,0:T(8,128)(2,1)S(1)} %copy-done.161), channel_id=1, source_target_pairs={{0,4},{4,0},{1,5},{5,1},{2,6},{6,2},{3,7},{7,3},{8,12},{12,8},{9,1... | collective-permute-start | bytes 2359304 | tf_op jit(solution)/shard_map/ppermute | solution.py:102
  138.4 90.8 %collective-permute-start.1 = (bf16[384,1024]{1,0:T(8,128)(2,1)S(1)}, bf16[384,1024]{1,0:T(8,128)(2,1)S(1)}, u32[]{:S(2)}, u32[]{:S(2)}) collective-permute-start(bf16[384,1024]{1,0:T(8,128)(2,1)S(1)} %copy-done.159), channel_id=1, source_target_pairs={{0,4},{4,0},{1,5},{5,1},{2,6},{6,2},{3,7},{7,3},{8,12},{12,8},{9,1... | collective-permute-start | bytes 2359304 | tf_op jit(solution)/shard_map/ppermute | solution.py:102
  139.5 116.9 %collective-permute-start = (bf16[384,1024]{1,0:T(8,128)(2,1)}, bf16[384,1024]{1,0:T(8,128)(2,1)}, u32[]{:S(2)}, u32[]{:S(2)}) collective-permute-start(bf16[384,1024]{1,0:T(8,128)(2,1)} %get-tuple-element.339), channel_id=1, source_target_pairs={{0,4},{4,0},{1,5},{5,1},{2,6},{6,2},{3,7},{7,3},{8,12},{12,8},{9,1... | collective-permute-start | bytes 2359304 | tf_op jit(solution)/shard_map/ppermute | solution.py:102
  151.3 51.5 %collective-permute-start.6 = (bf16[2,384,512]{2,1,0:T(8,128)(2,1)}, bf16[2,384,512]{2,1,0:T(8,128)(2,1)}, u32[]{:S(2)}, u32[]{:S(2)}) collective-permute-start(bf16[2,384,512]{2,1,0:T(8,128)(2,1)} %pad_maximum_fusion.22), channel_id=1, source_target_pairs={{0,8},{8,0},{1,9},{9,1},{2,10},{10,2},{3,11},{11,3},{4,12},{12,4},... | collective-permute-start | bytes 2359304 | tf_op jit(solution)/shard_map/ppermute | solution.py:102
  152.8 50.0 %collective-permute-start.5 = (bf16[2,384,512]{2,1,0:T(8,128)(2,1)}, bf16[2,384,512]{2,1,0:T(8,128)(2,1)}, u32[]{:S(2)}, u32[]{:S(2)}) collective-permute-start(bf16[2,384,512]{2,1,0:T(8,128)(2,1)} %pad_maximum_fusion.21), channel_id=1, source_target_pairs={{0,16},{16,0},{1,17},{17,1},{2,18},{18,2},{3,19},{19,3},{4,20},{20... | collective-permute-start | bytes 2359304 | tf_op jit(solution)/shard_map/ppermute | solution.py:102
  270.5 380.1 %all-gather.14.cloned.1.call-start = ((), (), s32[]{:S(2)}) async-start(), calls=%async_computation.8 | async-start | bytes 4866048 | tf_op jit(solution)/shard_map/all_gather | solution.py:908
  300.0 70.1 %collective-permute-start.17 = (bf16[768,1024]{1,0:T(8,128)(2,1)S(1)}, bf16[768,1024]{1,0:T(8,128)(2,1)S(1)}, u32[]{:S(2)}, u32[]{:S(2)}) collective-permute-start(bf16[768,1024]{1,0:T(8,128)(2,1)S(1)} %bitcast.494), channel_id=1, source_target_pairs={{0,16},{16,0},{1,17},{17,1},{2,18},{18,2},{3,19},{19,3},{4,20},{20... | collective-permute-start | bytes 4718600 | tf_op jit(solution)/shard_map/ppermute | solution.py:102
  301.7 70.9 %collective-permute-start.14 = (bf16[384,1664]{1,0:T(8,128)(2,1)S(1)}, bf16[384,1664]{1,0:T(8,128)(2,1)S(1)}, u32[]{:S(2)}, u32[]{:S(2)}) collective-permute-start(bf16[384,1664]{1,0:T(8,128)(2,1)S(1)} %concatenate.160.own_ref), channel_id=1, source_target_pairs={{0,1},{1,0},{2,3},{3,2},{4,5},{5,4},{6,7},{7,6},{8,9},{9,8},{10,11... | collective-permute-start | bytes 3833864 | tf_op jit(solution)/shard_map/ppermute | solution.py:69
  301.7 85.5 %collective-permute-start.12 = (bf16[384,1664]{1,0:T(8,128)(2,1)S(1)}, bf16[384,1664]{1,0:T(8,128)(2,1)S(1)}, u32[]{:S(2)}, u32[]{:S(2)}) collective-permute-start(bf16[384,1664]{1,0:T(8,128)(2,1)S(1)} %concatenate.160.own_ref), channel_id=1, source_target_pairs={{0,8},{8,0},{1,9},{9,1},{2,10},{10,2},{3,11},{11,3},{4,12},{12,4},... | collective-permute-start | bytes 3833864 | tf_op jit(solution)/shard_map/ppermute | solution.py:69
  303.5 83.7 %collective-permute-start.13 = (bf16[384,1664]{1,0:T(8,128)(2,1)S(1)}, bf16[384,1664]{1,0:T(8,128)(2,1)S(1)}, u32[]{:S(2)}, u32[]{:S(2)}) collective-permute-start(bf16[384,1664]{1,0:T(8,128)(2,1)S(1)} %concatenate.160.own_ref), channel_id=1, source_target_pairs={{0,2},{2,0},{1,3},{3,1},{4,6},{6,4},{5,7},{7,5},{8,10},{10,8},{9,1... | collective-permute-start | bytes 3833864 | tf_op jit(solution)/shard_map/ppermute | solution.py:69
  387.8 56.1 %collective-permute-start.23 = (bf16[384,1536]{1,0:T(8,128)(2,1)S(1)}, bf16[384,1536]{1,0:T(8,128)(2,1)}, u32[]{:S(2)}, u32[]{:S(2)}) collective-permute-start(bf16[384,1536]{1,0:T(8,128)(2,1)S(1)} %get-tuple-element.383), channel_id=1, source_target_pairs={{0,1},{1,0},{2,3},{3,2},{4,5},{5,4},{6,7},{7,6},{8,9},{9,8},{10,11... | collective-permute-start | bytes 3538952 | tf_op jit(solution)/shard_map/ppermute | solution.py:69
  473.4 58.3 %collective-permute-start.10 = (bf16[384,1024]{1,0:T(8,128)(2,1)S(1)}, bf16[384,1024]{1,0:T(8,128)(2,1)}, u32[]{:S(2)}, u32[]{:S(2)}) collective-permute-start(bf16[384,1024]{1,0:T(8,128)(2,1)S(1)} %copy-done.155), channel_id=1, source_target_pairs={{0,4},{4,0},{1,5},{5,1},{2,6},{6,2},{3,7},{7,3},{8,12},{12,8},{9,1... | collective-permute-start | bytes 2359304 | tf_op jit(solution)/shard_map/ppermute | solution.py:102
  475.4 120.9 %collective-permute-start.37 = (bf16[384,1024]{1,0:T(8,128)(2,1)}, bf16[384,1024]{1,0:T(8,128)(2,1)}, u32[]{:S(2)}, u32[]{:S(2)}) collective-permute-start(bf16[384,1024]{1,0:T(8,128)(2,1)} %get-tuple-element.411), channel_id=1, source_target_pairs={{0,4},{4,0},{1,5},{5,1},{2,6},{6,2},{3,7},{7,3},{8,12},{12,8},{9,1... | collective-permute-start | bytes 2359304 | tf_op jit(solution)/shard_map/ppermute | solution.py:102
  476.4 564.7 %reduce-scatter.5.cloned.1.call-start = ((), (), s32[]{:S(2)}) async-start(), calls=%async_computation.9 | async-start | bytes 4866048 | tf_op jit(solution)/shard_map/reduce_scatter | solution.py:830
  478.2 53.5 %collective-permute-start.24 = (bf16[384,1024]{1,0:T(8,128)(2,1)S(1)}, bf16[384,1024]{1,0:T(8,128)(2,1)S(1)}, u32[]{:S(2)}, u32[]{:S(2)}) collective-permute-start(bf16[384,1024]{1,0:T(8,128)(2,1)S(1)} %broadcast_select_fusion.5), channel_id=1, source_target_pairs={{0,8},{8,0},{1,9},{9,1},{2,10},{10,2},{3,11},{11,3},{4,12},{12,4},... | collective-permute-start | bytes 2359304 | tf_op jit(solution)/shard_map/ppermute | solution.py:69
  539.3 57.0 %collective-permute-start.38 = (bf16[768,1024]{1,0:T(8,128)(2,1)}, bf16[768,1024]{1,0:T(8,128)(2,1)}, u32[]{:S(2)}, u32[]{:S(2)}) collective-permute-start(bf16[768,1024]{1,0:T(8,128)(2,1)} %bitcast.61), channel_id=1, source_target_pairs={{0,16},{16,0},{1,17},{17,1},{2,18},{18,2},{3,19},{19,3},{4,20},{20... | collective-permute-start | bytes 4718600 | tf_op jit(solution)/shard_map/ppermute | solution.py:102
  542.9 67.5 %collective-permute-start.34 = (bf16[384,1024]{1,0:T(8,128)(2,1)}, bf16[384,1024]{1,0:T(8,128)(2,1)}, u32[]{:S(2)}, u32[]{:S(2)}) collective-permute-start(bf16[384,1024]{1,0:T(8,128)(2,1)} %broadcast_select_fusion.4), channel_id=1, source_target_pairs={{0,8},{8,0},{1,9},{9,1},{2,10},{10,2},{3,11},{11,3},{4,12},{12,4},... | collective-permute-start | bytes 2359304 | tf_op jit(solution)/shard_map/ppermute | solution.py:69
  677.7 48.3 %collective-permute-start.41 = (bf16[384,1536]{1,0:T(8,128)(2,1)S(1)}, bf16[384,1536]{1,0:T(8,128)(2,1)S(1)}, u32[]{:S(2)}, u32[]{:S(2)}) collective-permute-start(bf16[384,1536]{1,0:T(8,128)(2,1)S(1)} %bitcast.466), channel_id=1, source_target_pairs={{0,8},{8,0},{1,9},{9,1},{2,10},{10,2},{3,11},{11,3},{4,12},{12,4},... | collective-permute-start | bytes 3538952 | tf_op jit(solution)/shard_map/ppermute | solution.py:69
  681.3 47.2 %collective-permute-start.42 = (bf16[384,1536]{1,0:T(8,128)(2,1)S(1)}, bf16[384,1536]{1,0:T(8,128)(2,1)S(1)}, u32[]{:S(2)}, u32[]{:S(2)}) collective-permute-start(bf16[384,1536]{1,0:T(8,128)(2,1)S(1)} %bitcast.467), channel_id=1, source_target_pairs={{0,2},{2,0},{1,3},{3,1},{4,6},{6,4},{5,7},{7,5},{8,10},{10,8},{9,1... | collective-permute-start | bytes 3538952 | tf_op jit(solution)/shard_map/ppermute | solution.py:69
  729.8 43.5 %collective-permute-start.56 = (bf16[192,1664]{1,0:T(8,128)(2,1)}, bf16[192,1664]{1,0:T(8,128)(2,1)S(1)}, u32[]{:S(2)}, u32[]{:S(2)}) collective-permute-start(bf16[192,1664]{1,0:T(8,128)(2,1)} %slice.493), channel_id=1, source_target_pairs={{0,8},{8,0},{1,9},{9,1},{2,10},{10,2},{3,11},{11,3},{4,12},{12,4},... | collective-permute-start | bytes 1916936 | tf_op jit(solution)/shard_map/ppermute | solution.py:69
  732.3 70.2 %collective-permute-start.59 = (bf16[384,1664]{1,0:T(8,128)(2,1)S(1)}, bf16[384,1664]{1,0:T(8,128)(2,1)}, u32[]{:S(2)}, u32[]{:S(2)}) collective-permute-start(bf16[384,1664]{1,0:T(8,128)(2,1)S(1)} %get-tuple-element.476), channel_id=1, source_target_pairs={{0,1},{1,0},{2,3},{3,2},{4,5},{5,4},{6,7},{7,6},{8,9},{9,8},{10,11... | collective-permute-start | bytes 3833864 | tf_op jit(solution)/shard_map/ppermute | solution.py:69
  877.3 87.4 %collective-permute-start.68 = (bf16[768,1024]{1,0:T(8,128)(2,1)}, bf16[768,1024]{1,0:T(8,128)(2,1)}, u32[]{:S(2)}, u32[]{:S(2)}) collective-permute-start(bf16[768,1024]{1,0:T(8,128)(2,1)} %dynamic-slice_bitcast_fusion.5), channel_id=1, source_target_pairs={{0,16},{16,0},{1,17},{17,1},{2,18},{18,2},{3,19},{19,3},{4,20},{20... | collective-permute-start | bytes 4718600 | tf_op jit(solution)/shard_map/ppermute | solution.py:134
  890.5 77.5 %collective-permute-start.71 = (bf16[384,1536]{1,0:T(8,128)(2,1)}, bf16[384,1536]{1,0:T(8,128)(2,1)}, u32[]{:S(2)}, u32[]{:S(2)}) collective-permute-start(bf16[384,1536]{1,0:T(8,128)(2,1)} %get-tuple-element.534), channel_id=1, source_target_pairs={{0,1},{1,0},{2,3},{3,2},{4,5},{5,4},{6,7},{7,6},{8,9},{9,8},{10,11... | collective-permute-start | bytes 3538952 | tf_op jit(solution)/shard_map/ppermute | solution.py:69
  906.2 350.3 %reduce-scatter.7.cloned.1.call-start = ((), (), s32[]{:S(2)}) async-start(), calls=%async_computation.10 | async-start | bytes 8110080 | tf_op jit(solution)/shard_map/reduce_scatter | solution.py:830
  968.0 73.0 %collective-permute-start.79 = (bf16[1,384,1024]{2,1,0:T(8,128)(2,1)}, bf16[1,384,1024]{2,1,0:T(8,128)(2,1)}, u32[]{:S(2)}, u32[]{:S(2)}) collective-permute-start(bf16[1,384,1024]{2,1,0:T(8,128)(2,1)} %dynamic-slice_bitcast_fusion.15), channel_id=1, source_target_pairs={{0,8},{8,0},{1,9},{9,1},{2,10},{10,2},{3,11},{11,3},{4,12},{12,4},... | collective-permute-start | bytes 2359304 | tf_op jit(solution)/shard_map/ppermute | solution.py:69
  973.2 56.2 %collective-permute-start.82 = (bf16[2,384,512]{2,1,0:T(8,128)(2,1)}, bf16[2,384,512]{2,1,0:T(8,128)(2,1)S(1)}, u32[]{:S(2)}, u32[]{:S(2)}) collective-permute-start(bf16[2,384,512]{2,1,0:T(8,128)(2,1)} %dynamic-slice_bitcast_fusion.13), channel_id=1, source_target_pairs={{0,8},{8,0},{1,9},{9,1},{2,10},{10,2},{3,11},{11,3},{4,12},{12,4},... | collective-permute-start | bytes 2359304 | tf_op jit(solution)/shard_map/ppermute | solution.py:134
  975.1 56.7 %collective-permute-start.80 = (bf16[2,384,512]{2,1,0:T(8,128)(2,1)}, bf16[2,384,512]{2,1,0:T(8,128)(2,1)S(1)}, u32[]{:S(2)}, u32[]{:S(2)}) collective-permute-start(bf16[2,384,512]{2,1,0:T(8,128)(2,1)} %dynamic-slice_bitcast_fusion.14), channel_id=1, source_target_pairs={{0,16},{16,0},{1,17},{17,1},{2,18},{18,2},{3,19},{19,3},{4,20},{20... | collective-permute-start | bytes 2359304 | tf_op jit(solution)/shard_map/ppermute | solution.py:134
  1063.7 44.3 %collective-permute-start.85 = (bf16[768,1024]{1,0:T(8,128)(2,1)}, bf16[768,1024]{1,0:T(8,128)(2,1)}, u32[]{:S(2)}, u32[]{:S(2)}) collective-permute-start(bf16[768,1024]{1,0:T(8,128)(2,1)} %dynamic-slice_bitcast_fusion.4), channel_id=1, source_target_pairs={{0,16},{16,0},{1,17},{17,1},{2,18},{18,2},{3,19},{19,3},{4,20},{20... | collective-permute-start | bytes 4718600 | tf_op jit(solution)/shard_map/ppermute | solution.py:134
  1066.2 351.9 %reduce-scatter.9.cloned.1.call-start = ((), (), s32[]{:S(2)}) async-start(), calls=%async_computation.11 | async-start | bytes 4866048 | tf_op jit(solution)/shard_map/reduce_scatter | solution.py:830
  1109.8 50.7 %collective-permute-start.89 = (bf16[768,1024]{1,0:T(8,128)(2,1)}, bf16[768,1024]{1,0:T(8,128)(2,1)}, u32[]{:S(2)}, u32[]{:S(2)}) collective-permute-start(bf16[768,1024]{1,0:T(8,128)(2,1)} %dynamic-slice_bitcast_fusion.3), channel_id=1, source_target_pairs={{0,16},{16,0},{1,17},{17,1},{2,18},{18,2},{3,19},{19,3},{4,20},{20... | collective-permute-start | bytes 4718600 | tf_op jit(solution)/shard_map/ppermute | solution.py:134
  1111.5 74.1 %collective-permute-start.96 = (bf16[384,1664]{1,0:T(8,128)(2,1)S(1)}, bf16[384,1664]{1,0:T(8,128)(2,1)S(1)}, u32[]{:S(2)}, u32[]{:S(2)}) collective-permute-start(bf16[384,1664]{1,0:T(8,128)(2,1)S(1)} %get-tuple-element.590), channel_id=1, source_target_pairs={{0,1},{1,0},{2,3},{3,2},{4,5},{5,4},{6,7},{7,6},{8,9},{9,8},{10,11... | collective-permute-start | bytes 3833864 | tf_op jit(solution)/shard_map/ppermute | solution.py:69
  1125.5 60.1 %collective-permute-start.95 = (bf16[384,1664]{1,0:T(8,128)(2,1)S(1)}, bf16[384,1664]{1,0:T(8,128)(2,1)}, u32[]{:S(2)}, u32[]{:S(2)}) collective-permute-start(bf16[384,1664]{1,0:T(8,128)(2,1)S(1)} %get-tuple-element.589), channel_id=1, source_target_pairs={{0,1},{1,0},{2,3},{3,2},{4,5},{5,4},{6,7},{7,6},{8,9},{9,8},{10,11... | collective-permute-start | bytes 3833864 | tf_op jit(solution)/shard_map/ppermute | solution.py:69
  1128.1 57.6 %collective-permute-start.90 = (bf16[1,384,1024]{2,1,0:T(8,128)(2,1)S(1)}, bf16[1,384,1024]{2,1,0:T(8,128)(2,1)}, u32[]{:S(2)}, u32[]{:S(2)}) collective-permute-start(bf16[1,384,1024]{2,1,0:T(8,128)(2,1)S(1)} %dynamic-slice_bitcast_fusion.12), channel_id=1, source_target_pairs={{0,8},{8,0},{1,9},{9,1},{2,10},{10,2},{3,11},{11,3},{4,12},{12,4},... | collective-permute-start | bytes 2359304 | tf_op jit(solution)/shard_map/ppermute | solution.py:69
  1215.7 51.4 %collective-permute-start.102 = (bf16[384,1024]{1,0:T(8,128)(2,1)}, bf16[384,1024]{1,0:T(8,128)(2,1)}, u32[]{:S(2)}, u32[]{:S(2)}) collective-permute-start(bf16[384,1024]{1,0:T(8,128)(2,1)} %fusion.124), channel_id=1, source_target_pairs={{0,4},{4,0},{1,5},{5,1},{2,6},{6,2},{3,7},{7,3},{8,12},{12,8},{9,1... | collective-permute-start | bytes 2359304 | tf_op jit(solution)/shard_map/ppermute | solution.py:134
  1220.4 46.8 %collective-permute-start.101 = (bf16[1,384,1024]{2,1,0:T(8,128)(2,1)}, bf16[1,384,1024]{2,1,0:T(8,128)(2,1)}, u32[]{:S(2)}, u32[]{:S(2)}) collective-permute-start(bf16[1,384,1024]{2,1,0:T(8,128)(2,1)} %dynamic-slice_bitcast_fusion.11), channel_id=1, source_target_pairs={{0,8},{8,0},{1,9},{9,1},{2,10},{10,2},{3,11},{11,3},{4,12},{12,4},... | collective-permute-start | bytes 2359304 | tf_op jit(solution)/shard_map/ppermute | solution.py:69
  1298.4 302.8 %reduce-scatter.11.cloned.1.call-start = ((), (), s32[]{:S(2)}) async-start(), calls=%async_computation.12 | async-start | bytes 8515584 | tf_op jit(solution)/shard_map/reduce_scatter | solution.py:830
  1301.3 116.2 %collective-permute-start.110 = (bf16[768,1024]{1,0:T(8,128)(2,1)}, bf16[768,1024]{1,0:T(8,128)(2,1)}, u32[]{:S(2)}, u32[]{:S(2)}) collective-permute-start(bf16[768,1024]{1,0:T(8,128)(2,1)} %dynamic-slice_bitcast_fusion.1), channel_id=1, source_target_pairs={{0,16},{16,0},{1,17},{17,1},{2,18},{18,2},{3,19},{19,3},{4,20},{20... | collective-permute-start | bytes 4718600 | tf_op jit(solution)/shard_map/ppermute | solution.py:134
  1339.3 57.9 %collective-permute-start.112 = (bf16[2,384,512]{2,1,0:T(8,128)(2,1)}, bf16[2,384,512]{2,1,0:T(8,128)(2,1)S(1)}, u32[]{:S(2)}, u32[]{:S(2)}) collective-permute-start(bf16[2,384,512]{2,1,0:T(8,128)(2,1)} %dynamic-slice_bitcast_fusion.9), channel_id=1, source_target_pairs={{0,16},{16,0},{1,17},{17,1},{2,18},{18,2},{3,19},{19,3},{4,20},{20... | collective-permute-start | bytes 2359304 | tf_op jit(solution)/shard_map/ppermute | solution.py:134
  1365.2 52.4 %collective-permute-start.111 = (bf16[1,384,1024]{2,1,0:T(8,128)(2,1)}, bf16[1,384,1024]{2,1,0:T(8,128)(2,1)}, u32[]{:S(2)}, u32[]{:S(2)}) collective-permute-start(bf16[1,384,1024]{2,1,0:T(8,128)(2,1)} %dynamic-slice_bitcast_fusion.10), channel_id=1, source_target_pairs={{0,8},{8,0},{1,9},{9,1},{2,10},{10,2},{3,11},{11,3},{4,12},{12,4},... | collective-permute-start | bytes 2359304 | tf_op jit(solution)/shard_map/ppermute | solution.py:69
  1370.3 46.3 %collective-permute-start.115 = (bf16[384,512]{1,0:T(8,128)(2,1)S(1)}, bf16[384,512]{1,0:T(8,128)(2,1)S(1)}, u32[]{:S(2)}, u32[]{:S(2)}) collective-permute-start(bf16[384,512]{1,0:T(8,128)(2,1)S(1)} %dynamic-slice_bitcast_fusion.16), channel_id=1, source_target_pairs={{0,16},{16,0},{1,17},{17,1},{2,18},{18,2},{3,19},{19,3},{4,20},{20... | collective-permute-start | bytes 1179656 | tf_op jit(solution)/shard_map/ppermute | solution.py:134
  1452.0 73.9 %collective-permute-start.116 = (bf16[384,1024]{1,0:T(8,128)(2,1)S(1)}, bf16[384,1024]{1,0:T(8,128)(2,1)S(1)}, u32[]{:S(2)}, u32[]{:S(2)}) collective-permute-start(bf16[384,1024]{1,0:T(8,128)(2,1)S(1)} %fusion.116), channel_id=1, source_target_pairs={{0,4},{4,0},{1,5},{5,1},{2,6},{6,2},{3,7},{7,3},{8,12},{12,8},{9,1... | collective-permute-start | bytes 2359304 | tf_op jit(solution)/shard_map/ppermute | solution.py:134
  1473.2 69.9 %collective-permute-start.118 = (bf16[384,1024]{1,0:T(8,128)(2,1)S(1)}, bf16[384,1024]{1,0:T(8,128)(2,1)S(1)}, u32[]{:S(2)}, u32[]{:S(2)}) collective-permute-start(bf16[384,1024]{1,0:T(8,128)(2,1)S(1)} %fusion.112), channel_id=1, source_target_pairs={{0,4},{4,0},{1,5},{5,1},{2,6},{6,2},{3,7},{7,3},{8,12},{12,8},{9,1... | collective-permute-start | bytes 2359304 | tf_op jit(solution)/shard_map/ppermute | solution.py:134
  1484.0 59.6 %collective-permute-start.120 = (bf16[1,384,1024]{2,1,0:T(8,128)(2,1)S(1)}, bf16[1,384,1024]{2,1,0:T(8,128)(2,1)S(1)}, u32[]{:S(2)}, u32[]{:S(2)}) collective-permute-start(bf16[1,384,1024]{2,1,0:T(8,128)(2,1)S(1)} %dynamic-slice_bitcast_fusion.6), channel_id=1, source_target_pairs={{0,8},{8,0},{1,9},{9,1},{2,10},{10,2},{3,11},{11,3},{4,12},{12,4},... | collective-permute-start | bytes 2359304 | tf_op jit(solution)/shard_map/ppermute | solution.py:69
  1544.1 51.4 %collective-permute-start.121 = (bf16[384,1024]{1,0:T(8,128)(2,1)S(1)}, bf16[384,1024]{1,0:T(8,128)(2,1)S(1)}, u32[]{:S(2)}, u32[]{:S(2)}) collective-permute-start(bf16[384,1024]{1,0:T(8,128)(2,1)S(1)} %fusion.108), channel_id=1, source_target_pairs={{0,4},{4,0},{1,5},{5,1},{2,6},{6,2},{3,7},{7,3},{8,12},{12,8},{9,1... | collective-permute-start | bytes 2359304 | tf_op jit(solution)/shard_map/ppermute | solution.py:134
  (334 other events, 4618.0 us)
Sparse Core Ops, SparseCore 0:
  11.8 79.5 all-gather.5
  93.5 21.2 all-gather.7
  123.0 73.9 all-gather.9
  270.7 108.1 all-gather.11
  476.5 108.6 all-gather.13
  906.4 104.4 reduce-scatter.4
  1066.3 141.8 reduce-scatter.6
  1298.5 119.4 reduce-scatter.8
  1438.9 162.2 reduce-scatter.10

commit v3 on v2

--- a/solution.py
+++ b/solution.py
@@ -845,7 +845,7 @@
 DOWN1 = ("", "y0", "x0", "h0")
 IN1 = ("y0", "y1 x0", "x1 h0", "", "h1")
 DOWN0 = ()
-IN0 = ("", "y0", "y1 x0")
+IN0 = ("", "y0 y1", "x0")
 
 
 def local(

time: 1620 us -> 1630 us (level)
  waiting for transfers between devices: 623 us -> 664 us
  starting transfers between devices: 175 us -> 145 us
    ppermute x20, waiting for transfers between devices: 184 us -> 223 us  [scatter_start(): lax.ppermute(carried, axis, [(i, (i + 1) % size) for i in range(size)])]
    ppermute x20, starting transfers between devices: 67.9 us -> 38.4 us  [scatter_start(): lax.ppermute(carried, axis, [(i, (i + 1) % size) for i in range(size)])]
    unnamed x509 -> x521, local copies, waits for them, and re-layouts: 80.8 us -> 83.3 us
  transfers between devices with their start and end apart: 131 -> 131, of which waited for: 54 -> 55; matrix products, arithmetic and copies ran while one was open for 16% -> 16% of each run, Pallas kernels for 24% -> 24%
where the time goes in v3:
time: 1630 us; the launch traced here: 1620 us
  waiting for transfers between devices  664 us (41%)
  Pallas kernels  395 us (24%)
  local copies, waits for them, and re-layouts  165 us (10%)
  starting transfers between devices  145 us (9%)
  other arithmetic  139 us (9%)
  matrix products  91.8 us (6%)
  between operations  18.6 us (1%)
    ppermute x20, waiting for transfers between devices, ring_start(): lax.ppermute(values, axis, [(i, (i + 1) % size) for i in range(size)])  224 us
    ppermute x20, waiting for transfers between devices, scatter_start(): lax.ppermute(carried, axis, [(i, (i + 1) % size) for i in range(size)])  223 us
    ppermute x82, waiting for transfers between devices, swap(): return lax.ppermute(values, axis, [(0, 1), (1, 0)])  144 us
    pallas_call x8, Pallas kernels, experts_back(): pl.pallas_call(experts_back_kernel, in_specs=[pl.BlockSpec(memory_space=p...  97.7 us
    pallas_call x8, Pallas kernels, experts(): pl.pallas_call(experts_kernel, in_specs=[vmem] * 3 + [pl.BlockSpec(memory...  93.1 us
    pallas_call x4, Pallas kernels, expert_grads(): pl.pallas_call(grads_kernel, grid=(local, cols // step), in_specs=[pl.Blo...  92.9 us
    unnamed x521, local copies, waits for them, and re-layouts  83.3 us
    ppermute x82, starting transfers between devices, swap(): return lax.ppermute(values, axis, [(0, 1), (1, 0)])  74.1 us
  transfers between devices with their start and end apart: 131, of which 55 were waited for; matrix products, arithmetic and copies ran while one was open for 16% of the time, Pallas kernels for 24%

profile of v3, /device:TPU:0, one launch (start us, length us, event | category | flops | bytes accessed | tf_op | source)
XLA Modules:
  0.0 1618.0 jit_solution(12849597272222279756)
XLA Ops:
  24.6 66.7 %all-gather.6.cloned.1.call-done = bf16[1536,2688]{1,0:T(8,128)(2,1)} async-done(((bf16[48,2688]{1,0:T(8,128)(2,1)}), bf16[1536,2688]{1,0:T(8,128)(2,1)}) %all-gather.6.cloned.1.call-update) | async-done | bytes 8257552 | tf_op jit(solution)/shard_map/all_gather | solution.py:908
  156.1 46.6 %collective-permute-done.2 = bf16[384,1024]{1,0:T(8,128)(2,1)S(1)} collective-permute-done((bf16[384,1024]{1,0:T(8,128)(2,1)S(1)}, bf16[384,1024]{1,0:T(8,128)(2,1)S(1)}, u32[]{:S(2)}, u32[]{:S(2)}) %collective-permute-start.2) | collective-permute-done | bytes 786464 | tf_op jit(solution)/shard_map/ppermute | solution.py:102
  207.9 21.2 %attend.2 = (bf16[384,1536]{1,0:T(8,128)(2,1)S(1)}, f32[4,8,384]{2,1,0:T(8,128)S(1)}) custom-call(s32[2]{0:T(128)S(1)} %pad_add_fusion.1.place_ref, bf16[384,1536]{1,0:T(8,128)(2,1)S(1)} %fusion.104.q_ref, bf16[1536,512]{1,0:T(8,128)(2,1)S(1)} %bitcast.451, bf16[1536,512]{1,0:T(8,128)(2,1)S(1)} %bitcast.449), custom_call_target="tpu_custom_call" | custom-call | flops 12419999744 | bytes 1000 | tf_op jit(solution)/shard_map/attend/pallas_call | solution.py:390
  284.8 13.4 collective-permute-done.16
  307.5 18.4 %collective-permute-done.15 = bf16[768,1024]{1,0:T(8,128)(2,1)S(1)} collective-permute-done((bf16[768,1024]{1,0:T(8,128)(2,1)S(1)}, bf16[768,1024]{1,0:T(8,128)(2,1)S(1)}, u32[]{:S(2)}, u32[]{:S(2)}) %collective-permute-start.15) | collective-permute-done | bytes 1572896 | tf_op jit(solution)/shard_map/ppermute | solution.py:102
  328.3 41.7 %collective-permute-done.17 = bf16[768,1024]{1,0:T(8,128)(2,1)S(1)} collective-permute-done((bf16[768,1024]{1,0:T(8,128)(2,1)S(1)}, bf16[768,1024]{1,0:T(8,128)(2,1)S(1)}, u32[]{:S(2)}, u32[]{:S(2)}) %collective-permute-start.17) | collective-permute-done | bytes 1572896 | tf_op jit(solution)/shard_map/ppermute | solution.py:102
  372.5 11.2 experts.8
  393.8 11.2 experts.9
  411.2 11.0 experts.10
  422.3 21.5 %collective-permute-done.11 = bf16[384,1024]{1,0:T(8,128)(2,1)S(1)} collective-permute-done((bf16[384,1024]{1,0:T(8,128)(2,1)S(1)}, bf16[384,1024]{1,0:T(8,128)(2,1)S(1)}, u32[]{:S(2)}, u32[]{:S(2)}) %collective-permute-start.11) | collective-permute-done | bytes 786464 | tf_op jit(solution)/shard_map/ppermute | solution.py:102
  452.0 11.0 experts.11
  479.6 10.3 collective-permute-done.30
  490.0 13.2 collective-permute-done.31
  508.8 22.8 %collective-permute-done.10 = bf16[384,1024]{1,0:T(8,128)(2,1)} collective-permute-done((bf16[384,1024]{1,0:T(8,128)(2,1)S(1)}, bf16[384,1024]{1,0:T(8,128)(2,1)}, u32[]{:S(2)}, u32[]{:S(2)}) %collective-permute-start.10) | collective-permute-done | bytes 786464 | tf_op jit(solution)/shard_map/ppermute | solution.py:102
  559.6 17.8 %collective-permute-done.35 = bf16[384,512]{1,0:T(8,128)(2,1)S(1)} collective-permute-done((bf16[384,512]{1,0:T(8,128)(2,1)S(1)}, bf16[384,512]{1,0:T(8,128)(2,1)S(1)}, u32[]{:S(2)}, u32[]{:S(2)}) %collective-permute-start.35) | collective-permute-done | bytes 393248 | tf_op jit(solution)/shard_map/ppermute | solution.py:102
  577.4 13.8 collective-permute-done.36
  596.2 12.6 collective-permute-done.40
  616.9 21.2 %attend.3 = (bf16[384,1536]{1,0:T(8,128)(2,1)S(1)}, f32[4,8,384]{2,1,0:T(8,128)S(1)}) custom-call(s32[2]{0:T(128)S(1)} %pad_add_fusion.1.place_ref, bf16[384,1536]{1,0:T(8,128)(2,1)S(1)} %fusion.103.q_ref, bf16[1536,512]{1,0:T(8,128)(2,1)S(1)} %bitcast.455, bf16[1536,512]{1,0:T(8,128)(2,1)S(1)} %bitcast.453), custom_call_target="tpu_custom_call" | custom-call | flops 12419999744 | bytes 1000 | tf_op jit(solution)/shard_map/attend/pallas_call | solution.py:390
  688.0 12.0 experts.12
  706.0 11.9 experts_back.8
  736.2 12.0 experts.13
  755.0 13.1 experts_back.9
  773.6 12.3 experts.14
  788.4 11.7 experts_back.10
  810.9 12.4 experts.15
  824.4 11.7 experts_back.11
  852.0 18.0 %expert_grads.4 = bf16[1,1536,1024]{2,1,0:T(8,128)(2,1)} custom-call(bf16[2,2,240,1536]{3,2,1,0:T(8,128)(2,1)S(1)} %copy-done.26, bf16[2,2,240,1536]{3,2,1,0:T(8,128)(2,1)S(1)} %copy-done.27, bf16[2,2,240,1536]{3,2,1,0:T(8,128)(2,1)} %get-tuple-element.497.refs_2_, bf16[2,2,240,1536]{3,2,1,0:T(8,128)(2,1)} %get-tuple-element.498.refs_3_, ...), custom_call_target="tpu_custom_call" | custom-call | flops 6209999872 | bytes 1000 | tf_op jit(solution)/shard_map/expert_grads/pallas_call | solution.py:771
  877.2 10.3 collective-permute-done.70
  915.2 9.3 collective-permute-done.74
  930.3 34.3 %attend_back.2 = (bf16[384,1536]{1,0:T(8,128)(2,1)S(1)}, bf16[1536,512]{1,0:T(8,128)(2,1)S(1)}, bf16[1536,512]{1,0:T(8,128)(2,1)S(1)}) custom-call(s32[2]{0:T(128)S(1)} %pad_add_fusion.1.place_ref, bf16[384,1536]{1,0:T(8,128)(2,1)S(1)} %copy-done.17, bf16[1536,512]{1,0:T(8,128)(2,1)S(1)} %bitcast.456, bf16[1536,512]{1,0:T(8,128)(2,1)} %bitcast.454, ...), custom_call_target="tpu_custom_call" | custom-call | flops 18630000640 | bytes 1000 | tf_op jit(solution)/shard_map/attend_back/pallas_call | solution.py:486
  975.0 18.9 %collective-permute-start.80 = (bf16[2,384,512]{2,1,0:T(8,128)(2,1)}, bf16[2,384,512]{2,1,0:T(8,128)(2,1)S(1)}, u32[]{:S(2)}, u32[]{:S(2)}) collective-permute-start(bf16[2,384,512]{2,1,0:T(8,128)(2,1)} %dynamic-slice_bitcast_fusion.14), channel_id=1, source_target_pairs={{0,16},{16,0},{1,17},{17,1},{2,18},{18,2},{3,19},{19,3},{4,20},{20... | collective-permute-start | bytes 2359304 | tf_op jit(solution)/shard_map/ppermute | solution.py:134
  996.8 28.5 %expert_grads.5 = bf16[2,1536,1024]{2,1,0:T(8,128)(2,1)} custom-call(bf16[2,2,240,1536]{3,2,1,0:T(8,128)(2,1)} %copy-done.61, bf16[2,2,240,1536]{3,2,1,0:T(8,128)(2,1)} %copy-done.62, bf16[2,2,240,1536]{3,2,1,0:T(8,128)(2,1)} %copy-done.63, bf16[2,2,240,1536]{3,2,1,0:T(8,128)(2,1)} %copy-done.64, bf16[2,2,240,1024]{3,2,1,0:T(8,128)(2,1)S(1)} %copy-done.42, ...), custom_call_target="tpu_custom_call" | custom-call | flops 12419999744 | bytes 1000 | tf_op jit(solution)/shard_map/expert_grads/pallas_call | solution.py:771
  1069.8 12.1 experts_back.12
  1083.2 23.7 %collective-permute-done.84 = bf16[384,1024]{1,0:T(8,128)(2,1)S(1)} collective-permute-done((bf16[384,1024]{1,0:T(8,128)(2,1)S(1)}, bf16[384,1024]{1,0:T(8,128)(2,1)S(1)}, u32[]{:S(2)}, u32[]{:S(2)}) %collective-permute-start.84) | collective-permute-done | bytes 786464 | tf_op jit(solution)/shard_map/ppermute | solution.py:134
  1112.3 12.8 experts_back.13
  1131.5 28.7 %collective-permute-done.89 = bf16[768,1024]{1,0:T(8,128)(2,1)} collective-permute-done((bf16[768,1024]{1,0:T(8,128)(2,1)}, bf16[768,1024]{1,0:T(8,128)(2,1)}, u32[]{:S(2)}, u32[]{:S(2)}) %collective-permute-start.89) | collective-permute-done | bytes 1572896 | tf_op jit(solution)/shard_map/ppermute | solution.py:134
  1160.3 12.6 experts_back.14
  1172.8 12.2 collective-permute-done.92
  1193.7 11.8 experts_back.15
  1223.9 28.0 %expert_grads.6 = bf16[2,1536,1024]{2,1,0:T(8,128)(2,1)} custom-call(bf16[2,2,240,1536]{3,2,1,0:T(8,128)(2,1)} %copy-done.57, bf16[2,2,240,1536]{3,2,1,0:T(8,128)(2,1)} %copy-done.58, bf16[2,2,240,1536]{3,2,1,0:T(8,128)(2,1)} %copy-done.59, bf16[2,2,240,1536]{3,2,1,0:T(8,128)(2,1)} %copy-done.60, bf16[2,2,240,1024]{3,2,1,0:T(8,128)(2,1)S(1)} %copy-done.50, ...), custom_call_target="tpu_custom_call" | custom-call | flops 12419999744 | bytes 1000 | tf_op jit(solution)/shard_map/expert_grads/pallas_call | solution.py:771
  1299.6 34.2 %attend_back.3 = (bf16[384,1536]{1,0:T(8,128)(2,1)S(1)}, bf16[1536,512]{1,0:T(8,128)(2,1)S(1)}, bf16[1536,512]{1,0:T(8,128)(2,1)S(1)}) custom-call(s32[2]{0:T(128)S(1)} %pad_add_fusion.1.place_ref, bf16[384,1536]{1,0:T(8,128)(2,1)S(1)} %copy-done.15, bf16[1536,512]{1,0:T(8,128)(2,1)S(1)} %bitcast.452, bf16[1536,512]{1,0:T(8,128)(2,1)} %bitcast.450, ...), custom_call_target="tpu_custom_call" | custom-call | flops 18630000640 | bytes 1000 | tf_op jit(solution)/shard_map/attend_back/pallas_call | solution.py:486
  1335.5 36.5 %collective-permute-done.110 = bf16[768,1024]{1,0:T(8,128)(2,1)S(1)} collective-permute-done((bf16[768,1024]{1,0:T(8,128)(2,1)S(1)}, bf16[768,1024]{1,0:T(8,128)(2,1)S(1)}, u32[]{:S(2)}, u32[]{:S(2)}) %collective-permute-start.110) | collective-permute-done | bytes 1572896 | tf_op jit(solution)/shard_map/ppermute | solution.py:134
  1383.2 12.6 collective-permute-done.114
  1400.9 18.5 %expert_grads.7 = bf16[1,1536,1024]{2,1,0:T(8,128)(2,1)} custom-call(bf16[2,2,240,1536]{3,2,1,0:T(8,128)(2,1)S(1)} %copy-done.24, bf16[2,2,240,1536]{3,2,1,0:T(8,128)(2,1)S(1)} %copy-done.25, bf16[2,2,240,1536]{3,2,1,0:T(8,128)(2,1)} %get-tuple-element.652.refs_2_, bf16[2,2,240,1536]{3,2,1,0:T(8,128)(2,1)} %get-tuple-element.653.refs_3_, ...), custom_call_target="tpu_custom_call" | custom-call | flops 6209999872 | bytes 1000 | tf_op jit(solution)/shard_map/expert_grads/pallas_call | solution.py:771
  1445.5 11.3 collective-permute-done.117
  1464.2 24.9 %collective-permute-done.118 = bf16[384,1024]{1,0:T(8,128)(2,1)S(1)} collective-permute-done((bf16[384,1024]{1,0:T(8,128)(2,1)S(1)}, bf16[384,1024]{1,0:T(8,128)(2,1)S(1)}, u32[]{:S(2)}, u32[]{:S(2)}) %collective-permute-start.118) | collective-permute-done | bytes 786464 | tf_op jit(solution)/shard_map/ppermute | solution.py:134
  1503.9 43.6 %collective-permute-done.116 = bf16[384,1024]{1,0:T(8,128)(2,1)S(1)} collective-permute-done((bf16[384,1024]{1,0:T(8,128)(2,1)S(1)}, bf16[384,1024]{1,0:T(8,128)(2,1)S(1)}, u32[]{:S(2)}, u32[]{:S(2)}) %collective-permute-start.116) | collective-permute-done | bytes 786464 | tf_op jit(solution)/shard_map/ppermute | solution.py:134
  1552.1 45.2 %collective-permute-done.121 = bf16[384,1024]{1,0:T(8,128)(2,1)S(1)} collective-permute-done((bf16[384,1024]{1,0:T(8,128)(2,1)S(1)}, bf16[384,1024]{1,0:T(8,128)(2,1)S(1)}, u32[]{:S(2)}, u32[]{:S(2)}) %collective-permute-start.121) | collective-permute-done | bytes 786464 | tf_op jit(solution)/shard_map/ppermute | solution.py:134
  (1082 shorter events, 628.6 us)
Async XLA Ops:
  7.2 84.1 %all-gather.6.cloned.1.call-start = ((), (), s32[]{:S(2)}) async-start(), calls=%async_computation.4 | async-start | bytes 8515584 | tf_op jit(solution)/shard_map/all_gather | solution.py:908
  11.6 111.1 %all-gather.8.cloned.1.call-start = ((), (), s32[]{:S(2)}) async-start(), calls=%async_computation.5 | async-start | bytes 1327104 | tf_op jit(solution)/shard_map/all_gather | solution.py:1003
  91.3 155.8 %all-gather.10.cloned.1.call-start = ((), (), s32[]{:S(2)}) async-start(), calls=%async_computation.6 | async-start | bytes 5898240 | tf_op jit(solution)/shard_map/all_gather | solution.py:1004
  122.8 422.3 %all-gather.12.cloned.1.call-start = ((), (), s32[]{:S(2)}) async-start(), calls=%async_computation.7 | async-start | bytes 8515584 | tf_op jit(solution)/shard_map/all_gather | solution.py:908
  130.9 71.7 %collective-permute-start.2 = (bf16[384,1024]{1,0:T(8,128)(2,1)S(1)}, bf16[384,1024]{1,0:T(8,128)(2,1)S(1)}, u32[]{:S(2)}, u32[]{:S(2)}) collective-permute-start(bf16[384,1024]{1,0:T(8,128)(2,1)S(1)} %copy-done.162), channel_id=1, source_target_pairs={{0,4},{4,0},{1,5},{5,1},{2,6},{6,2},{3,7},{7,3},{8,12},{12,8},{9,1... | collective-permute-start | bytes 2359304 | tf_op jit(solution)/shard_map/ppermute | solution.py:102
  138.3 90.8 %collective-permute-start.1 = (bf16[384,1024]{1,0:T(8,128)(2,1)S(1)}, bf16[384,1024]{1,0:T(8,128)(2,1)S(1)}, u32[]{:S(2)}, u32[]{:S(2)}) collective-permute-start(bf16[384,1024]{1,0:T(8,128)(2,1)S(1)} %copy-done.160), channel_id=1, source_target_pairs={{0,4},{4,0},{1,5},{5,1},{2,6},{6,2},{3,7},{7,3},{8,12},{12,8},{9,1... | collective-permute-start | bytes 2359304 | tf_op jit(solution)/shard_map/ppermute | solution.py:102
  139.3 116.9 %collective-permute-start = (bf16[384,1024]{1,0:T(8,128)(2,1)}, bf16[384,1024]{1,0:T(8,128)(2,1)}, u32[]{:S(2)}, u32[]{:S(2)}) collective-permute-start(bf16[384,1024]{1,0:T(8,128)(2,1)} %get-tuple-element.339), channel_id=1, source_target_pairs={{0,4},{4,0},{1,5},{5,1},{2,6},{6,2},{3,7},{7,3},{8,12},{12,8},{9,1... | collective-permute-start | bytes 2359304 | tf_op jit(solution)/shard_map/ppermute | solution.py:102
  151.2 51.4 %collective-permute-start.6 = (bf16[2,384,512]{2,1,0:T(8,128)(2,1)}, bf16[2,384,512]{2,1,0:T(8,128)(2,1)}, u32[]{:S(2)}, u32[]{:S(2)}) collective-permute-start(bf16[2,384,512]{2,1,0:T(8,128)(2,1)} %pad_maximum_fusion.22), channel_id=1, source_target_pairs={{0,8},{8,0},{1,9},{9,1},{2,10},{10,2},{3,11},{11,3},{4,12},{12,4},... | collective-permute-start | bytes 2359304 | tf_op jit(solution)/shard_map/ppermute | solution.py:102
  152.7 50.0 %collective-permute-start.5 = (bf16[2,384,512]{2,1,0:T(8,128)(2,1)}, bf16[2,384,512]{2,1,0:T(8,128)(2,1)}, u32[]{:S(2)}, u32[]{:S(2)}) collective-permute-start(bf16[2,384,512]{2,1,0:T(8,128)(2,1)} %pad_maximum_fusion.21), channel_id=1, source_target_pairs={{0,16},{16,0},{1,17},{17,1},{2,18},{18,2},{3,19},{19,3},{4,20},{20... | collective-permute-start | bytes 2359304 | tf_op jit(solution)/shard_map/ppermute | solution.py:102
  270.5 380.0 %all-gather.14.cloned.1.call-start = ((), (), s32[]{:S(2)}) async-start(), calls=%async_computation.8 | async-start | bytes 4866048 | tf_op jit(solution)/shard_map/all_gather | solution.py:908
  283.0 42.9 %collective-permute-start.15 = (bf16[768,1024]{1,0:T(8,128)(2,1)S(1)}, bf16[768,1024]{1,0:T(8,128)(2,1)S(1)}, u32[]{:S(2)}, u32[]{:S(2)}) collective-permute-start(bf16[768,1024]{1,0:T(8,128)(2,1)S(1)} %bitcast.493), channel_id=1, source_target_pairs={{0,16},{16,0},{1,17},{17,1},{2,18},{18,2},{3,19},{19,3},{4,20},{20... | collective-permute-start | bytes 4718600 | tf_op jit(solution)/shard_map/ppermute | solution.py:102
  299.9 70.1 %collective-permute-start.17 = (bf16[768,1024]{1,0:T(8,128)(2,1)S(1)}, bf16[768,1024]{1,0:T(8,128)(2,1)S(1)}, u32[]{:S(2)}, u32[]{:S(2)}) collective-permute-start(bf16[768,1024]{1,0:T(8,128)(2,1)S(1)} %bitcast.494), channel_id=1, source_target_pairs={{0,16},{16,0},{1,17},{17,1},{2,18},{18,2},{3,19},{19,3},{4,20},{20... | collective-permute-start | bytes 4718600 | tf_op jit(solution)/shard_map/ppermute | solution.py:102
  301.6 70.9 %collective-permute-start.14 = (bf16[384,1664]{1,0:T(8,128)(2,1)S(1)}, bf16[384,1664]{1,0:T(8,128)(2,1)S(1)}, u32[]{:S(2)}, u32[]{:S(2)}) collective-permute-start(bf16[384,1664]{1,0:T(8,128)(2,1)S(1)} %concatenate.160.own_ref), channel_id=1, source_target_pairs={{0,1},{1,0},{2,3},{3,2},{4,5},{5,4},{6,7},{7,6},{8,9},{9,8},{10,11... | collective-permute-start | bytes 3833864 | tf_op jit(solution)/shard_map/ppermute | solution.py:69
  301.6 85.6 %collective-permute-start.12 = (bf16[384,1664]{1,0:T(8,128)(2,1)S(1)}, bf16[384,1664]{1,0:T(8,128)(2,1)S(1)}, u32[]{:S(2)}, u32[]{:S(2)}) collective-permute-start(bf16[384,1664]{1,0:T(8,128)(2,1)S(1)} %concatenate.160.own_ref), channel_id=1, source_target_pairs={{0,8},{8,0},{1,9},{9,1},{2,10},{10,2},{3,11},{11,3},{4,12},{12,4},... | collective-permute-start | bytes 3833864 | tf_op jit(solution)/shard_map/ppermute | solution.py:69
  303.4 83.8 %collective-permute-start.13 = (bf16[384,1664]{1,0:T(8,128)(2,1)S(1)}, bf16[384,1664]{1,0:T(8,128)(2,1)S(1)}, u32[]{:S(2)}, u32[]{:S(2)}) collective-permute-start(bf16[384,1664]{1,0:T(8,128)(2,1)S(1)} %concatenate.160.own_ref), channel_id=1, source_target_pairs={{0,2},{2,0},{1,3},{3,1},{4,6},{6,4},{5,7},{7,5},{8,10},{10,8},{9,1... | collective-permute-start | bytes 3833864 | tf_op jit(solution)/shard_map/ppermute | solution.py:69
  387.8 56.0 %collective-permute-start.23 = (bf16[384,1536]{1,0:T(8,128)(2,1)S(1)}, bf16[384,1536]{1,0:T(8,128)(2,1)}, u32[]{:S(2)}, u32[]{:S(2)}) collective-permute-start(bf16[384,1536]{1,0:T(8,128)(2,1)S(1)} %get-tuple-element.383), channel_id=1, source_target_pairs={{0,1},{1,0},{2,3},{3,2},{4,5},{5,4},{6,7},{7,6},{8,9},{9,8},{10,11... | collective-permute-start | bytes 3538952 | tf_op jit(solution)/shard_map/ppermute | solution.py:69
  473.3 58.3 %collective-permute-start.10 = (bf16[384,1024]{1,0:T(8,128)(2,1)S(1)}, bf16[384,1024]{1,0:T(8,128)(2,1)}, u32[]{:S(2)}, u32[]{:S(2)}) collective-permute-start(bf16[384,1024]{1,0:T(8,128)(2,1)S(1)} %copy-done.156), channel_id=1, source_target_pairs={{0,4},{4,0},{1,5},{5,1},{2,6},{6,2},{3,7},{7,3},{8,12},{12,8},{9,1... | collective-permute-start | bytes 2359304 | tf_op jit(solution)/shard_map/ppermute | solution.py:102
  475.3 120.9 %collective-permute-start.37 = (bf16[384,1024]{1,0:T(8,128)(2,1)}, bf16[384,1024]{1,0:T(8,128)(2,1)}, u32[]{:S(2)}, u32[]{:S(2)}) collective-permute-start(bf16[384,1024]{1,0:T(8,128)(2,1)} %get-tuple-element.411), channel_id=1, source_target_pairs={{0,4},{4,0},{1,5},{5,1},{2,6},{6,2},{3,7},{7,3},{8,12},{12,8},{9,1... | collective-permute-start | bytes 2359304 | tf_op jit(solution)/shard_map/ppermute | solution.py:102
  476.3 564.7 %reduce-scatter.5.cloned.1.call-start = ((), (), s32[]{:S(2)}) async-start(), calls=%async_computation.9 | async-start | bytes 4866048 | tf_op jit(solution)/shard_map/reduce_scatter | solution.py:830
  478.1 53.5 %collective-permute-start.24 = (bf16[384,1024]{1,0:T(8,128)(2,1)S(1)}, bf16[384,1024]{1,0:T(8,128)(2,1)S(1)}, u32[]{:S(2)}, u32[]{:S(2)}) collective-permute-start(bf16[384,1024]{1,0:T(8,128)(2,1)S(1)} %broadcast_select_fusion.5), channel_id=1, source_target_pairs={{0,8},{8,0},{1,9},{9,1},{2,10},{10,2},{3,11},{11,3},{4,12},{12,4},... | collective-permute-start | bytes 2359304 | tf_op jit(solution)/shard_map/ppermute | solution.py:69
  539.2 57.0 %collective-permute-start.38 = (bf16[768,1024]{1,0:T(8,128)(2,1)}, bf16[768,1024]{1,0:T(8,128)(2,1)}, u32[]{:S(2)}, u32[]{:S(2)}) collective-permute-start(bf16[768,1024]{1,0:T(8,128)(2,1)} %bitcast.61), channel_id=1, source_target_pairs={{0,16},{16,0},{1,17},{17,1},{2,18},{18,2},{3,19},{19,3},{4,20},{20... | collective-permute-start | bytes 4718600 | tf_op jit(solution)/shard_map/ppermute | solution.py:102
  542.7 67.5 %collective-permute-start.34 = (bf16[384,1024]{1,0:T(8,128)(2,1)}, bf16[384,1024]{1,0:T(8,128)(2,1)}, u32[]{:S(2)}, u32[]{:S(2)}) collective-permute-start(bf16[384,1024]{1,0:T(8,128)(2,1)} %broadcast_select_fusion.4), channel_id=1, source_target_pairs={{0,8},{8,0},{1,9},{9,1},{2,10},{10,2},{3,11},{11,3},{4,12},{12,4},... | collective-permute-start | bytes 2359304 | tf_op jit(solution)/shard_map/ppermute | solution.py:69
  677.5 48.4 %collective-permute-start.41 = (bf16[384,1536]{1,0:T(8,128)(2,1)S(1)}, bf16[384,1536]{1,0:T(8,128)(2,1)S(1)}, u32[]{:S(2)}, u32[]{:S(2)}) collective-permute-start(bf16[384,1536]{1,0:T(8,128)(2,1)S(1)} %bitcast.466), channel_id=1, source_target_pairs={{0,8},{8,0},{1,9},{9,1},{2,10},{10,2},{3,11},{11,3},{4,12},{12,4},... | collective-permute-start | bytes 3538952 | tf_op jit(solution)/shard_map/ppermute | solution.py:69
  681.1 47.2 %collective-permute-start.42 = (bf16[384,1536]{1,0:T(8,128)(2,1)S(1)}, bf16[384,1536]{1,0:T(8,128)(2,1)S(1)}, u32[]{:S(2)}, u32[]{:S(2)}) collective-permute-start(bf16[384,1536]{1,0:T(8,128)(2,1)S(1)} %bitcast.467), channel_id=1, source_target_pairs={{0,2},{2,0},{1,3},{3,1},{4,6},{6,4},{5,7},{7,5},{8,10},{10,8},{9,1... | collective-permute-start | bytes 3538952 | tf_op jit(solution)/shard_map/ppermute | solution.py:69
  729.7 43.6 %collective-permute-start.56 = (bf16[192,1664]{1,0:T(8,128)(2,1)}, bf16[192,1664]{1,0:T(8,128)(2,1)S(1)}, u32[]{:S(2)}, u32[]{:S(2)}) collective-permute-start(bf16[192,1664]{1,0:T(8,128)(2,1)} %slice.493), channel_id=1, source_target_pairs={{0,8},{8,0},{1,9},{9,1},{2,10},{10,2},{3,11},{11,3},{4,12},{12,4},... | collective-permute-start | bytes 1916936 | tf_op jit(solution)/shard_map/ppermute | solution.py:69
  732.2 70.3 %collective-permute-start.59 = (bf16[384,1664]{1,0:T(8,128)(2,1)S(1)}, bf16[384,1664]{1,0:T(8,128)(2,1)}, u32[]{:S(2)}, u32[]{:S(2)}) collective-permute-start(bf16[384,1664]{1,0:T(8,128)(2,1)S(1)} %get-tuple-element.476), channel_id=1, source_target_pairs={{0,1},{1,0},{2,3},{3,2},{4,5},{5,4},{6,7},{7,6},{8,9},{9,8},{10,11... | collective-permute-start | bytes 3833864 | tf_op jit(solution)/shard_map/ppermute | solution.py:69
  877.1 87.4 %collective-permute-start.68 = (bf16[768,1024]{1,0:T(8,128)(2,1)}, bf16[768,1024]{1,0:T(8,128)(2,1)}, u32[]{:S(2)}, u32[]{:S(2)}) collective-permute-start(bf16[768,1024]{1,0:T(8,128)(2,1)} %dynamic-slice_bitcast_fusion.5), channel_id=1, source_target_pairs={{0,16},{16,0},{1,17},{17,1},{2,18},{18,2},{3,19},{19,3},{4,20},{20... | collective-permute-start | bytes 4718600 | tf_op jit(solution)/shard_map/ppermute | solution.py:134
  890.4 77.4 %collective-permute-start.71 = (bf16[384,1536]{1,0:T(8,128)(2,1)}, bf16[384,1536]{1,0:T(8,128)(2,1)}, u32[]{:S(2)}, u32[]{:S(2)}) collective-permute-start(bf16[384,1536]{1,0:T(8,128)(2,1)} %get-tuple-element.534), channel_id=1, source_target_pairs={{0,1},{1,0},{2,3},{3,2},{4,5},{5,4},{6,7},{7,6},{8,9},{9,8},{10,11... | collective-permute-start | bytes 3538952 | tf_op jit(solution)/shard_map/ppermute | solution.py:69
  906.2 349.3 %reduce-scatter.7.cloned.1.call-start = ((), (), s32[]{:S(2)}) async-start(), calls=%async_computation.10 | async-start | bytes 8110080 | tf_op jit(solution)/shard_map/reduce_scatter | solution.py:830
  924.7 43.2 %collective-permute-start.75 = (bf16[384,1536]{1,0:T(8,128)(2,1)S(1)}, bf16[384,1536]{1,0:T(8,128)(2,1)S(1)}, u32[]{:S(2)}, u32[]{:S(2)}) collective-permute-start(bf16[384,1536]{1,0:T(8,128)(2,1)S(1)} %pad_maximum_fusion.17), channel_id=1, source_target_pairs={{0,8},{8,0},{1,9},{9,1},{2,10},{10,2},{3,11},{11,3},{4,12},{12,4},... | collective-permute-start | bytes 3538952 | tf_op jit(solution)/shard_map/ppermute | solution.py:69
  967.9 73.0 %collective-permute-start.79 = (bf16[1,384,1024]{2,1,0:T(8,128)(2,1)}, bf16[1,384,1024]{2,1,0:T(8,128)(2,1)}, u32[]{:S(2)}, u32[]{:S(2)}) collective-permute-start(bf16[1,384,1024]{2,1,0:T(8,128)(2,1)} %dynamic-slice_bitcast_fusion.15), channel_id=1, source_target_pairs={{0,8},{8,0},{1,9},{9,1},{2,10},{10,2},{3,11},{11,3},{4,12},{12,4},... | collective-permute-start | bytes 2359304 | tf_op jit(solution)/shard_map/ppermute | solution.py:69
  973.1 56.3 %collective-permute-start.82 = (bf16[2,384,512]{2,1,0:T(8,128)(2,1)}, bf16[2,384,512]{2,1,0:T(8,128)(2,1)S(1)}, u32[]{:S(2)}, u32[]{:S(2)}) collective-permute-start(bf16[2,384,512]{2,1,0:T(8,128)(2,1)} %dynamic-slice_bitcast_fusion.13), channel_id=1, source_target_pairs={{0,8},{8,0},{1,9},{9,1},{2,10},{10,2},{3,11},{11,3},{4,12},{12,4},... | collective-permute-start | bytes 2359304 | tf_op jit(solution)/shard_map/ppermute | solution.py:134
  975.0 56.7 %collective-permute-start.80 = (bf16[2,384,512]{2,1,0:T(8,128)(2,1)}, bf16[2,384,512]{2,1,0:T(8,128)(2,1)S(1)}, u32[]{:S(2)}, u32[]{:S(2)}) collective-permute-start(bf16[2,384,512]{2,1,0:T(8,128)(2,1)} %dynamic-slice_bitcast_fusion.14), channel_id=1, source_target_pairs={{0,16},{16,0},{1,17},{17,1},{2,18},{18,2},{3,19},{19,3},{4,20},{20... | collective-permute-start | bytes 2359304 | tf_op jit(solution)/shard_map/ppermute | solution.py:134
  1063.6 44.2 %collective-permute-start.85 = (bf16[768,1024]{1,0:T(8,128)(2,1)}, bf16[768,1024]{1,0:T(8,128)(2,1)}, u32[]{:S(2)}, u32[]{:S(2)}) collective-permute-start(bf16[768,1024]{1,0:T(8,128)(2,1)} %dynamic-slice_bitcast_fusion.4), channel_id=1, source_target_pairs={{0,16},{16,0},{1,17},{17,1},{2,18},{18,2},{3,19},{19,3},{4,20},{20... | collective-permute-start | bytes 4718600 | tf_op jit(solution)/shard_map/ppermute | solution.py:134
  1063.9 43.0 %collective-permute-start.86 = (bf16[384,1536]{1,0:T(8,128)(2,1)S(1)}, bf16[384,1536]{1,0:T(8,128)(2,1)S(1)}, u32[]{:S(2)}, u32[]{:S(2)}) collective-permute-start(bf16[384,1536]{1,0:T(8,128)(2,1)S(1)} %convert_element_type.685.own_ref), channel_id=1, source_target_pairs={{0,8},{8,0},{1,9},{9,1},{2,10},{10,2},{3,11},{11,3},{4,12},{12,4},... | collective-permute-start | bytes 3538952 | tf_op jit(solution)/shard_map/ppermute | solution.py:69
  1064.4 43.4 %collective-permute-start.87 = (bf16[384,1536]{1,0:T(8,128)(2,1)S(1)}, bf16[384,1536]{1,0:T(8,128)(2,1)S(1)}, u32[]{:S(2)}, u32[]{:S(2)}) collective-permute-start(bf16[384,1536]{1,0:T(8,128)(2,1)S(1)} %convert_element_type.685.own_ref), channel_id=1, source_target_pairs={{0,2},{2,0},{1,3},{3,1},{4,6},{6,4},{5,7},{7,5},{8,10},{10,8},{9,1... | collective-permute-start | bytes 3538952 | tf_op jit(solution)/shard_map/ppermute | solution.py:69
  1066.0 353.7 %reduce-scatter.9.cloned.1.call-start = ((), (), s32[]{:S(2)}) async-start(), calls=%async_computation.11 | async-start | bytes 4866048 | tf_op jit(solution)/shard_map/reduce_scatter | solution.py:830
  1109.6 50.7 %collective-permute-start.89 = (bf16[768,1024]{1,0:T(8,128)(2,1)}, bf16[768,1024]{1,0:T(8,128)(2,1)}, u32[]{:S(2)}, u32[]{:S(2)}) collective-permute-start(bf16[768,1024]{1,0:T(8,128)(2,1)} %dynamic-slice_bitcast_fusion.3), channel_id=1, source_target_pairs={{0,16},{16,0},{1,17},{17,1},{2,18},{18,2},{3,19},{19,3},{4,20},{20... | collective-permute-start | bytes 4718600 | tf_op jit(solution)/shard_map/ppermute | solution.py:134
  1111.3 73.8 %collective-permute-start.96 = (bf16[384,1664]{1,0:T(8,128)(2,1)S(1)}, bf16[384,1664]{1,0:T(8,128)(2,1)S(1)}, u32[]{:S(2)}, u32[]{:S(2)}) collective-permute-start(bf16[384,1664]{1,0:T(8,128)(2,1)S(1)} %get-tuple-element.590), channel_id=1, source_target_pairs={{0,1},{1,0},{2,3},{3,2},{4,5},{5,4},{6,7},{7,6},{8,9},{9,8},{10,11... | collective-permute-start | bytes 3833864 | tf_op jit(solution)/shard_map/ppermute | solution.py:69
  1125.2 59.9 %collective-permute-start.95 = (bf16[384,1664]{1,0:T(8,128)(2,1)S(1)}, bf16[384,1664]{1,0:T(8,128)(2,1)}, u32[]{:S(2)}, u32[]{:S(2)}) collective-permute-start(bf16[384,1664]{1,0:T(8,128)(2,1)S(1)} %get-tuple-element.589), channel_id=1, source_target_pairs={{0,1},{1,0},{2,3},{3,2},{4,5},{5,4},{6,7},{7,6},{8,9},{9,8},{10,11... | collective-permute-start | bytes 3833864 | tf_op jit(solution)/shard_map/ppermute | solution.py:69
  1127.7 57.3 %collective-permute-start.90 = (bf16[1,384,1024]{2,1,0:T(8,128)(2,1)S(1)}, bf16[1,384,1024]{2,1,0:T(8,128)(2,1)}, u32[]{:S(2)}, u32[]{:S(2)}) collective-permute-start(bf16[1,384,1024]{2,1,0:T(8,128)(2,1)S(1)} %dynamic-slice_bitcast_fusion.12), channel_id=1, source_target_pairs={{0,8},{8,0},{1,9},{9,1},{2,10},{10,2},{3,11},{11,3},{4,12},{12,4},... | collective-permute-start | bytes 2359304 | tf_op jit(solution)/shard_map/ppermute | solution.py:69
  1214.6 51.5 %collective-permute-start.102 = (bf16[384,1024]{1,0:T(8,128)(2,1)S(1)}, bf16[384,1024]{1,0:T(8,128)(2,1)}, u32[]{:S(2)}, u32[]{:S(2)}) collective-permute-start(bf16[384,1024]{1,0:T(8,128)(2,1)S(1)} %fusion.124), channel_id=1, source_target_pairs={{0,4},{4,0},{1,5},{5,1},{2,6},{6,2},{3,7},{7,3},{8,12},{12,8},{9,1... | collective-permute-start | bytes 2359304 | tf_op jit(solution)/shard_map/ppermute | solution.py:134
  1219.3 46.7 %collective-permute-start.101 = (bf16[1,384,1024]{2,1,0:T(8,128)(2,1)}, bf16[1,384,1024]{2,1,0:T(8,128)(2,1)}, u32[]{:S(2)}, u32[]{:S(2)}) collective-permute-start(bf16[1,384,1024]{2,1,0:T(8,128)(2,1)} %dynamic-slice_bitcast_fusion.11), channel_id=1, source_target_pairs={{0,8},{8,0},{1,9},{9,1},{2,10},{10,2},{3,11},{11,3},{4,12},{12,4},... | collective-permute-start | bytes 2359304 | tf_op jit(solution)/shard_map/ppermute | solution.py:69
  1297.2 309.1 %reduce-scatter.11.cloned.1.call-start = ((), (), s32[]{:S(2)}) async-start(), calls=%async_computation.12 | async-start | bytes 8515584 | tf_op jit(solution)/shard_map/reduce_scatter | solution.py:830
  1299.0 73.0 %collective-permute-start.110 = (bf16[768,1024]{1,0:T(8,128)(2,1)S(1)}, bf16[768,1024]{1,0:T(8,128)(2,1)S(1)}, u32[]{:S(2)}, u32[]{:S(2)}) collective-permute-start(bf16[768,1024]{1,0:T(8,128)(2,1)S(1)} %dynamic-slice_bitcast_fusion.1), channel_id=1, source_target_pairs={{0,16},{16,0},{1,17},{17,1},{2,18},{18,2},{3,19},{19,3},{4,20},{20... | collective-permute-start | bytes 4718600 | tf_op jit(solution)/shard_map/ppermute | solution.py:134
  1492.7 54.8 %collective-permute-start.116 = (bf16[384,1024]{1,0:T(8,128)(2,1)S(1)}, bf16[384,1024]{1,0:T(8,128)(2,1)S(1)}, u32[]{:S(2)}, u32[]{:S(2)}) collective-permute-start(bf16[384,1024]{1,0:T(8,128)(2,1)S(1)} %fusion.116), channel_id=1, source_target_pairs={{0,4},{4,0},{1,5},{5,1},{2,6},{6,2},{3,7},{7,3},{8,12},{12,8},{9,1... | collective-permute-start | bytes 2359304 | tf_op jit(solution)/shard_map/ppermute | solution.py:134
  1499.8 48.2 %collective-permute-start.120 = (bf16[1,384,1024]{2,1,0:T(8,128)(2,1)S(1)}, bf16[1,384,1024]{2,1,0:T(8,128)(2,1)S(1)}, u32[]{:S(2)}, u32[]{:S(2)}) collective-permute-start(bf16[1,384,1024]{2,1,0:T(8,128)(2,1)S(1)} %dynamic-slice_bitcast_fusion.6), channel_id=1, source_target_pairs={{0,8},{8,0},{1,9},{9,1},{2,10},{10,2},{3,11},{11,3},{4,12},{12,4},... | collective-permute-start | bytes 2359304 | tf_op jit(solution)/shard_map/ppermute | solution.py:69
  1548.5 48.9 %collective-permute-start.121 = (bf16[384,1024]{1,0:T(8,128)(2,1)S(1)}, bf16[384,1024]{1,0:T(8,128)(2,1)S(1)}, u32[]{:S(2)}, u32[]{:S(2)}) collective-permute-start(bf16[384,1024]{1,0:T(8,128)(2,1)S(1)} %fusion.108), channel_id=1, source_target_pairs={{0,4},{4,0},{1,5},{5,1},{2,6},{6,2},{3,7},{7,3},{8,12},{12,8},{9,1... | collective-permute-start | bytes 2359304 | tf_op jit(solution)/shard_map/ppermute | solution.py:134
  (340 other events, 4439.8 us)
Sparse Core Ops, SparseCore 0:
  11.8 79.5 all-gather.5
  93.5 21.2 all-gather.7
  122.9 74.0 all-gather.9
  270.6 108.0 all-gather.11
  476.4 104.5 all-gather.13
  906.3 104.4 reduce-scatter.4
  1066.1 141.8 reduce-scatter.6
  1297.3 118.9 reduce-scatter.8
  1437.9 168.3 reduce-scatter.10
